TPU v7x, 32 devices: a whole 2x2x4 slice. The times are simulated.
32 devices in a mesh: front: 4 (over x, core), row: 2 (over y), col: 4 (over z).
Axes of the slice: x: 2, y: 2, z: 4, core: 2. Of those that a mesh axis runs over, the one named last changes fastest.
Arguments:
- contrib: float32 [32768, 4096], P(('front', 'row'), 'col'), parts along dimension 0, as said below
- front_diag: float32 [32768], P(('front', 'row')), parts along dimension 0, may hold values from 1 to 4
- child_map: int32 [8, 32], P('front'), parts along dimension 0, may hold values from 0 to 63, as said below
- pivots: int32 [16], P('front'), parts along dimension 0, may hold values from 0 to 63, as said below
Outputs:
- lfactor: float32 [32768, 512], P(('front', 'row'), 'col'), parts along dimension 0
- schur_block: float32 [32768, 8192], P(('front', 'row'), 'col'), parts along dimension 0
There are 4 independent parts, one for each index of `front`. A program takes and returns all parts, laid end to end along the dimension named above; each array names one. Nothing has to cross between parts.
Inputs may be any that keep to these rules, and one draw needn't show every extreme that they name: child_map[c, b] is b or b + 32, chosen for each child and block. `pivots`: 4 distinct front blocks. `contrib`: each child's contribution block is symmetric positive definite.
All inputs are finite; a program needn't handle non-finite values.
Results may differ from a plain program's by a relative error of at most 0.0001.
Values sent between devices are 32-bit elements; how exact they have to be, the bound alone decides.
No kernel may reach another device: no remote copies, remote signals or barrier semaphores. Data moves between devices by JAX's collectives and lax.ppermute only.
A program may use at most 192 MiB of HBM per device.

v0:
```python
import jax
import jax.numpy as jnp
from jax import lax
from jax.sharding import PartitionSpec as P

NF = 8192
NPAN = 2
BLK = 128


highest = lax.Precision.HIGHEST


def swapped(shard, axis, bit):
    return lax.ppermute(shard, axis, [(i, i ^ 1 << bit) for i in range(lax.axis_size(axis))])


def broadcast(shard, axis, root):
    mine = lax.axis_index(axis) == root
    return lax.psum(jnp.where(mine, shard, jnp.zeros_like(shard)), axis)


def select_rows(mapping, chosen_ids, within, half_rows, row_index, row_count, row_slots):
    by_device = mapping.reshape(mapping.shape[0] // half_rows, half_rows)
    targets = jnp.take(lax.dynamic_index_in_dim(by_device, within, 1, keepdims=False), chosen_ids)
    slot_ids = jnp.arange(row_slots) * row_count + row_index
    return (targets[None, :] == slot_ids[:, None]).astype(jnp.float32)


def select_cols(mapping, col_index, col_count, col_slots):
    by_device = mapping.reshape(mapping.shape[0] // col_count, col_count)
    targets = lax.dynamic_index_in_dim(by_device, col_index, 1, keepdims=False)
    slot_ids = jnp.arange(col_slots) * col_count + col_index
    return (targets[None, :] == slot_ids[:, None]).astype(jnp.float32)


def place_blocks(pieces, row_select, col_select):
    blocks = pieces.reshape(row_select.shape[1], BLK, col_select.shape[1], BLK)
    placed = jnp.einsum("kj,jaib->kaib", row_select, blocks, precision=highest)
    placed = jnp.einsum("li,kaib->kalb", col_select, placed, precision=highest)
    return placed.reshape(row_select.shape[0] * BLK, col_select.shape[0] * BLK)


def per_device(contrib, front_diag, child_map, pivots):
    row_count = lax.axis_size("row")
    col_count = lax.axis_size("col")
    row_index = lax.axis_index("row")
    col_index = lax.axis_index("col")
    half_rows = row_count // 2
    half_bit = half_rows.bit_length() - 1
    sibling = row_index // half_rows
    within = row_index % half_rows
    local_rows = front_diag.shape[0]
    row_slots = local_rows // BLK
    col_width = NF // col_count
    col_slots = col_width // BLK
    child_rows = contrib.shape[0] // BLK
    own_map = lax.dynamic_index_in_dim(child_map, sibling, 0, keepdims=False)
    other_map = lax.dynamic_index_in_dim(child_map, 1 - sibling, 0, keepdims=False)
    partner = swapped(contrib, "row", half_bit)
    other_ids = jnp.arange(child_rows)
    own_rows = select_rows(
        own_map, jnp.arange(child_rows), within, half_rows, row_index, row_count, row_slots
    )
    other_rows = select_rows(
        other_map, other_ids, within, half_rows, row_index, row_count, row_slots
    )
    own_cols = select_cols(own_map, col_index, col_count, col_slots)
    other_cols = select_cols(other_map, col_index, col_count, col_slots)
    assembled = place_blocks(contrib, own_rows, own_cols) + place_blocks(
        partner, other_rows, other_cols
    )
    row_ids = jnp.arange(row_slots) * row_count + row_index
    col_ids = jnp.arange(col_slots) * col_count + col_index
    on_diagonal = (row_ids[:, None] == col_ids[None, :]).astype(jnp.float32)
    identity = jnp.eye(BLK, dtype=jnp.float32)
    diag_blocks = front_diag.reshape(row_slots, BLK)
    diag_part = (
        on_diagonal[:, None, :, None] * diag_blocks[:, :, None, None] * identity[None, :, None, :]
    )
    front_tile = assembled + diag_part.reshape(local_rows, col_width)
    factors = []
    for panel_index in range(NPAN):
        chosen = [pivots[2 * panel_index], pivots[2 * panel_index + 1]]
        columns = []
        for block_id in chosen:
            block_piece = lax.dynamic_slice_in_dim(front_tile, block_id // col_count * BLK, BLK, 1)
            columns.append(broadcast(block_piece, "col", block_id % col_count))
        panel_cols = jnp.concatenate(columns, axis=1)
        owned_rows = []
        for block_id in chosen:
            rows_here = lax.dynamic_slice_in_dim(panel_cols, block_id // row_count * BLK, BLK, 0)
            owned_rows.append(jnp.where(block_id % row_count == row_index, rows_here, 0.0))
        pivot_block = lax.psum(jnp.concatenate(owned_rows, axis=0), "row")
        lower_factor = jnp.linalg.cholesky(pivot_block)
        factor = lax.linalg.triangular_solve(
            lower_factor, panel_cols, left_side=False, lower=True, transpose_a=True
        )
        source_rows = []
        for slot_index in range(col_slots):
            source_rows.append(
                lax.dynamic_slice_in_dim(factor, col_ids[slot_index] // row_count * BLK, BLK, 0)
            )
        across = broadcast(jnp.concatenate(source_rows, axis=0), "row", col_index % row_count)
        update = jnp.einsum("ak,bk->ab", factor, across, precision=highest)
        row_hit = jnp.logical_or(row_ids == chosen[0], row_ids == chosen[1])
        col_hit = jnp.logical_or(col_ids == chosen[0], col_ids == chosen[1])
        row_keep = jnp.repeat(jnp.where(row_hit, 0.0, 1.0), BLK)
        col_keep = jnp.repeat(jnp.where(col_hit, 0.0, 1.0), BLK)
        front_tile = (front_tile - update) * row_keep[:, None] * col_keep[None, :]
        factors.append(factor)
    stacked = jnp.concatenate(factors, axis=1)
    col_share = stacked.shape[1] // col_count
    lfactor = lax.dynamic_slice_in_dim(stacked, col_index * col_share, col_share, 1)
    return (lfactor, front_tile)


def solution(mesh):
    placed = (P(("front", "row"), "col"), P(("front", "row")), P("front", None), P("front"))
    return jax.shard_map(
        per_device,
        mesh=mesh,
        in_specs=placed,
        out_specs=(P(("front", "row"), "col"), P(("front", "row"), "col")),
        check_vma=False,
    )
```

profile of v0, /device:TPU:6, one launch (start us, length us, event | category | flops | bytes accessed | tf_op | source)
XLA Modules:
  0.0 1320.9 jit_solution(14540624683325055229)
XLA Ops:
  7.8 1.4 fusion.118
  15.4 14.2 %copy.31 = f32[512,8,8,128]{3,2,1,0:T(8,128)} copy(f32[512,8,8,128]{3,1,2,0:T(8,128)} %bitcast.174) | data formatting | bytes 33554432
  31.9 27.0 %fusion.6 = f32[32,128,8,128]{3,0,2,1:T(8,128)} fusion(f32[32,128,8,128]{3,2,1,0:T(8,128)} %bitcast.172, s32[32]{0:T(128)S(1)} %compare_select_fusion.1, s32[32]{0:T(128)S(1)} %get-tuple-element.96), kind=kOutput, calls=%fused_computation.82 | convolution fusion | flops 1610613760 | bytes 33554688 | tf_op jit(solution)/shard_map/kj,jaib->kaib/dot_general | solution.py:39
  59.0 310.6 %collective-permute-done = f32[4096,1024]{1,0:T(8,128)} collective-permute-done((f32[4096,1024]{1,0:T(8,128)}, f32[4096,1024]{1,0:T(8,128)}, u32[]{:S(2)}, u32[]{:S(2)}) %collective-permute-start) | collective-permute-done | bytes 16777248 | tf_op jit(solution)/shard_map/ppermute | solution.py:15
  369.6 14.2 %copy.32 = f32[512,8,8,128]{3,2,1,0:T(8,128)} copy(f32[512,8,8,128]{3,1,2,0:T(8,128)} %bitcast.61) | data formatting | bytes 33554432
  383.7 26.7 %fusion.2 = f32[32,128,8,128]{3,0,2,1:T(8,128)} fusion(f32[32,128,8,128]{3,2,1,0:T(8,128)} %bitcast.173, s32[32]{0:T(128)S(1)} %get-tuple-element.95, s32[32]{0:T(128)S(1)} %get-tuple-element.96), kind=kOutput, calls=%fused_computation.78 | convolution fusion | flops 1610613760 | bytes 33554688 | tf_op jit(solution)/shard_map/kj,jaib->kaib/dot_general | solution.py:39
  410.4 34.0 %fusion = f32[32,128,128,16]{2,3,1,0:T(8,128)} fusion(f32[32,128,8,128]{3,0,2,1:T(8,128)} %fusion.2, s32[16]{0:T(128)S(1)} %multiply_add_fusion, s32[8]{0:T(128)S(1)} %get-tuple-element.94), kind=kOutput, calls=%fused_computation.76 | convolution fusion | flops 805306496 | bytes 50331744 | tf_op jit(solution)/shard_map/li,kaib->kalb/dot_general | solution.py:40
  444.4 39.2 %bitcast_add_fusion = f32[32,128,16,128]{3,2,1,0:T(8,128)} fusion(f32[32,128,128,16]{2,3,1,0:T(8,128)} %fusion, f32[128,128]{1,0:T(8,128)S(1)} %fusion.91, f32[32,128,16]{2,1,0:T(8,128)S(1)} %broadcast_multiply_fusion, f32[32,128,8,128]{3,0,2,1:T(8,128)} %fusion.6, s32[16]{0:T(128)S(1)} %multiply_add_fusion, s32[8]{0:T(128)S(1)} %get-tuple-element.93), kind=kOutput, calls=%fused_computation.7 | convolution fusion | flops 830472320 | bytes 84213856 | tf_op jit(solution)/shard_map/li,kaib->kalb/dot_general | solution.py:40
  483.6 29.9 %copy.45 = f32[512,8,16,128]{3,1,2,0:T(8,128)} copy(f32[512,8,16,128]{3,2,1,0:T(8,128)} %bitcast.170) | data formatting | bytes 67108864
  513.5 31.1 %copy.30 = f32[4096,2048]{0,1:T(8,128)} copy(f32[4096,2048]{1,0:T(8,128)} %bitcast.171) | data formatting | bytes 67108864 | tf_op jit(solution)/shard_map/add | solution.py:81
  544.6 4.7 dynamic-slice_select_fusion.2
  549.4 156.6 %all-reduce.20.cloned.1.call-done = (f32[4096,128]{0,1:T(8,128)}, f32[4096,128]{0,1:T(8,128)}) async-done(((f32[4096,128]{0,1:T(8,128)}, f32[4096,128]{0,1:T(8,128)}), (f32[4096,128]{0,1:T(8,128)}, f32[4096,128]{0,1:T(8,128)})) %all-reduce.20.cloned.1.call-update) | async-done | bytes 4194320 | tf_op jit(solution)/shard_map/psum | solution.py:20
  706.0 1.9 constant_dynamic-update-slice_fusion.1
  751.2 11.7 cholesky.130
  763.0 9.8 custom-call.13
  773.3 11.7 cholesky.147
  787.8 4.2 while.4
  788.6 1.4 bitcast_dynamic-update-slice_fusion.4
  790.6 1.4 bitcast_dynamic-update-slice_fusion.4
  792.0 19.7 %custom-call.14 = f32[2,128,128]{1,2,0:T(8,128)S(1)} custom-call(f32[2,128,128]{2,1,0:T(8,128)S(1)} %get-tuple-element.19), custom_call_target="InvertDiagBlocksLowerTriangular" | custom-call | tf_op jit(solution)/shard_map/triangular_solve/custom-call.0 | solution.py:96
  811.6 3.6 fusion.86
  815.3 2.0 convolution_subtract_fusion.1
  817.3 2.0 fusion.84
  820.7 1.5 broadcast_select_fusion.1
  827.1 1.3 or_select_fusion.2
  828.4 1.3 or_select_fusion.3
  829.8 53.6 %all-reduce.12.cloned.1.call-done = f32[2048,256]{0,1:T(8,128)} async-done(((f32[2048,256]{0,1:T(8,128)}), f32[2048,256]{0,1:T(8,128)}) %all-reduce.12.cloned.1.call-update) | async-done | bytes 2097168 | tf_op jit(solution)/shard_map/psum | solution.py:20
  883.4 37.9 %multiply_multiply_fusion.1 = f32[4096,2048]{0,1:T(8,128)} fusion(f32[4096,2048]{0,1:T(8,128)} %copy.30, f32[2048]{0:T(1024)S(1)} %broadcast_bitcast_fusion.3, f32[4096]{0:T(1024)S(1)} %broadcast_bitcast_fusion.1, f32[2048,256]{0,1:T(8,128)} %all-reduce.12.cloned.1.call-done, f32[4096,128]{0,1:T(8,128)} %copy-done.2, f32[4096,128]{0,1:T(8,128)S(1)} %bitcast.150), kind=kOutput, calls=%fused_computation.9 | convolution fusion | flops 25796018176 | bytes 73424896 | tf_op jit(solution)/shard_map/ak,bk->ab/dot_general | solution.py:105
  921.3 4.6 dynamic-slice_select_fusion
  926.1 156.3 %all-reduce.18.cloned.1.call-done = (f32[4096,128]{0,1:T(8,128)}, f32[4096,128]{0,1:T(8,128)}) async-done(((f32[4096,128]{0,1:T(8,128)}, f32[4096,128]{0,1:T(8,128)}), (f32[4096,128]{0,1:T(8,128)}, f32[4096,128]{0,1:T(8,128)})) %all-reduce.18.cloned.1.call-update) | async-done | bytes 4194320 | tf_op jit(solution)/shard_map/psum | solution.py:20
  1082.4 1.9 constant_dynamic-update-slice_fusion.3
  1085.8 21.2 %all-reduce.14.cloned.1.call-done = f32[256,256]{0,1:T(8,128)} async-done(((f32[256,256]{0,1:T(8,128)}), f32[256,256]{0,1:T(8,128)}) %all-reduce.14.cloned.1.call-update) | async-done | bytes 262160 | tf_op jit(solution)/shard_map/psum | solution.py:94
  1109.1 11.7 cholesky.164
  1120.9 9.8 custom-call.15
  1131.2 11.7 cholesky.181
  1145.5 4.1 while.5
  1146.4 1.3 bitcast_dynamic-update-slice_fusion.5
  1148.3 1.3 bitcast_dynamic-update-slice_fusion.5
  1149.6 19.7 %custom-call.16 = f32[2,128,128]{1,2,0:T(8,128)S(1)} custom-call(f32[2,128,128]{2,1,0:T(8,128)S(1)} %get-tuple-element.20), custom_call_target="InvertDiagBlocksLowerTriangular" | custom-call | tf_op jit(solution)/shard_map/triangular_solve/custom-call.0 | solution.py:96
  1169.3 3.6 fusion.81
  1173.0 2.0 convolution_subtract_fusion
  1175.0 2.0 fusion.79
  1178.3 1.4 broadcast_select_fusion
  1182.3 2.4 fusion.11
  1184.8 3.0 copy.18
  1187.8 55.1 %all-reduce.16.cloned.1.call-done = f32[2048,256]{0,1:T(8,128)} async-done(((f32[2048,256]{0,1:T(8,128)}), f32[2048,256]{0,1:T(8,128)}) %all-reduce.16.cloned.1.call-update) | async-done | bytes 2097168 | tf_op jit(solution)/shard_map/psum | solution.py:20
  1242.9 37.6 %multiply_multiply_fusion = f32[4096,2048]{0,1:T(8,128)} fusion(f32[4096,2048]{0,1:T(8,128)} %multiply_multiply_fusion.1, f32[2048]{0:T(1024)S(1)} %broadcast_bitcast_fusion.2, f32[4096]{0:T(1024)S(1)} %broadcast_bitcast_fusion, f32[2048,256]{0,1:T(8,128)} %all-reduce.16.cloned.1.call-done, f32[4096,128]{0,1:T(8,128)} %copy-done.3, f32[4096,128]{0,1:T(8,128)S(1)} %bitcast.169), kind=kOutput, calls=%fused_computation.8 | convolution fusion | flops 25796018176 | bytes 73424896 | tf_op jit(solution)/shard_map/ak,bk->ab/dot_general | solution.py:105
  1280.5 33.3 %copy.19 = f32[4096,2048]{1,0:T(8,128)} copy(f32[4096,2048]{0,1:T(8,128)} %multiply_multiply_fusion) | data formatting | bytes 67108864
  (125 shorter events, 23.4 us)
Async XLA Ops:
  7.2 698.8 %all-reduce.20.cloned.1.call-start = ((), (), s32[]{:S(2)}) async-start(), calls=%async_computation.5 | async-start | bytes 8388608 | tf_op jit(solution)/shard_map/psum | solution.py:20
  7.2 362.3 %collective-permute-start = (f32[4096,1024]{1,0:T(8,128)}, f32[4096,1024]{1,0:T(8,128)}, u32[]{:S(2)}, u32[]{:S(2)}) collective-permute-start(f32[4096,1024]{1,0:T(8,128)} %param.9), channel_id=1, source_target_pairs={{0,4},{4,0},{1,5},{5,1},{2,6},{6,2},{3,7},{7,3},{8,12},{12,8},{9,1... | collective-permute-start | bytes 50331656 | tf_op jit(solution)/shard_map/ppermute | solution.py:15
  15.4 16.0 %copy-start.8 = (f32[4096]{0:T(1024)S(1)}, f32[4096]{0:T(1024)}, u32[]{:S(2)}) copy-start(f32[4096]{0:T(1024)} %param.10) | copy-start | bytes 49156
  549.3 199.9 %all-reduce.10.cloned.1.call-start = ((), (), s32[]{:S(2)}) async-start(), calls=%async_computation | async-start | bytes 524288 | tf_op jit(solution)/shard_map/psum | solution.py:94
  706.0 2.2 copy-start.4
  709.2 174.1 %all-reduce.12.cloned.1.call-start = ((), (), s32[]{:S(2)}) async-start(), calls=%async_computation.1 | async-start | bytes 4194304 | tf_op jit(solution)/shard_map/psum | solution.py:20
  811.6 3.7 copy-start.5
  819.3 1.3 copy-start.2
  822.2 260.2 %all-reduce.18.cloned.1.call-start = ((), (), s32[]{:S(2)}) async-start(), calls=%async_computation.4 | async-start | bytes 8388608 | tf_op jit(solution)/shard_map/psum | solution.py:20
  926.0 181.1 %all-reduce.14.cloned.1.call-start = ((), (), s32[]{:S(2)}) async-start(), calls=%async_computation.2 | async-start | bytes 524288 | tf_op jit(solution)/shard_map/psum | solution.py:94
  1082.4 2.2 copy-start.6
  1085.6 157.3 %all-reduce.16.cloned.1.call-start = ((), (), s32[]{:S(2)}) async-start(), calls=%async_computation.3 | async-start | bytes 4194304 | tf_op jit(solution)/shard_map/psum | solution.py:20
  1169.3 3.7 copy-start.7
  1173.0 4.6 copy-start
  1177.0 1.3 copy-start.3
  1184.8 58.1 %copy-start.1 = (f32[128,4096]{1,0:T(8,128)S(1)}, f32[128,4096]{1,0:T(8,128)}, u32[]{:S(2)}) copy-start(f32[128,4096]{1,0:T(8,128)} %copy-done) | copy-start | bytes 6291460
Sparse Core Ops, SparseCore 0:
  549.4 156.5 all-reduce.19
  709.3 21.2 all-reduce.9
  822.3 60.9 all-reduce.11
  926.1 156.2 all-reduce.17
  1085.7 21.2 all-reduce.13
  1179.9 62.9 all-reduce.15
where the time goes:
time: 1330 us; the launch traced here: 1320 us
  waiting for transfers between devices  753 us (57%)
  matrix products  219 us (16%)
  local copies, waits for them, and re-layouts  147 us (11%)
  other arithmetic  133 us (10%)
  between operations  66.6 us (5%)
    psum x4, waiting for transfers between devices, broadcast(): return lax.psum(jnp.where(mine, shard, jnp.zeros_like(shard)), axis)  422 us
    ppermute x1, waiting for transfers between devices, swapped(): lax.ppermute(shard, axis, [(i, i ^ 1 << bit) for i in range(lax.axis_size...  311 us
    unnamed x25, local copies, waits for them, and re-layouts  101 us
    dot_general x2, matrix products, per_device(): update = jnp.einsum('ak,bk->ab', factor, across, precision=highest)  75.5 us
    dot_general x2, matrix products, place_blocks(): placed = jnp.einsum('li,kaib->kalb', col_select, placed, precision=highest)  73.2 us
    another operation x14, other arithmetic, per_device(): lower_factor = jnp.linalg.cholesky(pivot_block)  69.3 us
    dot_general x2, matrix products, place_blocks(): placed = jnp.einsum('kj,jaib->kaib', row_select, blocks, precision=highest)  53.7 us
    another operation x5, other arithmetic, per_device(): lax.linalg.triangular_solve(lower_factor, panel_cols, left_side=False, lo...  39.4 us
  transfers between devices with their start and end apart: 7, of which 6 were waited for; matrix products, arithmetic and copies ran while one was open for 4% of the time, Pallas kernels for 0%

commit v1 on v0

v1 whole, which is shorter than its diff:
```python
import functools

import jax
import jax.numpy as jnp
import numpy as np
from jax import lax
from jax.experimental import pallas as pl
from jax.experimental.pallas import tpu as pltpu
from jax.sharding import PartitionSpec as P

NF = 8192
BLK = 128
CHUNKS = 4
ROWS_AT_ONCE = 2

highest = lax.Precision.HIGHEST


def swapped(shard, axis, bit):
    return lax.ppermute(shard, axis, [(i, i ^ 1 << bit) for i in range(lax.axis_size(axis))])


def tied(values, after):
    return lax.optimization_barrier((values, after))[0]


def spread_plan(rows, cols):
    sources = cols // rows
    where = -np.ones((sources, rows, cols), np.int32)
    for r in range(rows):
        for s in range(sources):
            where[s, r, r + s * rows] = 0
    steps = []
    while (where < 0).any():
        for buffer in range(len(steps) + 1):
            moves = []
            for r in range(rows):
                sign = 1 if r <= cols - 1 - (r + (sources - 1) * rows) else -1
                taken = set()
                for h in range(cols)[::sign]:
                    for s in range(sources):
                        if where[s, r, h] != buffer:
                            continue
                        open_to = [
                            d for d in range(cols)
                            if where[s, r, d] < 0 and d not in taken and abs(d - h) <= rows
                        ]
                        if open_to:
                            d = max(open_to, key=lambda d: sign * (d - h))
                            taken.add(d)
                            moves.append((s, r, h, d))
            if moves:
                break
        steps.append((buffer, [(r * cols + h, r * cols + d) for _, r, h, d in moves]))
        for s, r, _, d in moves:
            where[s, r, d] = len(steps)
    return steps, where


def fold_plan(where):
    sources, rows, cols = where.shape
    steps = where.max()
    order = -np.ones((steps + 1, rows, cols), np.int32)
    folded = np.zeros_like(where)
    for r in range(rows):
        for d in range(cols):
            got = sorted((where[s, r, d], s) for s in range(sources) if where[s, r, d] > 0)
            for n, (step, s) in enumerate(got):
                order[step, r, d] = n
                folded[s, r, d] = n + 1
    return order, folded


class Meta:
    def __init__(self, child_blocks, pivot_count, sources):
        self.child_blocks, self.pivot_count, self.sources = child_blocks, pivot_count, sources

    def pack(self, child_map, pivots, row_index, col_index, where):
        place = jnp.stack([row_index, col_index]).astype(jnp.int32)
        held = jnp.asarray(where)[:, row_index, col_index]
        return jnp.concatenate([child_map.reshape(-1), pivots, place, held])

    def has(self, meta, child, block, front_block):
        return meta[child * self.child_blocks + block] == front_block

    def pivot(self, meta, p):
        return meta[2 * self.child_blocks + p]

    def row(self, meta):
        return meta[2 * self.child_blocks + self.pivot_count]

    def col(self, meta):
        return meta[2 * self.child_blocks + self.pivot_count + 1]

    def held(self, meta, s):
        return meta[2 * self.child_blocks + self.pivot_count + 2 + s]

    def is_pivot(self, meta, front_block):
        hit = front_block == self.pivot(meta, 0)
        for p in range(1, self.pivot_count):
            hit = jnp.logical_or(hit, front_block == self.pivot(meta, p))
        return hit


def as_float(flag):
    return jnp.where(flag, 1.0, 0.0).astype(jnp.float32)


def eye_mask():
    return lax.broadcasted_iota(jnp.int32, (BLK, BLK), 0) == lax.broadcasted_iota(jnp.int32, (BLK, BLK), 1)


def split(value):
    high = value.astype(jnp.bfloat16)
    return high, (value - high.astype(jnp.float32)).astype(jnp.bfloat16)


def dot_t(a, b):
    return lax.dot_general(
        a, b, (((1,), (1,)), ((), ())), precision=highest, preferred_element_type=jnp.float32
    )


def dot(a, b):
    return jnp.dot(a, b, precision=highest, preferred_element_type=jnp.float32)


def pick_kernel(info, rows, cols, meta, child, diag, panel, pivot_part):
    half = rows // 2
    r, q = info.row(meta), info.col(meta)
    mine, within = r // half, r % half
    p = pl.program_id(0)
    front_block = info.pivot(meta, p)
    block = front_block % info.child_blocks
    present = jnp.logical_and(info.has(meta, mine, block, front_block), block % half == within)
    panel[0] = child[0] * as_float(present)
    first = p * (p + 1) // 2
    for t in range(info.pivot_count):
        other = info.pivot(meta, t)
        other_block = other % info.child_blocks
        here = jnp.logical_and(info.has(meta, mine, other_block, other), other_block % cols == q)

        @pl.when(t <= p)
        def _():
            at = pl.multiple_of(other_block // cols * BLK, BLK)
            pivot_part[first + t] = panel[0, :, pl.ds(at, BLK)] * as_float(here)

    on_diagonal = jnp.logical_and(front_block % rows == r, front_block % cols == q)

    @pl.when(on_diagonal)
    def _():
        pivot_part[first + p] += jnp.where(eye_mask(), diag[0], 0.0)


def cholesky_kernel(count, blocks, lower, inverse, work, rest):
    at = lambda i, j: i * (i + 1) // 2 + j
    span = lambda i: slice(i * BLK, (i + 1) * BLK)
    lower[...] = jnp.zeros_like(lower)
    inverse[...] = jnp.zeros_like(inverse)
    rest[...] = blocks[...]
    row_ids = lax.broadcasted_iota(jnp.int32, (BLK, BLK), 0)
    col_ids = lax.broadcasted_iota(jnp.int32, (BLK, BLK), 1)
    wide_ids = lax.broadcasted_iota(jnp.int32, (1, 2 * BLK), 1)
    column_ids = lax.broadcasted_iota(jnp.int32, (BLK, 1), 0)
    for p in range(count):
        work[:, :BLK] = rest[at(p, p)]
        work[:, BLK:] = jnp.where(row_ids == col_ids, 1.0, 0.0)

        def eliminate(j, carry):
            row = work[pl.ds(j, 1), :]
            lead = jnp.sum(jnp.where(wide_ids == j, row, 0.0), axis=1, keepdims=True)
            left = work[:, :BLK]
            column = jnp.sum(jnp.where(col_ids == j, left, 0.0), axis=1, keepdims=True)
            column = jnp.where(column_ids > j, column, 0.0)
            scaled = row / lead
            work[...] = work[...] - column * scaled
            return carry

        lax.fori_loop(0, BLK, eliminate, 0)
        left = work[:, :BLK]
        lead = jnp.sum(jnp.where(row_ids == col_ids, left, 0.0), axis=1, keepdims=True)
        scale = 1.0 / jnp.sqrt(lead)
        lower[span(p), span(p)] = jnp.where(row_ids <= col_ids, left * scale, 0.0).T
        inverse[span(p), span(p)] = work[:, BLK:] * scale
        own_inverse = inverse[span(p), span(p)]
        for i in range(p + 1, count):
            lower[span(i), span(p)] = dot_t(rest[at(i, p)], own_inverse)
        for i in range(p + 1, count):
            for k in range(p + 1, i + 1):
                rest[at(i, k)] -= dot_t(lower[span(i), span(p)], lower[span(k), span(p)])
    for i in range(1, count):
        for j in range(i):
            known = slice(j * BLK, i * BLK)
            partial = dot(lower[span(i), known], inverse[known, span(j)])
            inverse[span(i), span(j)] = -dot(inverse[span(i), span(i)], partial)


def columns_kernel(info, rows, cols, child_slots, width, meta, own, other, inverse, high, low):
    r, q = info.row(meta), info.col(meta)
    mine = r // (rows // 2)
    v, step = pl.program_id(0), pl.program_id(1)
    parts = []
    for i in range(width):
        block = (step * width + i) * cols + q
        front_block = block + v * info.child_blocks
        keep = jnp.logical_not(info.is_pivot(meta, front_block))
        lanes = slice(i * BLK, (i + 1) * BLK)
        take = as_float(jnp.logical_and(keep, info.has(meta, mine, block, front_block)))
        take_other = as_float(jnp.logical_and(keep, info.has(meta, 1 - mine, block, front_block)))
        parts.append(own[:, lanes] * take + other[:, lanes] * take_other)
    high[...], low[...] = split(dot(inverse[...], jnp.concatenate(parts, axis=1)))


def rows_kernel(info, rows, cols, width, share, held_count, meta, *refs):
    own, other = refs[:held_count], refs[held_count : 2 * held_count]
    lower, inverse, factor, high, low, work = refs[2 * held_count :]
    r, q = info.row(meta), info.col(meta)
    mine = r // (rows // 2)
    s, step = pl.program_id(0), pl.program_id(1)
    holder = info.held(meta, s)

    def chosen(pieces):
        value = pieces[0][...]
        for n in range(1, held_count):
            value = jnp.where(holder == n, pieces[n][...], value)
        return value

    mine_value, other_value = chosen(own), chosen(other)
    parts = []
    for v in range(2):
        for i in range(width):
            block = (step * width + i) * cols + r + s * rows
            front_block = block + v * info.child_blocks
            lanes = slice(i * BLK, (i + 1) * BLK)
            take = as_float(info.has(meta, mine, block, front_block))
            take_other = as_float(info.has(meta, 1 - mine, block, front_block))
            parts.append(mine_value[:, lanes] * take + other_value[:, lanes] * take_other)
    work[...] = dot_t(jnp.concatenate(parts, axis=1).T, inverse[...])
    at = pl.multiple_of(q * share // BLK * BLK, BLK)
    for v in range(2):
        for i in range(width):
            n = v * width + i
            high[v, i, 0], low[v, i, 0] = split(work[n * BLK : (n + 1) * BLK, :])
            factor[v, i, 0] = work[n * BLK : (n + 1) * BLK, pl.ds(at, BLK)]
            block = (step * width + i) * cols + r + s * rows
            for p in range(info.pivot_count):

                @pl.when(block + v * info.child_blocks == info.pivot(meta, p))
                def _():
                    factor[v, i, 0] = lower[p * BLK : (p + 1) * BLK, pl.ds(at, BLK)]
                    high[v, i, 0] = jnp.zeros_like(high[v, i, 0])
                    low[v, i, 0] = jnp.zeros_like(low[v, i, 0])


def update_kernel(info, rows, cols, child_slots, width, first, row_half, meta, *refs):
    own, other, high, low, col_high, col_low, diag = refs[:7]
    tile = refs[-1]
    r, q = info.row(meta), info.col(meta)
    mine = r // (rows // 2)
    step = pl.program_id(0)
    depth = high.shape[-1]
    count = 2 * ROWS_AT_ONCE * BLK
    a_high, a_low = high[...].reshape(count, depth), low[...].reshape(count, depth)
    left = jnp.concatenate([a_high, a_low, a_high], axis=1)

    def row_block(u, j):
        return (first + step * ROWS_AT_ONCE + j) * rows + r + u * info.child_blocks

    takes = {}
    for u in range(2):
        for j in range(ROWS_AT_ONCE):
            front_block = row_block(u, j)
            block = front_block - u * info.child_blocks
            keep = jnp.logical_not(info.is_pivot(meta, front_block))
            takes[u, j] = [
                as_float(jnp.logical_and(keep, info.has(meta, c, block, front_block))) for c in (mine, 1 - mine)
            ]
    for v in range(2):
        for start in range(0, child_slots, width):
            lanes = slice((v * child_slots + start) * BLK, (v * child_slots + start + width) * BLK)
            b_high, b_low = col_high[:, lanes], col_low[:, lanes]
            right = jnp.concatenate([b_high, b_high, b_low], axis=0)
            change = jnp.dot(left, right, preferred_element_type=jnp.float32)
            for i in range(width):
                block = (start + i) * cols + q
                front_block = block + v * info.child_blocks
                keep = jnp.logical_not(info.is_pivot(meta, front_block))
                col_takes = [
                    as_float(jnp.logical_and(keep, info.has(meta, c, block, front_block))) for c in (mine, 1 - mine)
                ]
                from_lanes = slice((start + i) * BLK, (start + i + 1) * BLK)
                to_lanes = slice((v * child_slots + start + i) * BLK, (v * child_slots + start + i + 1) * BLK)
                for u in range(2):
                    for j in range(ROWS_AT_ONCE):
                        n = u * ROWS_AT_ONCE + j
                        tile[u, j, :, to_lanes] = (
                            own[j, 0, :, from_lanes] * (takes[u, j][0] * col_takes[0])
                            + other[j, :, from_lanes] * (takes[u, j][1] * col_takes[1])
                            - change[n * BLK : (n + 1) * BLK, i * BLK : (i + 1) * BLK]
                        )
    for u in range(2):
        for j in range(ROWS_AT_ONCE):
            front_block = row_block(u, j)
            keep = jnp.logical_not(info.is_pivot(meta, front_block))

            @pl.when(jnp.logical_and(keep, front_block % cols == q))
            def _():
                at = pl.multiple_of(front_block // cols * BLK, BLK)
                tile[u, j, :, pl.ds(at, BLK)] += jnp.where(eye_mask(), diag[u, j], 0.0)


def params(grid_size, mib=56):
    return pltpu.CompilerParams(
        dimension_semantics=("arbitrary",) * grid_size, vmem_limit_bytes=mib * 1024 * 1024
    )


def per_device(contrib, front_diag, child_map, pivots):
    rows, cols = lax.axis_size("row"), lax.axis_size("col")
    r, q = lax.axis_index("row"), lax.axis_index("col")
    half = rows // 2
    half_bit = half.bit_length() - 1
    sources = cols // rows
    local_rows, child_width = front_diag.shape[0], contrib.shape[1]
    row_slots = local_rows // BLK
    tile_cols = NF // cols
    child_slots = child_width // BLK
    child_rows = contrib.shape[0] // BLK
    row_half = child_rows // 2
    child_blocks, pivot_count = child_map.shape[1], pivots.shape[0]
    depth = pivot_count * BLK
    width = min(2, child_slots)
    steps, where = spread_plan(rows, cols)
    order = None
    if len(steps) > 2 * sources:
        order, where = fold_plan(where)
    held_count = int(where.max()) + 1
    info = Meta(child_blocks, pivot_count, sources)
    meta = info.pack(child_map, pivots, r, q, where)
    f32, bf16 = jnp.float32, jnp.bfloat16
    shape = jax.ShapeDtypeStruct

    lower_count = pivot_count * (pivot_count + 1) // 2
    panel, pivot_part = pl.pallas_call(
        functools.partial(pick_kernel, info, rows, cols),
        grid_spec=pltpu.PrefetchScalarGridSpec(
            num_scalar_prefetch=1,
            grid=(pivot_count,),
            in_specs=[
                pl.BlockSpec(
                    (1, BLK, child_width), lambda p, m: (info.pivot(m, p) % child_blocks // half, 0, 0)
                ),
                pl.BlockSpec((1, 1, BLK), lambda p, m: (info.pivot(m, p) // rows, 0, 0)),
            ],
            out_specs=[
                pl.BlockSpec((1, BLK, child_width), lambda p, m: (p, 0, 0)),
                pl.BlockSpec((lower_count, BLK, BLK), lambda p, m: (0, 0, 0)),
            ],
        ),
        out_shape=[
            shape((pivot_count, BLK, child_width), f32),
            shape((lower_count, BLK, BLK), f32),
        ],
        compiler_params=params(1),
        name="pick",
    )(meta, contrib.reshape(child_rows, BLK, child_width), front_diag.reshape(row_slots, 1, BLK))
    pivot_blocks = lax.psum(pivot_part, ("row", "col"))
    own = panel.reshape(depth, child_width)
    for bit in range(half_bit):
        own = own + swapped(own, "row", bit)
    other = swapped(own, "row", half_bit)

    def spread(piece):
        held = [piece]
        for buffer, pairs in steps:
            held.append(lax.ppermute(held[buffer], ("row", "col"), pairs))
        if order is None:
            return held
        mine_order = jnp.asarray(order)[:, r, q]
        folded = [piece]
        for n in range(held_count - 1):
            folded.append(sum(jnp.where(mine_order[k] == n, held[k], 0.0) for k in range(1, len(held))))
        return folded

    own_held = spread(own)
    other_held = spread(other)

    own_view = contrib.reshape(row_half, 2, BLK, child_width)
    mine = r // half
    chunk = max(row_half // CHUNKS, ROWS_AT_ONCE)
    received = []
    for first in range(0, row_half, chunk):
        part = lax.dynamic_slice(
            own_view, (first, 1 - mine, 0, 0), (chunk, 1, BLK, child_width)
        ).reshape(chunk, BLK, child_width)
        part = tied(part, received[-2] if len(received) > 1 else other)
        received.append(swapped(part, "row", half_bit))

    lower, inverse = pl.pallas_call(
        functools.partial(cholesky_kernel, pivot_count),
        out_shape=[shape((depth, depth), f32), shape((depth, depth), f32)],
        scratch_shapes=[pltpu.VMEM((BLK, 2 * BLK), f32), pltpu.VMEM((lower_count, BLK, BLK), f32)],
        compiler_params=params(0, 32),
        name="factor_pivots",
    )(pivot_blocks)

    lanes = width * BLK
    groups = child_slots // width
    whole = lambda *_: (0, 0)
    col_high, col_low = pl.pallas_call(
        functools.partial(columns_kernel, info, rows, cols, child_slots, width),
        grid_spec=pltpu.PrefetchScalarGridSpec(
            num_scalar_prefetch=1,
            grid=(2, groups),
            in_specs=[
                pl.BlockSpec((depth, lanes), lambda v, g, m: (0, g)),
                pl.BlockSpec((depth, lanes), lambda v, g, m: (0, g)),
                pl.BlockSpec((depth, depth), whole),
            ],
            out_specs=[pl.BlockSpec((depth, lanes), lambda v, g, m: (0, v * groups + g))] * 2,
        ),
        out_shape=[shape((depth, tile_cols), bf16)] * 2,
        compiler_params=params(2),
        name="factor_at_columns",
    )(meta, own, other, inverse)

    share = depth // cols

    def held_spec(n):
        return pl.BlockSpec(
            (depth, lanes), lambda s, g, m: (0, jnp.where(info.held(m, s) == n, g, 0))
        )

    by_group = lambda s, g, m: (0, g, s, 0, 0)
    factor, row_high, row_low = pl.pallas_call(
        functools.partial(rows_kernel, info, rows, cols, width, share, held_count),
        grid_spec=pltpu.PrefetchScalarGridSpec(
            num_scalar_prefetch=1,
            grid=(sources, groups),
            in_specs=[held_spec(n) for n in range(held_count)] * 2 + [pl.BlockSpec((depth, depth), whole)] * 2,
            out_specs=[
                pl.BlockSpec((2, width, 1, BLK, BLK), by_group),
                pl.BlockSpec((2, width, 1, BLK, depth), by_group),
                pl.BlockSpec((2, width, 1, BLK, depth), by_group),
            ],
            scratch_shapes=[pltpu.VMEM((2 * lanes, depth), f32)],
        ),
        out_shape=[
            shape((2, child_slots, sources, BLK, BLK), f32),
            shape((2, child_slots, sources, BLK, depth), bf16),
            shape((2, child_slots, sources, BLK, depth), bf16),
        ],
        compiler_params=params(2),
        name="factor_at_rows",
    )(meta, *own_held, *other_held, lower, inverse)
    row_high = row_high.reshape(2, row_half, BLK, depth)
    row_low = row_low.reshape(2, row_half, BLK, depth)
    factor = factor.reshape(local_rows, BLK)
    if share < BLK:
        factor = lax.dynamic_slice_in_dim(factor, q * share % BLK, share, 1)

    tile = None
    diag_view = front_diag.reshape(2, row_half, 1, BLK)
    for n, part in enumerate(received):
        first = n * chunk
        at = first // ROWS_AT_ONCE
        mine_of = lambda m: info.row(m) // half
        in_specs = [
            pl.BlockSpec((ROWS_AT_ONCE, 1, BLK, child_width), lambda t, m, at=at: (at + t, mine_of(m), 0, 0)),
            pl.BlockSpec((ROWS_AT_ONCE, BLK, child_width), lambda t, m: (t, 0, 0)),
            pl.BlockSpec((2, ROWS_AT_ONCE, BLK, depth), lambda t, m, at=at: (0, at + t, 0, 0)),
            pl.BlockSpec((2, ROWS_AT_ONCE, BLK, depth), lambda t, m, at=at: (0, at + t, 0, 0)),
            pl.BlockSpec((depth, tile_cols), whole),
            pl.BlockSpec((depth, tile_cols), whole),
            pl.BlockSpec((2, ROWS_AT_ONCE, 1, BLK), lambda t, m, at=at: (0, at + t, 0, 0)),
        ]
        operands = [own_view, part, row_high, row_low, col_high, col_low, diag_view]
        aliases = {}
        if tile is not None:
            in_specs.append(pl.BlockSpec(memory_space=pl.ANY))
            operands.append(tile)
            aliases = {len(operands): 0}
        tile = pl.pallas_call(
            functools.partial(update_kernel, info, rows, cols, child_slots, width, first, row_half),
            grid_spec=pltpu.PrefetchScalarGridSpec(
                num_scalar_prefetch=1,
                grid=(chunk // ROWS_AT_ONCE,),
                in_specs=in_specs,
                out_specs=pl.BlockSpec(
                    (2, ROWS_AT_ONCE, BLK, tile_cols), lambda t, m, at=at: (0, at + t, 0, 0)
                ),
            ),
            out_shape=shape((2, row_half, BLK, tile_cols), f32),
            input_output_aliases=aliases,
            compiler_params=params(1),
            name="update_tile",
        )(meta, *operands)
    return factor, tile.reshape(local_rows, tile_cols)


def solution(mesh):
    placed = (P(("front", "row"), "col"), P(("front", "row")), P("front", None), P("front"))
    return jax.shard_map(
        per_device,
        mesh=mesh,
        in_specs=placed,
        out_specs=(P(("front", "row"), "col"), P(("front", "row"), "col")),
        check_vma=False,
    )
```

time: 1330 us -> 436 us (0.33)
  waiting for transfers between devices: 753 us -> 230 us
  matrix products: 219 us -> 0 us
  Pallas kernels: 0 us -> 155 us
  other arithmetic: 133 us -> 0 us
  local copies, waits for them, and re-layouts: 147 us -> 14.2 us
  between operations: 66.6 us -> 14.2 us
  starting transfers between devices: 1.16 us -> 20 us
    psum x6 -> x1, waiting for transfers between devices: 443 us -> 108 us  [per_device(): pivot_blocks = lax.psum(pivot_part, ('row', 'col'))]
    ppermute x1 -> x5, waiting for transfers between devices: 311 us -> 78 us  [swapped(): lax.ppermute(shard, axis, [(i, i ^ 1 << bit) for i in range(lax.axis_size...]
    dot_general x6 -> x0, matrix products: 202 us -> none  [the longest x2 75.5 us: per_device(): update = jnp.einsum('ak,bk->ab', factor, across, precision=highest)]
    pallas_call x0 -> x8, Pallas kernels: none -> 155 us  [the longest x1 58.8 us: per_device(): pl.pallas_call(functools.partial(cholesky_kernel, pivot_count), out_shape...]
    another operation x19 -> x0, other arithmetic: 109 us -> none  [the longest x14 69.3 us: per_device(): lower_factor = jnp.linalg.cholesky(pivot_block)]
    unnamed x25 -> x18, local copies, waits for them, and re-layouts: 101 us -> 4.52 us
    ppermute x0 -> x8, waiting for transfers between devices: none -> 43.5 us  [spread(): held.append(lax.ppermute(held[buffer], ('row', 'col'), pairs))]
    add x1 -> x0, local copies, waits for them, and re-layouts: 31.1 us -> none  [per_device(): front_tile = assembled + diag_part.reshape(local_rows, col_width)]
  transfers between devices with their start and end apart: 7 -> 14, of which waited for: 6 -> 5; matrix products, arithmetic and copies ran while one was open for 4% -> 2% of each run, Pallas kernels for 0% -> 32%
where the time goes in v1:
time: 436 us; the launch traced here: 433 us
  waiting for transfers between devices  230 us (53%)
  Pallas kernels  155 us (36%)
  starting transfers between devices  20 us (5%)
  local copies, waits for them, and re-layouts  14.2 us (3%)
  between operations  14.2 us (3%)
    psum x1, waiting for transfers between devices, per_device(): pivot_blocks = lax.psum(pivot_part, ('row', 'col'))  108 us
    ppermute x5, waiting for transfers between devices, swapped(): lax.ppermute(shard, axis, [(i, i ^ 1 << bit) for i in range(lax.axis_size...  78 us
    pallas_call x1, Pallas kernels, per_device(): pl.pallas_call(functools.partial(cholesky_kernel, pivot_count), out_shape...  58.8 us
    pallas_call x4, Pallas kernels, per_device(): pl.pallas_call(functools.partial(update_kernel, info, rows, cols, child_s...  52.4 us
    ppermute x8, waiting for transfers between devices, spread(): held.append(lax.ppermute(held[buffer], ('row', 'col'), pairs))  43.5 us
    pallas_call x1, Pallas kernels, per_device(): pl.pallas_call(functools.partial(rows_kernel, info, rows, cols, width, sh...  25.6 us
    pallas_call x1, Pallas kernels, per_device(): pl.pallas_call(functools.partial(columns_kernel, info, rows, cols, child_...  13.2 us
    ppermute x8, starting transfers between devices, spread(): held.append(lax.ppermute(held[buffer], ('row', 'col'), pairs))  10.9 us
  transfers between devices with their start and end apart: 14, of which 5 were waited for; matrix products, arithmetic and copies ran while one was open for 2% of the time, Pallas kernels for 32%

profile of v1, /device:TPU:6, one launch (start us, length us, event | category | flops | bytes accessed | tf_op | source)
XLA Modules:
  0.0 432.9 jit_solution(9402846521425809781)
XLA Ops:
  7.2 0.0 all-reduce.2.cloned.1.call-start
  7.2 0.8 reshape.46
  8.0 0.7 fusion
  8.7 1.3 concatenate.3.meta
  9.9 4.9 %pick.1 = (f32[4,128,1024]{2,1,0:T(8,128)}, f32[10,128,128]{2,1,0:T(8,128)}) custom-call(s32[72]{0:T(128)} %concatenate.3.meta, f32[32,128,1024]{2,1,0:T(8,128)} %bitcast.22, f32[32,1,128]{2,1,0:T(1,128)} %bitcast.42), custom_call_target="tpu_custom_call" | custom-call | tf_op jit(solution)/shard_map/pick/pallas_call | solution.py:344
  14.8 0.5 collective-permute-start.4
  15.3 2.0 collective-permute-start.2
  17.3 1.3 collective-permute-start
  18.6 0.0 copy-start.3
  18.6 6.9 %dynamic-slice_bitcast_fusion = (f32[4,128,1024]{2,1,0:T(8,128)S(1)}, f32[4,128,1024]{2,1,0:T(8,128)}, f32[4,128,1024]{2,1,0:T(8,128)S(1)}, f32[4,128,1024]{2,1,0:T(8,128)}) fusion(f32[16,2,128,1024]{3,2,1,0:T(8,128)} %bitcast.23, s32[]{:T(128)S(6)} %select_n.17), kind=kLoop, calls=%fused_computation | loop fusion | bytes 16777220 | tf_op jit(solution)/shard_map/reshape | solution.py:395
  25.5 37.0 %collective-permute-done.4.refs_5_.other = f32[512,1024]{1,0:T(8,128)} collective-permute-done((f32[512,1024]{1,0:T(8,128)}, f32[512,1024]{1,0:T(8,128)}, u32[]{:S(2)}, u32[]{:S(2)}) %collective-permute-start.4) | collective-permute-done | bytes 2097184 | tf_op jit(solution)/shard_map/ppermute | solution.py:20
  62.5 1.3 collective-permute-start.5
  63.8 5.0 %collective-permute-start.9 = (f32[4,128,1024]{2,1,0:T(8,128)S(1)}, f32[4,128,1024]{2,1,0:T(8,128)S(1)}, u32[]{:S(2)}, u32[]{:S(2)}) collective-permute-start(f32[4,128,1024]{2,1,0:T(8,128)S(1)} %get-tuple-element.20), channel_id=1, source_target_pairs={{0,4},{4,0},{1,5},{5,1},{2,6},{6,2},{3,7},{7,3},{8,12},{12,8},{9,1... | collective-permute-start | bytes 6291464 | tf_op jit(solution)/shard_map/ppermute | solution.py:20
  68.8 0.0 collective-permute-start.11
  68.8 0.0 collective-permute-done.2.refs_3_
  68.8 0.8 collective-permute-start.1
  69.6 0.8 collective-permute-done.refs_1_
  70.5 0.8 collective-permute-start.7
  71.3 42.7 %collective-permute-done.5.refs_6_ = f32[512,1024]{1,0:T(8,128)} collective-permute-done((f32[512,1024]{1,0:T(8,128)}, f32[512,1024]{1,0:T(8,128)}, u32[]{:S(2)}, u32[]{:S(2)}) %collective-permute-start.5) | collective-permute-done | bytes 2097184 | tf_op jit(solution)/shard_map/ppermute | solution.py:376
  114.0 2.0 collective-permute-start.6
  115.9 0.0 collective-permute-done.9.refs_1_
  115.9 1.3 collective-permute-start.3
  117.2 41.0 %collective-permute-done.11.refs_1_ = f32[4,128,1024]{2,1,0:T(8,128)S(1)} collective-permute-done((f32[4,128,1024]{2,1,0:T(8,128)S(1)}, f32[4,128,1024]{2,1,0:T(8,128)S(1)}, u32[]{:S(2)}, u32[]{:S(2)}) %collective-permute-start.11) | collective-permute-done | bytes 2097184 | tf_op jit(solution)/shard_map/ppermute | solution.py:20
  158.2 1.5 collective-permute-start.8
  159.7 0.0 collective-permute-done.1.refs_2_
  159.7 2.3 collective-permute-start.12
  162.0 0.0 copy-done.5
  162.0 0.0 collective-permute-done.7.refs_8_
  162.0 1.3 collective-permute-start.10
  163.3 0.1 copy-done.7
  163.4 0.0 all-reduce.2.cloned.1.call-update
  163.4 108.2 %all-reduce.2.cloned.1.call-done.blocks = f32[10,128,128]{2,1,0:T(8,128)} async-done(((f32[10,128,128]{2,1,0:T(8,128)}), f32[10,128,128]{2,1,0:T(8,128)}) %all-reduce.2.cloned.1.call-update) | async-done | bytes 655376 | tf_op jit(solution)/shard_map/psum | solution.py:367
  271.7 1.1 copy-done.2
  272.7 58.8 %factor_pivots.1 = (f32[512,512]{1,0:T(8,128)S(1)}, f32[512,512]{1,0:T(8,128)S(1)}) custom-call(f32[10,128,128]{2,1,0:T(8,128)S(1)} %copy-done.2), custom_call_target="tpu_custom_call" | custom-call | tf_op jit(solution)/shard_map/factor_pivots/pallas_call | solution.py:399
  331.6 1.0 copy-done
  332.6 1.0 copy-done.1
  333.5 13.2 %factor_at_columns.1 = (bf16[512,2048]{1,0:T(8,128)(2,1)}, bf16[512,2048]{1,0:T(8,128)(2,1)}) custom-call(s32[72]{0:T(128)} %concatenate.3.meta, f32[512,1024]{1,0:T(8,128)} %bitcast.39, f32[512,1024]{1,0:T(8,128)} %collective-permute-done.4.refs_5_.other, f32[512,512]{1,0:T(8,128)} %copy-done), custom_call_target="tpu_custom_call" | custom-call | tf_op jit(solution)/shard_map/factor_at_columns/pallas_call | solution.py:410
  346.7 0.0 collective-permute-done.6.refs_7_
  346.7 0.0 collective-permute-done.3.refs_4_
  346.7 0.0 collective-permute-done.8.refs_9_
  346.7 25.6 %factor_at_rows.1 = (f32[2,8,2,128,128]{4,3,2,1,0:T(8,128)}, bf16[2,8,2,128,512]{4,3,2,1,0:T(8,128)(2,1)}, bf16[2,8,2,128,512]{4,3,2,1,0:T(8,128)(2,1)}) custom-call(s32[72]{0:T(128)} %concatenate.3.meta, f32[512,1024]{1,0:T(8,128)} %bitcast.40, f32[512,1024]{1,0:T(8,128)} %collective-permute-done.refs_1_, f32[512,1024]{1,0:T(8,128)} %copy-done.6, ...), custom_call_target="tpu_custom_call" | custom-call | tf_op jit(solution)/shard_map/factor_at_rows/pallas_call | solution.py:435
  372.3 13.0 %update_tile.4.refs_7_ = f32[2,16,128,2048]{3,2,1,0:T(8,128)} custom-call(s32[72]{0:T(128)} %concatenate.3.meta, f32[16,2,128,1024]{3,2,1,0:T(8,128)} %bitcast.24, f32[4,128,1024]{2,1,0:T(8,128)} %copy-done.5, bf16[2,16,128,512]{3,2,1,0:T(8,128)(2,1)} %bitcast.28, bf16[2,16,128,512]{3,2,1,0:T(8,128)(2,1)} %bitcast.32, ...), custom_call_target="tpu_custom_call" | custom-call | tf_op jit(solution)/shard_map/update_tile/pallas_call | solution.py:483
  385.4 13.3 %update_tile.5.refs_7_ = f32[2,16,128,2048]{3,2,1,0:T(8,128)} custom-call(s32[72]{0:T(128)} %concatenate.3.meta, f32[16,2,128,1024]{3,2,1,0:T(8,128)} %bitcast.25, f32[4,128,1024]{2,1,0:T(8,128)} %copy-done.4, bf16[2,16,128,512]{3,2,1,0:T(8,128)(2,1)} %bitcast.29, bf16[2,16,128,512]{3,2,1,0:T(8,128)(2,1)} %bitcast.33, ...), custom_call_target="tpu_custom_call", output_to_operand_aliasing={{}: (8, {})} | custom-call | tf_op jit(solution)/shard_map/update_tile/pallas_call | solution.py:483
  398.6 0.0 collective-permute-done.12.refs_1_
  398.6 13.0 %update_tile.6.refs_7_ = f32[2,16,128,2048]{3,2,1,0:T(8,128)} custom-call(s32[72]{0:T(128)} %concatenate.3.meta, f32[16,2,128,1024]{3,2,1,0:T(8,128)} %bitcast.26, f32[4,128,1024]{2,1,0:T(8,128)} %collective-permute-done.12.refs_1_, bf16[2,16,128,512]{3,2,1,0:T(8,128)(2,1)} %bitcast.30, ...), custom_call_target="tpu_custom_call", output_to_operand_aliasing={{}: (8, {})} | custom-call | tf_op jit(solution)/shard_map/update_tile/pallas_call | solution.py:483
  411.7 0.0 collective-permute-done.10.refs_1_
  411.7 1.4 copy-done.8
  413.1 13.0 %update_tile.7 = f32[2,16,128,2048]{3,2,1,0:T(8,128)} custom-call(s32[72]{0:T(128)} %concatenate.3.meta, f32[16,2,128,1024]{3,2,1,0:T(8,128)} %bitcast.27, f32[4,128,1024]{2,1,0:T(8,128)} %copy-done.8, bf16[2,16,128,512]{3,2,1,0:T(8,128)(2,1)} %bitcast.31, bf16[2,16,128,512]{3,2,1,0:T(8,128)(2,1)} %bitcast.35, ...), custom_call_target="tpu_custom_call", output_to_operand_aliasing={{}: (8, {})} | custom-call | tf_op jit(solution)/shard_map/update_tile/pallas_call | solution.py:483
  (11 shorter events, 0.0 us)
Async XLA Ops:
  7.2 264.5 %all-reduce.2.cloned.1.call-start = ((), (), s32[]{:S(2)}) async-start(), calls=%async_computation | async-start | bytes 1310720 | tf_op jit(solution)/shard_map/psum | solution.py:367
  14.8 47.7 %collective-permute-start.4 = (f32[512,1024]{1,0:T(8,128)}, f32[512,1024]{1,0:T(8,128)}, u32[]{:S(2)}, u32[]{:S(2)}) collective-permute-start(f32[512,1024]{1,0:T(8,128)} %bitcast.36), channel_id=1, source_target_pairs={{0,4},{4,0},{1,5},{5,1},{2,6},{6,2},{3,7},{7,3},{8,12},{12,8},{9,1... | collective-permute-start | bytes 6291464 | tf_op jit(solution)/shard_map/ppermute | solution.py:20
  15.3 53.5 %collective-permute-start.2 = (f32[512,1024]{1,0:T(8,128)}, f32[512,1024]{1,0:T(8,128)}, u32[]{:S(2)}, u32[]{:S(2)}) collective-permute-start(f32[512,1024]{1,0:T(8,128)} %bitcast.37), channel_id=1, source_target_pairs={{2,1},{5,6},{10,9},{13,14},{18,17},{21,22},{26,25},{29,30}} | collective-permute-start | bytes 6291464 | tf_op jit(solution)/shard_map/ppermute | solution.py:376
  17.3 53.1 %collective-permute-start = (f32[512,1024]{1,0:T(8,128)}, f32[512,1024]{1,0:T(8,128)}, u32[]{:S(2)}, u32[]{:S(2)}) collective-permute-start(f32[512,1024]{1,0:T(8,128)} %bitcast.38), channel_id=1, source_target_pairs={{0,2},{2,3},{7,5},{5,4},{8,10},{10,11},{15,13},{13,12},{16,18},{18... | collective-permute-start | bytes 6291464 | tf_op jit(solution)/shard_map/ppermute | solution.py:376
  18.6 50.2 %copy-start.3 = (f32[4,128,1024]{2,1,0:T(8,128)S(1)}, f32[4,128,1024]{2,1,0:T(8,128)}, u32[]{:S(2)}) copy-start(f32[4,128,1024]{2,1,0:T(8,128)} %get-tuple-element.15) | copy-start | bytes 6291460
  62.5 51.5 %collective-permute-start.5 = (f32[512,1024]{1,0:T(8,128)}, f32[512,1024]{1,0:T(8,128)}, u32[]{:S(2)}, u32[]{:S(2)}) collective-permute-start(f32[512,1024]{1,0:T(8,128)} %collective-permute-done.4.refs_5_.other), channel_id=1, source_target_pairs={{0,2},{2,3},{7,5},{5,4},{8,10},{10,11},{15,13},{13,12},{16,18},{18... | collective-permute-start | bytes 6291464 | tf_op jit(solution)/shard_map/ppermute | solution.py:376
  63.8 52.2 %collective-permute-start.9 = (f32[4,128,1024]{2,1,0:T(8,128)S(1)}, f32[4,128,1024]{2,1,0:T(8,128)S(1)}, u32[]{:S(2)}, u32[]{:S(2)}) collective-permute-start(f32[4,128,1024]{2,1,0:T(8,128)S(1)} %get-tuple-element.20), channel_id=1, source_target_pairs={{0,4},{4,0},{1,5},{5,1},{2,6},{6,2},{3,7},{7,3},{8,12},{12,8},{9,1... | collective-permute-start | bytes 6291464 | tf_op jit(solution)/shard_map/ppermute | solution.py:20
  68.8 89.4 %collective-permute-start.11 = (f32[4,128,1024]{2,1,0:T(8,128)S(1)}, f32[4,128,1024]{2,1,0:T(8,128)S(1)}, u32[]{:S(2)}, u32[]{:S(2)}) collective-permute-start(f32[4,128,1024]{2,1,0:T(8,128)S(1)} %get-tuple-element.26), channel_id=1, source_target_pairs={{0,4},{4,0},{1,5},{5,1},{2,6},{6,2},{3,7},{7,3},{8,12},{12,8},{9,1... | collective-permute-start | bytes 6291464 | tf_op jit(solution)/shard_map/ppermute | solution.py:20
  68.8 90.9 %collective-permute-start.1 = (f32[512,1024]{1,0:T(8,128)S(1)}, f32[512,1024]{1,0:T(8,128)S(1)}, u32[]{:S(2)}, u32[]{:S(2)}) collective-permute-start(f32[512,1024]{1,0:T(8,128)S(1)} %bitcast.41), channel_id=1, source_target_pairs={{0,1},{2,0},{7,6},{5,7},{8,9},{10,8},{15,14},{13,15},{16,17},{18,1... | collective-permute-start | bytes 6291464 | tf_op jit(solution)/shard_map/ppermute | solution.py:376
  70.5 91.5 %collective-permute-start.7 = (f32[512,1024]{1,0:T(8,128)}, f32[512,1024]{1,0:T(8,128)S(1)}, u32[]{:S(2)}, u32[]{:S(2)}) collective-permute-start(f32[512,1024]{1,0:T(8,128)} %collective-permute-done.4.refs_5_.other), channel_id=1, source_target_pairs={{2,1},{5,6},{10,9},{13,14},{18,17},{21,22},{26,25},{29,30}} | collective-permute-start | bytes 6291464 | tf_op jit(solution)/shard_map/ppermute | solution.py:376
  114.0 232.8 %collective-permute-start.6 = (f32[512,1024]{1,0:T(8,128)}, f32[512,1024]{1,0:T(8,128)}, u32[]{:S(2)}, u32[]{:S(2)}) collective-permute-start(f32[512,1024]{1,0:T(8,128)} %collective-permute-done.4.refs_5_.other), channel_id=1, source_target_pairs={{0,1},{2,0},{7,6},{5,7},{8,9},{10,8},{15,14},{13,15},{16,17},{18,1... | collective-permute-start | bytes 6291464 | tf_op jit(solution)/shard_map/ppermute | solution.py:376
  115.9 43.8 %copy-start.4 = (f32[4,128,1024]{2,1,0:T(8,128)}, f32[4,128,1024]{2,1,0:T(8,128)S(1)}, u32[]{:S(2)}) copy-start(f32[4,128,1024]{2,1,0:T(8,128)S(1)} %collective-permute-done.9.refs_1_) | copy-start | bytes 6291460
  115.9 230.8 %collective-permute-start.3 = (f32[512,1024]{1,0:T(8,128)}, f32[512,1024]{1,0:T(8,128)}, u32[]{:S(2)}, u32[]{:S(2)}) collective-permute-start(f32[512,1024]{1,0:T(8,128)} %collective-permute-done.refs_1_), channel_id=1, source_target_pairs={{2,3},{5,4},{10,11},{13,12},{18,19},{21,20},{26,27},{29,28}} | collective-permute-start | bytes 6291464 | tf_op jit(solution)/shard_map/ppermute | solution.py:376
  158.2 3.8 copy-start.5
  158.2 188.5 %collective-permute-start.8 = (f32[512,1024]{1,0:T(8,128)}, f32[512,1024]{1,0:T(8,128)}, u32[]{:S(2)}, u32[]{:S(2)}) collective-permute-start(f32[512,1024]{1,0:T(8,128)} %collective-permute-done.5.refs_6_), channel_id=1, source_target_pairs={{2,3},{5,4},{10,11},{13,12},{18,19},{21,20},{26,27},{29,28}} | collective-permute-start | bytes 6291464 | tf_op jit(solution)/shard_map/ppermute | solution.py:376
  159.7 2.3 copy-start.6
  159.7 238.9 %collective-permute-start.12 = (f32[4,128,1024]{2,1,0:T(8,128)}, f32[4,128,1024]{2,1,0:T(8,128)}, u32[]{:S(2)}, u32[]{:S(2)}) collective-permute-start(f32[4,128,1024]{2,1,0:T(8,128)} %get-tuple-element.27), channel_id=1, source_target_pairs={{0,4},{4,0},{1,5},{5,1},{2,6},{6,2},{3,7},{7,3},{8,12},{12,8},{9,1... | collective-permute-start | bytes 6291464 | tf_op jit(solution)/shard_map/ppermute | solution.py:20
  162.0 1.4 copy-start.7
  162.0 249.6 %collective-permute-start.10 = (f32[4,128,1024]{2,1,0:T(8,128)}, f32[4,128,1024]{2,1,0:T(8,128)S(1)}, u32[]{:S(2)}, u32[]{:S(2)}) collective-permute-start(f32[4,128,1024]{2,1,0:T(8,128)} %get-tuple-element.21), channel_id=1, source_target_pairs={{0,4},{4,0},{1,5},{5,1},{2,6},{6,2},{3,7},{7,3},{8,12},{12,8},{9,1... | collective-permute-start | bytes 6291464 | tf_op jit(solution)/shard_map/ppermute | solution.py:20
  271.7 1.1 copy-start.2
  331.6 1.0 copy-start
  332.6 1.0 copy-start.1
  411.7 1.4 copy-start.8
Sparse Core Ops, SparseCore 0:
  163.5 108.0 all-reduce.1

commit v2 on v1

--- a/solution.py
+++ b/solution.py
@@ -10,7 +10,7 @@
 
 NF = 8192
 BLK = 128
-CHUNKS = 4
+CHUNKS = (10, 4, 2)
 ROWS_AT_ONCE = 2
 
 highest = lax.Precision.HIGHEST
@@ -211,101 +211,94 @@
     high[...], low[...] = split(dot(inverse[...], jnp.concatenate(parts, axis=1)))
 
 
-def rows_kernel(info, rows, cols, width, share, held_count, meta, *refs):
-    own, other = refs[:held_count], refs[held_count : 2 * held_count]
-    lower, inverse, factor, high, low, work = refs[2 * held_count :]
+def chosen(holder, pieces):
+    value = pieces[0][...]
+    for n in range(1, len(pieces)):
+        value = jnp.where(holder == n, pieces[n][...], value)
+    return value
+
+
+def rows_first_kernel(info, meta, *refs):
+    pieces, inverse, product = refs[:-2], refs[-2], refs[-1]
+    product[0] = dot_t(chosen(info.held(meta, pl.program_id(0)), pieces).T, inverse[...])
+
+
+def rows_kernel(info, rows, cols, width, share, meta, *refs):
+    pieces = refs[:-7]
+    own, lower, inverse, factor, high, low, work = refs[-7:]
     r, q = info.row(meta), info.col(meta)
     mine = r // (rows // 2)
     s, step = pl.program_id(0), pl.program_id(1)
-    holder = info.held(meta, s)
-
-    def chosen(pieces):
-        value = pieces[0][...]
-        for n in range(1, held_count):
-            value = jnp.where(holder == n, pieces[n][...], value)
-        return value
-
-    mine_value, other_value = chosen(own), chosen(other)
-    parts = []
-    for v in range(2):
-        for i in range(width):
-            block = (step * width + i) * cols + r + s * rows
+    other = dot_t(chosen(info.held(meta, s), pieces).T, inverse[...])
+    at = pl.multiple_of(q * share // BLK * BLK, BLK)
+    for i in range(width):
+        block = (step * width + i) * cols + r + s * rows
+        span = slice(i * BLK, (i + 1) * BLK)
+        for v in range(2):
             front_block = block + v * info.child_blocks
-            lanes = slice(i * BLK, (i + 1) * BLK)
             take = as_float(info.has(meta, mine, block, front_block))
             take_other = as_float(info.has(meta, 1 - mine, block, front_block))
-            parts.append(mine_value[:, lanes] * take + other_value[:, lanes] * take_other)
-    work[...] = dot_t(jnp.concatenate(parts, axis=1).T, inverse[...])
-    at = pl.multiple_of(q * share // BLK * BLK, BLK)
-    for v in range(2):
-        for i in range(width):
-            n = v * width + i
-            high[v, i, 0], low[v, i, 0] = split(work[n * BLK : (n + 1) * BLK, :])
-            factor[v, i, 0] = work[n * BLK : (n + 1) * BLK, pl.ds(at, BLK)]
-            block = (step * width + i) * cols + r + s * rows
+            value = own[0, span, :] * take + other[span, :] * take_other
+            high[v, i, 0], low[v, i, 0] = split(value)
+            work[...] = value
+            factor[v, i, 0] = work[:, pl.ds(at, BLK)]
             for p in range(info.pivot_count):
 
-                @pl.when(block + v * info.child_blocks == info.pivot(meta, p))
+                @pl.when(front_block == info.pivot(meta, p))
                 def _():
                     factor[v, i, 0] = lower[p * BLK : (p + 1) * BLK, pl.ds(at, BLK)]
                     high[v, i, 0] = jnp.zeros_like(high[v, i, 0])
                     low[v, i, 0] = jnp.zeros_like(low[v, i, 0])
 
 
-def update_kernel(info, rows, cols, child_slots, width, first, row_half, meta, *refs):
+def update_kernel(info, rows, cols, child_slots, width, first, meta, *refs):
     own, other, high, low, col_high, col_low, diag = refs[:7]
     tile = refs[-1]
     r, q = info.row(meta), info.col(meta)
     mine = r // (rows // 2)
-    step = pl.program_id(0)
+    step, v = pl.program_id(0), pl.program_id(1)
     depth = high.shape[-1]
     count = 2 * ROWS_AT_ONCE * BLK
     a_high, a_low = high[...].reshape(count, depth), low[...].reshape(count, depth)
     left = jnp.concatenate([a_high, a_low, a_high], axis=1)
 
-    def row_block(u, j):
-        return (first + step * ROWS_AT_ONCE + j) * rows + r + u * info.child_blocks
-
-    takes = {}
+    def takes(block, front_block):
+        keep = jnp.logical_not(info.is_pivot(meta, front_block))
+        return [as_float(jnp.logical_and(keep, info.has(meta, c, block, front_block))) for c in (mine, 1 - mine)]
+
+    def row_block(j):
+        return (first + step * ROWS_AT_ONCE + j) * rows + r
+
+    row_takes = {
+        (u, j): takes(row_block(j), row_block(j) + u * info.child_blocks)
+        for u in range(2)
+        for j in range(ROWS_AT_ONCE)
+    }
+    for start in range(0, child_slots, width):
+        at = pl.multiple_of((v * child_slots + start) * BLK, BLK)
+        b_high, b_low = col_high[:, pl.ds(at, width * BLK)], col_low[:, pl.ds(at, width * BLK)]
+        right = jnp.concatenate([b_high, b_high, b_low], axis=0)
+        change = jnp.dot(left, right, preferred_element_type=jnp.float32)
+        for i in range(width):
+            block = (start + i) * cols + q
+            col_takes = takes(block, block + v * info.child_blocks)
+            lanes = slice((start + i) * BLK, (start + i + 1) * BLK)
+            for (u, j), row_take in row_takes.items():
+                n = u * ROWS_AT_ONCE + j
+                tile[u, j, :, lanes] = (
+                    own[j, 0, :, lanes] * (row_take[0] * col_takes[0])
+                    + other[j, :, lanes] * (row_take[1] * col_takes[1])
+                    - change[n * BLK : (n + 1) * BLK, i * BLK : (i + 1) * BLK]
+                )
     for u in range(2):
         for j in range(ROWS_AT_ONCE):
-            front_block = row_block(u, j)
-            block = front_block - u * info.child_blocks
-            keep = jnp.logical_not(info.is_pivot(meta, front_block))
-            takes[u, j] = [
-                as_float(jnp.logical_and(keep, info.has(meta, c, block, front_block))) for c in (mine, 1 - mine)
-            ]
-    for v in range(2):
-        for start in range(0, child_slots, width):
-            lanes = slice((v * child_slots + start) * BLK, (v * child_slots + start + width) * BLK)
-            b_high, b_low = col_high[:, lanes], col_low[:, lanes]
-            right = jnp.concatenate([b_high, b_high, b_low], axis=0)
-            change = jnp.dot(left, right, preferred_element_type=jnp.float32)
-            for i in range(width):
-                block = (start + i) * cols + q
-                front_block = block + v * info.child_blocks
-                keep = jnp.logical_not(info.is_pivot(meta, front_block))
-                col_takes = [
-                    as_float(jnp.logical_and(keep, info.has(meta, c, block, front_block))) for c in (mine, 1 - mine)
-                ]
-                from_lanes = slice((start + i) * BLK, (start + i + 1) * BLK)
-                to_lanes = slice((v * child_slots + start + i) * BLK, (v * child_slots + start + i + 1) * BLK)
-                for u in range(2):
-                    for j in range(ROWS_AT_ONCE):
-                        n = u * ROWS_AT_ONCE + j
-                        tile[u, j, :, to_lanes] = (
-                            own[j, 0, :, from_lanes] * (takes[u, j][0] * col_takes[0])
-                            + other[j, :, from_lanes] * (takes[u, j][1] * col_takes[1])
-                            - change[n * BLK : (n + 1) * BLK, i * BLK : (i + 1) * BLK]
-                        )
-    for u in range(2):
-        for j in range(ROWS_AT_ONCE):
-            front_block = row_block(u, j)
-            keep = jnp.logical_not(info.is_pivot(meta, front_block))
-
-            @pl.when(jnp.logical_and(keep, front_block % cols == q))
+            front_block = row_block(j) + u * info.child_blocks
+            slot = front_block // cols
+            here = jnp.logical_and(front_block % cols == q, slot // child_slots == v)
+
+            @pl.when(jnp.logical_and(here, jnp.logical_not(info.is_pivot(meta, front_block))))
             def _():
-                at = pl.multiple_of(front_block // cols * BLK, BLK)
+                at = pl.multiple_of(slot % child_slots * BLK, BLK)
                 tile[u, j, :, pl.ds(at, BLK)] += jnp.where(eye_mask(), diag[u, j], 0.0)
 
 
@@ -329,7 +322,7 @@
     row_half = child_rows // 2
     child_blocks, pivot_count = child_map.shape[1], pivots.shape[0]
     depth = pivot_count * BLK
-    width = min(2, child_slots)
+    width = min(4, child_slots)
     steps, where = spread_plan(rows, cols)
     order = None
     if len(steps) > 2 * sources:
@@ -364,16 +357,25 @@
         compiler_params=params(1),
         name="pick",
     )(meta, contrib.reshape(child_rows, BLK, child_width), front_diag.reshape(row_slots, 1, BLK))
-    pivot_blocks = lax.psum(pivot_part, ("row", "col"))
+    pivot_blocks = pivot_part
+    first_blocks = None
+    for bit in range(cols.bit_length() - 1):
+        received_blocks = swapped(pivot_blocks, "col", bit)
+        first_blocks = received_blocks if first_blocks is None else first_blocks
+        pivot_blocks = pivot_blocks + received_blocks
+    for bit in range(half_bit, -1, -1):
+        received_blocks = swapped(pivot_blocks, "row", bit)
+        pivot_blocks = pivot_blocks + received_blocks
     own = panel.reshape(depth, child_width)
     for bit in range(half_bit):
         own = own + swapped(own, "row", bit)
     other = swapped(own, "row", half_bit)
 
-    def spread(piece):
+    def spread(piece, late=(), wait=None):
         held = [piece]
-        for buffer, pairs in steps:
-            held.append(lax.ppermute(held[buffer], ("row", "col"), pairs))
+        for n, (buffer, pairs) in enumerate(steps):
+            sent = tied(held[buffer], wait) if n in late else held[buffer]
+            held.append(lax.ppermute(sent, ("row", "col"), pairs))
         if order is None:
             return held
         mine_order = jnp.asarray(order)[:, r, q]
@@ -382,19 +384,7 @@
             folded.append(sum(jnp.where(mine_order[k] == n, held[k], 0.0) for k in range(1, len(held))))
         return folded
 
-    own_held = spread(own)
-    other_held = spread(other)
-
-    own_view = contrib.reshape(row_half, 2, BLK, child_width)
-    mine = r // half
-    chunk = max(row_half // CHUNKS, ROWS_AT_ONCE)
-    received = []
-    for first in range(0, row_half, chunk):
-        part = lax.dynamic_slice(
-            own_view, (first, 1 - mine, 0, 0), (chunk, 1, BLK, child_width)
-        ).reshape(chunk, BLK, child_width)
-        part = tied(part, received[-2] if len(received) > 1 else other)
-        received.append(swapped(part, "row", half_bit))
+    own_held = spread(tied(own, first_blocks))
 
     lower, inverse = pl.pallas_call(
         functools.partial(cholesky_kernel, pivot_count),
@@ -402,7 +392,22 @@
         scratch_shapes=[pltpu.VMEM((BLK, 2 * BLK), f32), pltpu.VMEM((lower_count, BLK, BLK), f32)],
         compiler_params=params(0, 32),
         name="factor_pivots",
-    )(pivot_blocks)
+    )(tied(pivot_blocks, [own_held[n] for n in (1, 3) if n < held_count]))
+
+    other_held = spread(other, [n for n, (_, pairs) in enumerate(steps) if n not in (0, 2)], inverse)
+
+    own_view = contrib.reshape(row_half, 2, BLK, child_width)
+    mine = r // half
+    chunks = CHUNKS if sum(CHUNKS) == row_half else (ROWS_AT_ONCE,) * (row_half // ROWS_AT_ONCE)
+    received = []
+    first = 0
+    for chunk in chunks:
+        part = lax.dynamic_slice(
+            own_view, (first, 1 - mine, 0, 0), (chunk, 1, BLK, child_width)
+        ).reshape(chunk, BLK, child_width)
+        part = tied(part, (received[-2] if len(received) > 1 else own, inverse) if received else (other, received_blocks))
+        received.append(swapped(part, "row", half_bit))
+        first += chunk
 
     lanes = width * BLK
     groups = child_slots // width
@@ -432,18 +437,32 @@
         )
 
     by_group = lambda s, g, m: (0, g, s, 0, 0)
-    factor, row_high, row_low = pl.pallas_call(
-        functools.partial(rows_kernel, info, rows, cols, width, share, held_count),
+    own_rows = pl.pallas_call(
+        functools.partial(rows_first_kernel, info),
         grid_spec=pltpu.PrefetchScalarGridSpec(
             num_scalar_prefetch=1,
             grid=(sources, groups),
-            in_specs=[held_spec(n) for n in range(held_count)] * 2 + [pl.BlockSpec((depth, depth), whole)] * 2,
+            in_specs=[held_spec(n) for n in range(held_count)] + [pl.BlockSpec((depth, depth), whole)],
+            out_specs=pl.BlockSpec((1, lanes, depth), lambda s, g, m: (s, g, 0)),
+        ),
+        out_shape=shape((sources, child_width, depth), f32),
+        compiler_params=params(2),
+        name="factor_at_rows_first",
+    )(meta, *own_held, inverse)
+    factor, row_high, row_low = pl.pallas_call(
+        functools.partial(rows_kernel, info, rows, cols, width, share),
+        grid_spec=pltpu.PrefetchScalarGridSpec(
+            num_scalar_prefetch=1,
+            grid=(sources, groups),
+            in_specs=[held_spec(n) for n in range(held_count)]
+            + [pl.BlockSpec((1, lanes, depth), lambda s, g, m: (s, g, 0))]
+            + [pl.BlockSpec((depth, depth), whole)] * 2,
             out_specs=[
                 pl.BlockSpec((2, width, 1, BLK, BLK), by_group),
                 pl.BlockSpec((2, width, 1, BLK, depth), by_group),
                 pl.BlockSpec((2, width, 1, BLK, depth), by_group),
             ],
-            scratch_shapes=[pltpu.VMEM((2 * lanes, depth), f32)],
+            scratch_shapes=[pltpu.VMEM((BLK, depth), f32)],
         ),
         out_shape=[
             shape((2, child_slots, sources, BLK, BLK), f32),
@@ -452,7 +471,7 @@
         ],
         compiler_params=params(2),
         name="factor_at_rows",
-    )(meta, *own_held, *other_held, lower, inverse)
+    )(meta, *other_held, own_rows, lower, inverse)
     row_high = row_high.reshape(2, row_half, BLK, depth)
     row_low = row_low.reshape(2, row_half, BLK, depth)
     factor = factor.reshape(local_rows, BLK)
@@ -461,18 +480,18 @@
 
     tile = None
     diag_view = front_diag.reshape(2, row_half, 1, BLK)
-    for n, part in enumerate(received):
-        first = n * chunk
+    mine_of = lambda m: info.row(m) // half
+    first = 0
+    for part in received:
         at = first // ROWS_AT_ONCE
-        mine_of = lambda m: info.row(m) // half
         in_specs = [
-            pl.BlockSpec((ROWS_AT_ONCE, 1, BLK, child_width), lambda t, m, at=at: (at + t, mine_of(m), 0, 0)),
-            pl.BlockSpec((ROWS_AT_ONCE, BLK, child_width), lambda t, m: (t, 0, 0)),
-            pl.BlockSpec((2, ROWS_AT_ONCE, BLK, depth), lambda t, m, at=at: (0, at + t, 0, 0)),
-            pl.BlockSpec((2, ROWS_AT_ONCE, BLK, depth), lambda t, m, at=at: (0, at + t, 0, 0)),
+            pl.BlockSpec((ROWS_AT_ONCE, 1, BLK, child_width), lambda t, v, m, at=at: (at + t, mine_of(m), 0, 0)),
+            pl.BlockSpec((ROWS_AT_ONCE, BLK, child_width), lambda t, v, m: (t, 0, 0)),
+            pl.BlockSpec((2, ROWS_AT_ONCE, BLK, depth), lambda t, v, m, at=at: (0, at + t, 0, 0)),
+            pl.BlockSpec((2, ROWS_AT_ONCE, BLK, depth), lambda t, v, m, at=at: (0, at + t, 0, 0)),
             pl.BlockSpec((depth, tile_cols), whole),
             pl.BlockSpec((depth, tile_cols), whole),
-            pl.BlockSpec((2, ROWS_AT_ONCE, 1, BLK), lambda t, m, at=at: (0, at + t, 0, 0)),
+            pl.BlockSpec((2, ROWS_AT_ONCE, 1, BLK), lambda t, v, m, at=at: (0, at + t, 0, 0)),
         ]
         operands = [own_view, part, row_high, row_low, col_high, col_low, diag_view]
         aliases = {}
@@ -481,20 +500,21 @@
             operands.append(tile)
             aliases = {len(operands): 0}
         tile = pl.pallas_call(
-            functools.partial(update_kernel, info, rows, cols, child_slots, width, first, row_half),
+            functools.partial(update_kernel, info, rows, cols, child_slots, width, first),
             grid_spec=pltpu.PrefetchScalarGridSpec(
                 num_scalar_prefetch=1,
-                grid=(chunk // ROWS_AT_ONCE,),
+                grid=(part.shape[0] // ROWS_AT_ONCE, 2),
                 in_specs=in_specs,
                 out_specs=pl.BlockSpec(
-                    (2, ROWS_AT_ONCE, BLK, tile_cols), lambda t, m, at=at: (0, at + t, 0, 0)
+                    (2, ROWS_AT_ONCE, BLK, child_width), lambda t, v, m, at=at: (0, at + t, 0, v)
                 ),
             ),
             out_shape=shape((2, row_half, BLK, tile_cols), f32),
             input_output_aliases=aliases,
-            compiler_params=params(1),
+            compiler_params=params(2),
             name="update_tile",
         )(meta, *operands)
+        first += part.shape[0]
     return factor, tile.reshape(local_rows, tile_cols)
 
 

time: 436 us -> 335 us (0.77)
  waiting for transfers between devices: 230 us -> 107 us
  starting transfers between devices: 20 us -> 43.1 us
  between operations: 14.2 us -> 0.83 us
    psum x1 -> x0, waiting for transfers between devices: 108 us -> none  [per_device(): pivot_blocks = lax.psum(pivot_part, ('row', 'col'))]
    ppermute x5 -> x7, waiting for transfers between devices: 78 us -> 53.1 us  [swapped(): lax.ppermute(shard, axis, [(i, i ^ 1 << bit) for i in range(lax.axis_size...]
    ppermute x5 -> x7, starting transfers between devices: 9.14 us -> 31.6 us  [swapped(): lax.ppermute(shard, axis, [(i, i ^ 1 << bit) for i in range(lax.axis_size...]
    pallas_call x0 -> x1, Pallas kernels: none -> 14 us  [per_device(): pl.pallas_call(functools.partial(rows_first_kernel, info), grid_spec=pltp...]
    ppermute x8, waiting for transfers between devices: 43.5 us -> 54.3 us  [spread(): held.append(lax.ppermute(sent, ('row', 'col'), pairs))]
    pallas_call x1, Pallas kernels: 25.6 us -> 19.3 us  [per_device(): pl.pallas_call(functools.partial(rows_kernel, info, rows, cols, width, sh...]
    pallas_call x4 -> x3, Pallas kernels: 52.4 us -> 49.8 us  [per_device(): pl.pallas_call(functools.partial(update_kernel, info, rows, cols, child_s...]
    reshape x1 -> x3, local copies, waits for them, and re-layouts: 6.91 us -> 8.96 us  [per_device(): part = lax.dynamic_slice(own_view, (first, 1 - mine, 0, 0), (chunk, 1, BL...]
  transfers between devices with their start and end apart: 14 -> 15, of which waited for: 5 -> 5; matrix products, arithmetic and copies ran while one was open for 2% -> 3% of each run, Pallas kernels for 32% -> 44%
where the time goes in v2:
time: 335 us; the launch traced here: 329 us
  Pallas kernels  158 us (47%)
  waiting for transfers between devices  107 us (32%)
  starting transfers between devices  43.1 us (13%)
  local copies, waits for them, and re-layouts  17.7 us (5%)
    pallas_call x1, Pallas kernels, per_device(): pl.pallas_call(functools.partial(cholesky_kernel, pivot_count), out_shape...  58.8 us
    ppermute x8, waiting for transfers between devices, spread(): held.append(lax.ppermute(sent, ('row', 'col'), pairs))  54.3 us
    ppermute x7, waiting for transfers between devices, swapped(): lax.ppermute(shard, axis, [(i, i ^ 1 << bit) for i in range(lax.axis_size...  53.1 us
    pallas_call x3, Pallas kernels, per_device(): pl.pallas_call(functools.partial(update_kernel, info, rows, cols, child_s...  49.8 us
    ppermute x7, starting transfers between devices, swapped(): lax.ppermute(shard, axis, [(i, i ^ 1 << bit) for i in range(lax.axis_size...  31.6 us
    pallas_call x1, Pallas kernels, per_device(): pl.pallas_call(functools.partial(rows_kernel, info, rows, cols, width, sh...  19.3 us
    pallas_call x1, Pallas kernels, per_device(): pl.pallas_call(functools.partial(rows_first_kernel, info), grid_spec=pltp...  14 us
    ppermute x8, starting transfers between devices, spread(): held.append(lax.ppermute(sent, ('row', 'col'), pairs))  11.5 us
  transfers between devices with their start and end apart: 15, of which 5 were waited for; matrix products, arithmetic and copies ran while one was open for 3% of the time, Pallas kernels for 44%

profile of v2, /device:TPU:6, one launch (start us, length us, event | category | flops | bytes accessed | tf_op | source)
XLA Modules:
  0.0 328.5 jit_solution(986711833861630414)
XLA Ops:
  0.6 0.8 reshape.43
  1.4 0.7 fusion
  2.1 1.2 concatenate.3.meta
  3.3 4.9 %pick.1 = (f32[4,128,1024]{2,1,0:T(8,128)}, f32[10,128,128]{2,1,0:T(8,128)}) custom-call(s32[72]{0:T(128)} %concatenate.3.meta, f32[32,128,1024]{2,1,0:T(8,128)} %bitcast.19, f32[32,1,128]{2,1,0:T(1,128)} %bitcast.39), custom_call_target="tpu_custom_call" | custom-call | tf_op jit(solution)/shard_map/pick/pallas_call | solution.py:337
  8.2 0.5 collective-permute-start
  8.7 1.6 collective-permute-start.2
  10.3 14.8 %collective-permute-done.2 = f32[10,128,128]{2,1,0:T(8,128)S(1)} collective-permute-done((f32[10,128,128]{2,1,0:T(8,128)}, f32[10,128,128]{2,1,0:T(8,128)S(1)}, u32[]{:S(2)}, u32[]{:S(2)}) %collective-permute-start.2) | collective-permute-done | bytes 655392 | tf_op jit(solution)/shard_map/ppermute | solution.py:20
  25.1 1.2 add.24
  26.3 2.6 collective-permute-start.3
  29.0 27.6 %collective-permute-done.3 = f32[10,128,128]{2,1,0:T(8,128)S(1)} collective-permute-done((f32[10,128,128]{2,1,0:T(8,128)S(1)}, f32[10,128,128]{2,1,0:T(8,128)S(1)}, u32[]{:S(2)}, u32[]{:S(2)}) %collective-permute-start.3) | collective-permute-done | bytes 655392 | tf_op jit(solution)/shard_map/ppermute | solution.py:20
  56.6 0.1 add.25
  56.7 1.6 collective-permute-start.4
  58.3 3.5 %dynamic-slice_bitcast_fusion = f32[10,128,1024]{2,1,0:T(8,128)S(1)} fusion(f32[16,2,128,1024]{3,2,1,0:T(8,128)} %bitcast.20, s32[]{:T(128)S(6)} %select_n.16), kind=kLoop, calls=%fused_computation | loop fusion | bytes 10485764 | tf_op jit(solution)/shard_map/reshape | solution.py:407
  61.7 10.6 %collective-permute-done.4 = f32[10,128,128]{2,1,0:T(8,128)S(1)} collective-permute-done((f32[10,128,128]{2,1,0:T(8,128)S(1)}, f32[10,128,128]{2,1,0:T(8,128)S(1)}, u32[]{:S(2)}, u32[]{:S(2)}) %collective-permute-start.4) | collective-permute-done | bytes 655392 | tf_op jit(solution)/shard_map/ppermute | solution.py:20
  72.3 1.5 collective-permute-start.12
  73.8 1.3 collective-permute-start.5
  75.1 0.8 collective-permute-start.6
  75.9 1.3 collective-permute-start.1
  77.2 0.8 collective-permute-start.10
  78.0 46.3 %collective-permute-done.5.refs_1_ = f32[512,1024]{1,0:T(8,128)S(1)} collective-permute-done((f32[512,1024]{1,0:T(8,128)S(1)}, f32[512,1024]{1,0:T(8,128)S(1)}, u32[]{:S(2)}, u32[]{:S(2)}) %collective-permute-start.5) | collective-permute-done | bytes 2097184 | tf_op jit(solution)/shard_map/ppermute | solution.py:378
  124.3 1.3 collective-permute-start.11
  125.6 0.1 add.26.blocks
  125.6 0.0 collective-permute-done.6.refs_3_
  125.7 2.2 collective-permute-start.8
  127.8 58.8 %factor_pivots.1 = (f32[512,512]{1,0:T(8,128)S(1)}, f32[512,512]{1,0:T(8,128)S(1)}) custom-call(f32[10,128,128]{2,1,0:T(8,128)S(1)} %add.26.blocks), custom_call_target="tpu_custom_call" | custom-call | tf_op jit(solution)/shard_map/factor_pivots/pallas_call | solution.py:389
  186.6 0.0 collective-permute-done.1.refs_1_
  186.7 2.5 collective-permute-start.7
  189.1 0.0 collective-permute-done.10.refs_2_
  189.1 1.5 collective-permute-start.9
  190.6 3.2 dynamic-slice_bitcast_fusion.1
  193.8 2.3 copy-done.4
  196.1 23.8 %collective-permute-start.14 = (f32[4,128,1024]{2,1,0:T(8,128)}, f32[4,128,1024]{2,1,0:T(8,128)S(1)}, u32[]{:S(2)}, u32[]{:S(2)}) collective-permute-start(f32[4,128,1024]{2,1,0:T(8,128)} %dynamic-slice_bitcast_fusion.1), channel_id=1, source_target_pairs={{0,4},{4,0},{1,5},{5,1},{2,6},{6,2},{3,7},{7,3},{8,12},{12,8},{9,1... | collective-permute-start | bytes 6291464 | tf_op jit(solution)/shard_map/ppermute | solution.py:20
  219.9 2.3 dynamic-slice_bitcast_fusion.2
  222.2 0.0 collective-permute-done.11.refs_4_
  222.2 1.4 copy-done.9
  223.6 0.0 collective-permute-start.13
  223.6 11.3 %factor_at_columns.1 = (bf16[512,2048]{1,0:T(8,128)(2,1)}, bf16[512,2048]{1,0:T(8,128)(2,1)}) custom-call(s32[72]{0:T(128)} %concatenate.3.meta, f32[512,1024]{1,0:T(8,128)} %bitcast.34, f32[512,1024]{1,0:T(8,128)} %copy-done.2, f32[512,512]{1,0:T(8,128)} %copy-done), custom_call_target="tpu_custom_call" | custom-call | tf_op jit(solution)/shard_map/factor_at_columns/pallas_call | solution.py:415
  235.0 14.0 %factor_at_rows_first.1.refs_5_ = f32[2,1024,512]{2,1,0:T(8,128)} custom-call(s32[72]{0:T(128)} %concatenate.3.meta, f32[512,1024]{1,0:T(8,128)} %bitcast.35, f32[512,1024]{1,0:T(8,128)} %copy-done.6, f32[512,1024]{1,0:T(8,128)} %copy-done.8, f32[512,1024]{1,0:T(8,128)} %copy-done.7, f32[512,1024]{1,0:T(8,128)} %copy-done.9, f32[512,512]{1,0:T(8,128)} %copy-done), custom_call_target="tpu_custom_call" | custom-call | tf_op jit(solution)/shard_map/factor_at_rows_first/pallas_call | solution.py:440
  249.0 0.0 collective-permute-done.8.refs_3_
  249.0 0.0 collective-permute-done.7.refs_2_
  249.0 8.1 %collective-permute-done.9.refs_4_ = f32[512,1024]{1,0:T(8,128)} collective-permute-done((f32[512,1024]{1,0:T(8,128)S(1)}, f32[512,1024]{1,0:T(8,128)}, u32[]{:S(2)}, u32[]{:S(2)}) %collective-permute-start.9) | collective-permute-done | bytes 2097184 | tf_op jit(solution)/shard_map/ppermute | solution.py:378
  257.1 19.3 %factor_at_rows.1 = (f32[2,8,2,128,128]{4,3,2,1,0:T(8,128)}, bf16[2,8,2,128,512]{4,3,2,1,0:T(8,128)(2,1)}, bf16[2,8,2,128,512]{4,3,2,1,0:T(8,128)(2,1)}) custom-call(s32[72]{0:T(128)} %concatenate.3.meta, f32[512,1024]{1,0:T(8,128)} %copy-done.2, f32[512,1024]{1,0:T(8,128)} %copy-done.5, f32[512,1024]{1,0:T(8,128)} %collective-permute-done.7.refs_2_, ...), custom_call_target="tpu_custom_call" | custom-call | tf_op jit(solution)/shard_map/factor_at_rows/pallas_call | solution.py:452
  276.4 27.1 %update_tile.3.refs_7_ = f32[2,16,128,2048]{3,2,1,0:T(8,128)} custom-call(s32[72]{0:T(128)} %concatenate.3.meta, f32[16,2,128,1024]{3,2,1,0:T(8,128)} %bitcast.23, f32[10,128,1024]{2,1,0:T(8,128)} %copy-done.4, bf16[2,16,128,512]{3,2,1,0:T(8,128)(2,1)} %bitcast.27, bf16[2,16,128,512]{3,2,1,0:T(8,128)(2,1)} %bitcast.30, ...), custom_call_target="tpu_custom_call" | custom-call | tf_op jit(solution)/shard_map/update_tile/pallas_call | solution.py:502
  303.5 0.0 collective-permute-done.14.refs_1_
  303.5 1.3 copy-done.10
  304.8 13.6 %update_tile.4.refs_7_ = f32[2,16,128,2048]{3,2,1,0:T(8,128)} custom-call(s32[72]{0:T(128)} %concatenate.3.meta, f32[16,2,128,1024]{3,2,1,0:T(8,128)} %bitcast.24, f32[4,128,1024]{2,1,0:T(8,128)} %copy-done.10, bf16[2,16,128,512]{3,2,1,0:T(8,128)(2,1)} %bitcast.28, bf16[2,16,128,512]{3,2,1,0:T(8,128)(2,1)} %bitcast.31, ...), custom_call_target="tpu_custom_call", output_to_operand_aliasing={{}: (8, {})} | custom-call | tf_op jit(solution)/shard_map/update_tile/pallas_call | solution.py:502
  318.4 1.0 copy-done.11
  319.4 9.1 %update_tile.5 = f32[2,16,128,2048]{3,2,1,0:T(8,128)} custom-call(s32[72]{0:T(128)} %concatenate.3.meta, f32[16,2,128,1024]{3,2,1,0:T(8,128)} %bitcast.25, f32[2,128,1024]{2,1,0:T(8,128)} %copy-done.11, bf16[2,16,128,512]{3,2,1,0:T(8,128)(2,1)} %bitcast.29, bf16[2,16,128,512]{3,2,1,0:T(8,128)(2,1)} %bitcast.32, ...), custom_call_target="tpu_custom_call", output_to_operand_aliasing={{}: (8, {})} | custom-call | tf_op jit(solution)/shard_map/update_tile/pallas_call | solution.py:502
  (23 shorter events, 0.0 us)
Async XLA Ops:
  8.2 64.1 %collective-permute-start = (f32[512,1024]{1,0:T(8,128)}, f32[512,1024]{1,0:T(8,128)S(1)}, u32[]{:S(2)}, u32[]{:S(2)}) collective-permute-start(f32[512,1024]{1,0:T(8,128)} %bitcast.33), channel_id=1, source_target_pairs={{0,4},{4,0},{1,5},{5,1},{2,6},{6,2},{3,7},{7,3},{8,12},{12,8},{9,1... | collective-permute-start | bytes 6291464 | tf_op jit(solution)/shard_map/ppermute | solution.py:20
  8.7 16.4 %collective-permute-start.2 = (f32[10,128,128]{2,1,0:T(8,128)}, f32[10,128,128]{2,1,0:T(8,128)S(1)}, u32[]{:S(2)}, u32[]{:S(2)}) collective-permute-start(f32[10,128,128]{2,1,0:T(8,128)} %get-tuple-element.19), channel_id=1, source_target_pairs={{0,1},{1,0},{2,3},{3,2},{4,5},{5,4},{6,7},{7,6},{8,9},{9,8},{10,11... | collective-permute-start | bytes 1966088 | tf_op jit(solution)/shard_map/ppermute | solution.py:20
  26.3 30.3 %collective-permute-start.3 = (f32[10,128,128]{2,1,0:T(8,128)S(1)}, f32[10,128,128]{2,1,0:T(8,128)S(1)}, u32[]{:S(2)}, u32[]{:S(2)}) collective-permute-start(f32[10,128,128]{2,1,0:T(8,128)S(1)} %add.24), channel_id=1, source_target_pairs={{0,2},{1,3},{2,0},{3,1},{4,6},{5,7},{6,4},{7,5},{8,10},{9,11},{10,... | collective-permute-start | bytes 1966088 | tf_op jit(solution)/shard_map/ppermute | solution.py:20
  56.7 15.6 %collective-permute-start.4 = (f32[10,128,128]{2,1,0:T(8,128)S(1)}, f32[10,128,128]{2,1,0:T(8,128)S(1)}, u32[]{:S(2)}, u32[]{:S(2)}) collective-permute-start(f32[10,128,128]{2,1,0:T(8,128)S(1)} %add.25), channel_id=1, source_target_pairs={{0,4},{4,0},{1,5},{5,1},{2,6},{6,2},{3,7},{7,3},{8,12},{12,8},{9,1... | collective-permute-start | bytes 1966088 | tf_op jit(solution)/shard_map/ppermute | solution.py:20
  58.3 15.6 %copy-start.3 = (f32[4,128,1024]{2,1,0:T(8,128)S(1)}, f32[4,128,1024]{2,1,0:T(8,128)}, u32[]{:S(2)}) copy-start(f32[4,128,1024]{2,1,0:T(8,128)} %get-tuple-element.18) | copy-start | bytes 6291460
  72.3 121.4 %copy-start.2 = (f32[512,1024]{1,0:T(8,128)}, f32[512,1024]{1,0:T(8,128)S(1)}, u32[]{:S(2)}) copy-start(f32[512,1024]{1,0:T(8,128)S(1)} %collective-permute-done.refs_0_.other) | copy-start | bytes 6291460
  72.3 121.5 %collective-permute-start.12 = (f32[10,128,1024]{2,1,0:T(8,128)S(1)}, f32[10,128,1024]{2,1,0:T(8,128)S(1)}, u32[]{:S(2)}, u32[]{:S(2)}) collective-permute-start(f32[10,128,1024]{2,1,0:T(8,128)S(1)} %dynamic-slice_bitcast_fusion), channel_id=1, source_target_pairs={{0,4},{4,0},{1,5},{5,1},{2,6},{6,2},{3,7},{7,3},{8,12},{12,8},{9,1... | collective-permute-start | bytes 15728648 | tf_op jit(solution)/shard_map/ppermute | solution.py:20
  73.8 50.5 %collective-permute-start.5 = (f32[512,1024]{1,0:T(8,128)S(1)}, f32[512,1024]{1,0:T(8,128)S(1)}, u32[]{:S(2)}, u32[]{:S(2)}) collective-permute-start(f32[512,1024]{1,0:T(8,128)S(1)} %bitcast.36), channel_id=1, source_target_pairs={{0,2},{2,3},{7,5},{5,4},{8,10},{10,11},{15,13},{13,12},{16,18},{18... | collective-permute-start | bytes 6291464 | tf_op jit(solution)/shard_map/ppermute | solution.py:378
  75.1 50.5 %collective-permute-start.6 = (f32[512,1024]{1,0:T(8,128)S(1)}, f32[512,1024]{1,0:T(8,128)S(1)}, u32[]{:S(2)}, u32[]{:S(2)}) collective-permute-start(f32[512,1024]{1,0:T(8,128)S(1)} %bitcast.37), channel_id=1, source_target_pairs={{2,1},{5,6},{10,9},{13,14},{18,17},{21,22},{26,25},{29,30}} | collective-permute-start | bytes 6291464 | tf_op jit(solution)/shard_map/ppermute | solution.py:378
  75.9 110.7 %collective-permute-start.1 = (f32[512,1024]{1,0:T(8,128)S(1)}, f32[512,1024]{1,0:T(8,128)S(1)}, u32[]{:S(2)}, u32[]{:S(2)}) collective-permute-start(f32[512,1024]{1,0:T(8,128)S(1)} %collective-permute-done.refs_0_.other), channel_id=1, source_target_pairs={{0,2},{2,3},{7,5},{5,4},{8,10},{10,11},{15,13},{13,12},{16,18},{18... | collective-permute-start | bytes 6291464 | tf_op jit(solution)/shard_map/ppermute | solution.py:378
  77.2 111.9 %collective-permute-start.10 = (f32[512,1024]{1,0:T(8,128)S(1)}, f32[512,1024]{1,0:T(8,128)S(1)}, u32[]{:S(2)}, u32[]{:S(2)}) collective-permute-start(f32[512,1024]{1,0:T(8,128)S(1)} %bitcast.38), channel_id=1, source_target_pairs={{0,1},{2,0},{7,6},{5,7},{8,9},{10,8},{15,14},{13,15},{16,17},{18,1... | collective-permute-start | bytes 6291464 | tf_op jit(solution)/shard_map/ppermute | solution.py:378
  124.3 95.6 %copy-start.6 = (f32[512,1024]{1,0:T(8,128)}, f32[512,1024]{1,0:T(8,128)S(1)}, u32[]{:S(2)}) copy-start(f32[512,1024]{1,0:T(8,128)S(1)} %collective-permute-done.5.refs_1_) | copy-start | bytes 6291460
  124.3 97.9 %collective-permute-start.11 = (f32[512,1024]{1,0:T(8,128)S(1)}, f32[512,1024]{1,0:T(8,128)S(1)}, u32[]{:S(2)}, u32[]{:S(2)}) collective-permute-start(f32[512,1024]{1,0:T(8,128)S(1)} %collective-permute-done.5.refs_1_), channel_id=1, source_target_pairs={{2,3},{5,4},{10,11},{13,12},{18,19},{21,20},{26,27},{29,28}} | collective-permute-start | bytes 6291464 | tf_op jit(solution)/shard_map/ppermute | solution.py:378
  125.7 96.6 %copy-start.7 = (f32[512,1024]{1,0:T(8,128)}, f32[512,1024]{1,0:T(8,128)S(1)}, u32[]{:S(2)}) copy-start(f32[512,1024]{1,0:T(8,128)S(1)} %collective-permute-done.6.refs_3_) | copy-start | bytes 6291460
  125.7 123.4 %collective-permute-start.8 = (f32[512,1024]{1,0:T(8,128)S(1)}, f32[512,1024]{1,0:T(8,128)}, u32[]{:S(2)}, u32[]{:S(2)}) collective-permute-start(f32[512,1024]{1,0:T(8,128)S(1)} %collective-permute-done.refs_0_.other), channel_id=1, source_target_pairs={{2,1},{5,6},{10,9},{13,14},{18,17},{21,22},{26,25},{29,30}} | collective-permute-start | bytes 6291464 | tf_op jit(solution)/shard_map/ppermute | solution.py:378
  186.6 7.1 %copy-start = (f32[512,512]{1,0:T(8,128)}, f32[512,512]{1,0:T(8,128)S(1)}, u32[]{:S(2)}) copy-start(f32[512,512]{1,0:T(8,128)S(1)} %get-tuple-element.22.refs_5_.refs_7_.inverse) | copy-start | bytes 3145732
  186.6 7.1 %copy-start.1 = (f32[512,512]{1,0:T(8,128)}, f32[512,512]{1,0:T(8,128)S(1)}, u32[]{:S(2)}) copy-start(f32[512,512]{1,0:T(8,128)S(1)} %get-tuple-element.25.refs_6_) | copy-start | bytes 3145732
  186.7 7.1 %copy-start.5 = (f32[512,1024]{1,0:T(8,128)}, f32[512,1024]{1,0:T(8,128)S(1)}, u32[]{:S(2)}) copy-start(f32[512,1024]{1,0:T(8,128)S(1)} %collective-permute-done.1.refs_1_) | copy-start | bytes 6291460
  186.7 62.4 %collective-permute-start.7 = (f32[512,1024]{1,0:T(8,128)S(1)}, f32[512,1024]{1,0:T(8,128)}, u32[]{:S(2)}, u32[]{:S(2)}) collective-permute-start(f32[512,1024]{1,0:T(8,128)S(1)} %collective-permute-done.refs_0_.other), channel_id=1, source_target_pairs={{0,1},{2,0},{7,6},{5,7},{8,9},{10,8},{15,14},{13,15},{16,17},{18,1... | collective-permute-start | bytes 6291464 | tf_op jit(solution)/shard_map/ppermute | solution.py:378
  189.1 33.1 %copy-start.8 = (f32[512,1024]{1,0:T(8,128)}, f32[512,1024]{1,0:T(8,128)S(1)}, u32[]{:S(2)}) copy-start(f32[512,1024]{1,0:T(8,128)S(1)} %collective-permute-done.10.refs_2_) | copy-start | bytes 6291460
  189.1 68.0 %collective-permute-start.9 = (f32[512,1024]{1,0:T(8,128)S(1)}, f32[512,1024]{1,0:T(8,128)}, u32[]{:S(2)}, u32[]{:S(2)}) collective-permute-start(f32[512,1024]{1,0:T(8,128)S(1)} %collective-permute-done.1.refs_1_), channel_id=1, source_target_pairs={{2,3},{5,4},{10,11},{13,12},{18,19},{21,20},{26,27},{29,28}} | collective-permute-start | bytes 6291464 | tf_op jit(solution)/shard_map/ppermute | solution.py:378
  193.8 2.3 copy-start.4
  196.1 107.4 %collective-permute-start.14 = (f32[4,128,1024]{2,1,0:T(8,128)}, f32[4,128,1024]{2,1,0:T(8,128)S(1)}, u32[]{:S(2)}, u32[]{:S(2)}) collective-permute-start(f32[4,128,1024]{2,1,0:T(8,128)} %dynamic-slice_bitcast_fusion.1), channel_id=1, source_target_pairs={{0,4},{4,0},{1,5},{5,1},{2,6},{6,2},{3,7},{7,3},{8,12},{12,8},{9,1... | collective-permute-start | bytes 6291464 | tf_op jit(solution)/shard_map/ppermute | solution.py:20
  222.2 1.4 copy-start.9
  223.6 94.8 %collective-permute-start.13 = (f32[2,128,1024]{2,1,0:T(8,128)}, f32[2,128,1024]{2,1,0:T(8,128)S(1)}, u32[]{:S(2)}, u32[]{:S(2)}) collective-permute-start(f32[2,128,1024]{2,1,0:T(8,128)} %dynamic-slice_bitcast_fusion.2), channel_id=1, source_target_pairs={{0,4},{4,0},{1,5},{5,1},{2,6},{6,2},{3,7},{7,3},{8,12},{12,8},{9,1... | collective-permute-start | bytes 3145736 | tf_op jit(solution)/shard_map/ppermute | solution.py:20
  303.5 1.3 copy-start.10
  318.4 1.0 copy-start.11

commit v3 on v2

v3 whole, which is shorter than its diff:
```python
import functools

import jax
import jax.numpy as jnp
import numpy as np
from jax import lax
from jax.experimental import pallas as pl
from jax.experimental.pallas import tpu as pltpu
from jax.sharding import PartitionSpec as P

NF = 8192
BLK = 128
HALVES = 2
CHUNKS = (4, 4)
ROWS_AT_ONCE = 2
PACE = 1.0
LATE = 1.0

highest = lax.Precision.HIGHEST


def swapped(shard, axis, bit):
    return lax.ppermute(shard, axis, [(i, i ^ 1 << bit) for i in range(lax.axis_size(axis))])


def one_after(*arrays):
    first = [array[(0,) * array.ndim] for array in arrays]
    there = functools.reduce(jnp.logical_and, [value == value for value in first])
    return jnp.where(there, 1, 0)


def gated(value, *arrays):
    return value * one_after(*arrays).astype(value.dtype)


def spread_plan(rows, cols):
    sources = cols // rows
    where = -np.ones((sources, rows, cols), np.int32)
    for r in range(rows):
        for s in range(sources):
            where[s, r, r + s * rows] = 0
    steps = []
    while (where < 0).any():
        for buffer in range(len(steps) + 1):
            moves = []
            for r in range(rows):
                sign = 1 if r <= cols - 1 - (r + (sources - 1) * rows) else -1
                taken = set()
                for h in range(cols)[::-sign]:
                    for s in range(sources):
                        if where[s, r, h] != buffer:
                            continue
                        open_to = [
                            d for d in range(cols)
                            if where[s, r, d] < 0 and d not in taken and abs(d - h) <= rows
                        ]
                        if open_to:
                            d = max(open_to, key=lambda d: sign * (d - h))
                            taken.add(d)
                            moves.append((s, r, h, d))
            if moves:
                break
        steps.append((buffer, [(r * cols + h, r * cols + d) for _, r, h, d in moves]))
        for s, r, _, d in moves:
            where[s, r, d] = len(steps)
    return steps, where


def fold_plan(where):
    sources, rows, cols = where.shape
    steps = where.max()
    order = -np.ones((steps + 1, rows, cols), np.int32)
    folded = np.zeros_like(where)
    for r in range(rows):
        for d in range(cols):
            got = sorted((where[s, r, d], s) for s in range(sources) if where[s, r, d] > 0)
            for n, (step, s) in enumerate(got):
                order[step, r, d] = n
                folded[s, r, d] = n + 1
    return order, folded


class Meta:
    def __init__(self, child_blocks, pivot_count, sources):
        self.child_blocks, self.pivot_count, self.sources = child_blocks, pivot_count, sources

    def pack(self, child_map, pivots, row_index, col_index, where, turns):
        place = jnp.stack([row_index, col_index]).astype(jnp.int32)
        held = jnp.asarray(np.concatenate([where, turns]))[:, row_index, col_index]
        return jnp.concatenate([child_map.reshape(-1), pivots, place, held])

    def has(self, meta, child, block, front_block):
        return meta[child * self.child_blocks + block] == front_block

    def pivot(self, meta, p):
        return meta[2 * self.child_blocks + p]

    def row(self, meta):
        return meta[2 * self.child_blocks + self.pivot_count]

    def col(self, meta):
        return meta[2 * self.child_blocks + self.pivot_count + 1]

    def held(self, meta, s):
        return meta[2 * self.child_blocks + self.pivot_count + 2 + s]

    def source(self, meta, turn):
        return self.held(meta, self.sources + turn)

    def is_pivot(self, meta, front_block):
        hit = front_block == self.pivot(meta, 0)
        for p in range(1, self.pivot_count):
            hit = jnp.logical_or(hit, front_block == self.pivot(meta, p))
        return hit


def as_float(flag):
    return jnp.where(flag, 1.0, 0.0).astype(jnp.float32)


def eye_mask():
    return lax.broadcasted_iota(jnp.int32, (BLK, BLK), 0) == lax.broadcasted_iota(jnp.int32, (BLK, BLK), 1)


def split(value):
    high = value.astype(jnp.bfloat16)
    return high, (value - high.astype(jnp.float32)).astype(jnp.bfloat16)


def dot_t(a, b):
    return lax.dot_general(
        a, b, (((1,), (1,)), ((), ())), precision=highest, preferred_element_type=jnp.float32
    )


def dot(a, b):
    return jnp.dot(a, b, precision=highest, preferred_element_type=jnp.float32)


def pick_kernel(info, rows, cols, meta, child, diag, panel, pivot_part):
    half = rows // 2
    r, q = info.row(meta), info.col(meta)
    mine, within = r // half, r % half
    p = pl.program_id(0)
    front_block = info.pivot(meta, p)
    block = front_block % info.child_blocks
    present = jnp.logical_and(info.has(meta, mine, block, front_block), block % half == within)
    panel[0] = child[0] * as_float(present)
    first = p * (p + 1) // 2
    for t in range(info.pivot_count):
        other = info.pivot(meta, t)
        other_block = other % info.child_blocks
        here = jnp.logical_and(info.has(meta, mine, other_block, other), other_block % cols == q)

        @pl.when(t <= p)
        def _():
            at = pl.multiple_of(other_block // cols * BLK, BLK)
            pivot_part[first + t] = panel[0, :, pl.ds(at, BLK)] * as_float(here)

    on_diagonal = jnp.logical_and(front_block % rows == r, front_block % cols == q)

    @pl.when(on_diagonal)
    def _():
        pivot_part[first + p] += jnp.where(eye_mask(), diag[0], 0.0)


def cholesky_kernel(count, blocks, lower, inverse, inverse_t, work, rest):
    at = lambda i, j: i * (i + 1) // 2 + j
    span = lambda i: slice(i * BLK, (i + 1) * BLK)
    lower[...] = jnp.zeros_like(lower)
    inverse[...] = jnp.zeros_like(inverse)
    rest[...] = blocks[...]
    row_ids = lax.broadcasted_iota(jnp.int32, (BLK, BLK), 0)
    col_ids = lax.broadcasted_iota(jnp.int32, (BLK, BLK), 1)
    wide_ids = lax.broadcasted_iota(jnp.int32, (1, 2 * BLK), 1)
    column_ids = lax.broadcasted_iota(jnp.int32, (BLK, 1), 0)
    for p in range(count):
        work[:, :BLK] = rest[at(p, p)]
        work[:, BLK:] = jnp.where(row_ids == col_ids, 1.0, 0.0)

        def eliminate(j, carry):
            row = work[pl.ds(j, 1), :]
            lead = jnp.sum(jnp.where(wide_ids == j, row, 0.0), axis=1, keepdims=True)
            left = work[:, :BLK]
            column = jnp.sum(jnp.where(col_ids == j, left, 0.0), axis=1, keepdims=True)
            column = jnp.where(column_ids > j, column, 0.0)
            scaled = row / lead
            work[...] = work[...] - column * scaled
            return carry

        lax.fori_loop(0, BLK, eliminate, 0)
        left = work[:, :BLK]
        lead = jnp.sum(jnp.where(row_ids == col_ids, left, 0.0), axis=1, keepdims=True)
        scale = 1.0 / jnp.sqrt(lead)
        lower[span(p), span(p)] = jnp.where(row_ids <= col_ids, left * scale, 0.0).T
        inverse[span(p), span(p)] = work[:, BLK:] * scale
        own_inverse = inverse[span(p), span(p)]
        for i in range(p + 1, count):
            lower[span(i), span(p)] = dot_t(rest[at(i, p)], own_inverse)
        for i in range(p + 1, count):
            for k in range(p + 1, i + 1):
                rest[at(i, k)] -= dot_t(lower[span(i), span(p)], lower[span(k), span(p)])
    for i in range(1, count):
        for j in range(i):
            known = slice(j * BLK, i * BLK)
            partial = dot(lower[span(i), known], inverse[known, span(j)])
            inverse[span(i), span(j)] = -dot(inverse[span(i), span(i)], partial)
    inverse_t[...] = inverse[...].T


def columns_kernel(info, rows, cols, child_slots, width, meta, own, other, inverse, *refs):
    stacked = refs[-1]
    r, q = info.row(meta), info.col(meta)
    mine = r // (rows // 2)
    v, step = pl.program_id(0), pl.program_id(1)
    parts = []
    for i in range(width):
        block = (step * width + i) * cols + q
        front_block = block + v * info.child_blocks
        keep = jnp.logical_not(info.is_pivot(meta, front_block))
        lanes = slice(i * BLK, (i + 1) * BLK)
        take = as_float(jnp.logical_and(keep, info.has(meta, mine, block, front_block)))
        take_other = as_float(jnp.logical_and(keep, info.has(meta, 1 - mine, block, front_block)))
        parts.append(own[:, lanes] * take + other[:, lanes] * take_other)
    high, low = split(dot(inverse[...], jnp.concatenate(parts, axis=1)))
    depth = high.shape[0]
    stacked[:depth], stacked[depth : 2 * depth], stacked[2 * depth :] = high, high, low


def chosen(holder, used, pieces):
    value = pieces[0][...]
    for n, piece in zip(used[1:], pieces[1:]):
        value = jnp.where(holder == n, piece[...], value)
    return value


def rows_kernel(info, rows, cols, width, share, turn, first, used, meta, *refs):
    r, q = info.row(meta), info.col(meta)
    mine = r // (rows // 2)
    s, step = info.source(meta, turn), pl.program_id(0) + first
    lower, inverse_t = refs[len(used) :][:2]
    factor, parts, work = refs[-3:]
    piece = chosen(info.held(meta, s), used, refs[: len(used)])
    half_depth = piece.shape[0] // 2
    own_value = dot(piece[:half_depth].T, inverse_t[...])
    other_value = dot(piece[half_depth:].T, inverse_t[...])
    at = pl.multiple_of(q * share // BLK * BLK, BLK)
    depth = lower.shape[0]
    for i in range(width):
        block = (step * width + i) * cols + r + s * rows
        span = slice(i * BLK, (i + 1) * BLK)
        for v in range(2):
            front_block = block + v * info.child_blocks
            take = as_float(info.has(meta, mine, block, front_block))
            take_other = as_float(info.has(meta, 1 - mine, block, front_block))
            value = own_value[span, :] * take + other_value[span, :] * take_other
            high, low = split(value)
            parts[v, i, :, :depth], parts[v, i, :, depth : 2 * depth], parts[v, i, :, 2 * depth :] = high, low, high
            work[...] = value
            factor[v, i, 0] = work[:, pl.ds(at, BLK)]
            for p in range(info.pivot_count):

                @pl.when(front_block == info.pivot(meta, p))
                def _():
                    factor[v, i, 0] = lower[p * BLK : (p + 1) * BLK, pl.ds(at, BLK)]
                    parts[v, i] = jnp.zeros_like(parts[v, i])


def update_kernel(info, rows, cols, child_slots, width, turn, first, meta, *refs):
    own, other, left, right, diag = refs[:5]
    tile, token = refs[-2:]
    token[...] = jnp.zeros_like(token)
    r, q = info.row(meta), info.col(meta)
    mine = r // (rows // 2)
    step, v = pl.program_id(0), pl.program_id(1)
    left_rows = left[...].reshape(2 * ROWS_AT_ONCE * BLK, left.shape[-1])

    def takes(block, front_block):
        keep = jnp.logical_not(info.is_pivot(meta, front_block))
        return [as_float(jnp.logical_and(keep, info.has(meta, c, block, front_block))) for c in (mine, 1 - mine)]

    def row_block(j):
        return (first + step * ROWS_AT_ONCE + j) * cols + info.source(meta, turn) * rows + r

    row_takes = {
        (u, j): takes(row_block(j), row_block(j) + u * info.child_blocks)
        for u in range(2)
        for j in range(ROWS_AT_ONCE)
    }
    for start in range(0, child_slots, width):
        at = pl.multiple_of((v * child_slots + start) * BLK, BLK)
        change = jnp.dot(left_rows, right[:, pl.ds(at, width * BLK)], preferred_element_type=jnp.float32)
        for i in range(width):
            block = (start + i) * cols + q
            col_takes = takes(block, block + v * info.child_blocks)
            lanes = slice((start + i) * BLK, (start + i + 1) * BLK)
            for (u, j), row_take in row_takes.items():
                n = u * ROWS_AT_ONCE + j
                tile[u, j, 0, :, lanes] = (
                    own[j, 0, 0, :, lanes] * (row_take[0] * col_takes[0])
                    + other[j, :, lanes] * (row_take[1] * col_takes[1])
                    - change[n * BLK : (n + 1) * BLK, i * BLK : (i + 1) * BLK]
                )
    for u in range(2):
        for j in range(ROWS_AT_ONCE):
            front_block = row_block(j) + u * info.child_blocks
            slot = front_block // cols
            here = jnp.logical_and(front_block % cols == q, slot // child_slots == v)

            @pl.when(jnp.logical_and(here, jnp.logical_not(info.is_pivot(meta, front_block))))
            def _():
                at = pl.multiple_of(slot % child_slots * BLK, BLK)
                tile[u, j, 0, :, pl.ds(at, BLK)] += jnp.where(eye_mask(), diag[u, j, 0], 0.0)


def params(grid_size, mib=32):
    return pltpu.CompilerParams(
        dimension_semantics=("arbitrary",) * grid_size, vmem_limit_bytes=mib * 1024 * 1024
    )


def about(micros):
    micros *= PACE
    return pl.CostEstimate(flops=int(micros * 1.15e9), bytes_accessed=int(micros * 3.69e6), transcendentals=0)


def per_device(contrib, front_diag, child_map, pivots):
    rows, cols = lax.axis_size("row"), lax.axis_size("col")
    r, q = lax.axis_index("row"), lax.axis_index("col")
    half = rows // 2
    half_bit = half.bit_length() - 1
    sources = cols // rows
    local_rows, child_width = front_diag.shape[0], contrib.shape[1]
    row_slots = local_rows // BLK
    tile_cols = NF // cols
    child_slots = child_width // BLK
    child_rows = contrib.shape[0] // BLK
    row_half = child_rows // 2
    child_blocks, pivot_count = child_map.shape[1], pivots.shape[0]
    depth = pivot_count * BLK
    width = min(4, child_slots)
    steps, where = spread_plan(rows, cols)
    turns = np.argsort(where, axis=0, kind="stable").astype(np.int32)
    early = set(np.take_along_axis(where, turns[:1], 0).ravel()) - {0}
    order = None
    if len(steps) > 2 * sources:
        order, where = fold_plan(where)
    held_count = int(where.max()) + 1
    info = Meta(child_blocks, pivot_count, sources)
    meta = info.pack(child_map, pivots, r, q, where, turns)
    f32, bf16 = jnp.float32, jnp.bfloat16
    shape = jax.ShapeDtypeStruct

    lower_count = pivot_count * (pivot_count + 1) // 2
    panel, pivot_part = pl.pallas_call(
        functools.partial(pick_kernel, info, rows, cols),
        grid_spec=pltpu.PrefetchScalarGridSpec(
            num_scalar_prefetch=1,
            grid=(pivot_count,),
            in_specs=[
                pl.BlockSpec(
                    (1, BLK, child_width), lambda p, m: (info.pivot(m, p) % child_blocks // half, 0, 0)
                ),
                pl.BlockSpec((1, 1, BLK), lambda p, m: (info.pivot(m, p) // rows, 0, 0)),
            ],
            out_specs=[
                pl.BlockSpec((1, BLK, child_width), lambda p, m: (p, 0, 0)),
                pl.BlockSpec((lower_count, BLK, BLK), lambda p, m: (0, 0, 0)),
            ],
        ),
        out_shape=[
            shape((pivot_count, BLK, child_width), f32),
            shape((lower_count, BLK, BLK), f32),
        ],
        compiler_params=params(1),
        name="pick",
        cost_estimate=about(5),
    )(meta, contrib.reshape(child_rows, BLK, child_width), front_diag.reshape(row_slots, 1, BLK))
    own = panel.reshape(depth, child_width)
    for bit in range(half_bit):
        own = own + swapped(own, "row", bit)
    other = swapped(own, "row", half_bit)

    def folded(held):
        if order is None:
            return held
        mine_order = jnp.asarray(order)[:, r, q]
        merged = [held[0]]
        for n in range(held_count - 1):
            merged.append(sum(jnp.where(mine_order[k] == n, held[k], 0.0) for k in range(1, len(held))))
        return merged

    pivot_blocks = pivot_part
    for bit in range(cols.bit_length() - 1):
        across = swapped(pivot_blocks, "col", bit)
        pivot_blocks = pivot_blocks + across
    pivot_blocks = gated(pivot_blocks, other)
    for bit in range(half_bit, -1, -1):
        pivot_blocks = pivot_blocks + swapped(pivot_blocks, "row", bit)

    both = jnp.concatenate([own, other]) * one_after(across).astype(f32)
    halves = HALVES if child_slots // ROWS_AT_ONCE % HALVES == 0 and order is None else 1
    held = [[both]]
    for n, (buffer, pairs) in enumerate(steps):
        sent = held[buffer][0]
        if n + 1 not in early:
            sent = jnp.split(sent, halves, axis=1)
        else:
            sent = [sent]
        held.append([lax.ppermute(part, ("row", "col"), pairs) for part in sent])
    meanwhile = [part for n in early for part in held[n]]
    if order is not None:
        held = [[part] for part in folded([parts[0] for parts in held])]

    lower, inverse, inverse_t = pl.pallas_call(
        functools.partial(cholesky_kernel, pivot_count),
        out_shape=[shape((depth, depth), f32)] * 3,
        scratch_shapes=[pltpu.VMEM((BLK, 2 * BLK), f32), pltpu.VMEM((lower_count, BLK, BLK), f32)],
        compiler_params=params(0),
        name="factor_pivots",
        cost_estimate=about(59),
    )(pivot_blocks)

    own_view = contrib.reshape(child_slots, sources, 2, BLK, child_width)
    mine = r // half
    partner_turns = jnp.asarray(turns)[:, r ^ half, q]
    received = []
    for turn in range(sources):
        chunks = (child_slots,)
        if turn > 0 and sum(CHUNKS) == child_slots:
            chunks = CHUNKS
        first = 0
        for chunk in chunks:
            if not received:
                start = one_after(pivot_blocks)
            elif len(received) == 1:
                start = one_after(inverse)
            else:
                start = one_after(*[part for _, _, part in received[:-1]])
            part = lax.dynamic_slice(
                own_view,
                (first, partner_turns[turn] * start, 1 - mine, 0, 0),
                (chunk, 1, 1, BLK, child_width),
            ).reshape(chunk, BLK, child_width)
            received.append((turn, first, swapped(part, "row", half_bit)))
            first += chunk
    meanwhile.append(received[0][2])

    lanes = width * BLK
    groups = child_slots // width
    whole = lambda *_: (0, 0)
    untouched = pl.BlockSpec(memory_space=pl.ANY)
    col_parts = pl.pallas_call(
        functools.partial(columns_kernel, info, rows, cols, child_slots, width),
        grid_spec=pltpu.PrefetchScalarGridSpec(
            num_scalar_prefetch=1,
            grid=(2, groups),
            in_specs=[
                pl.BlockSpec((depth, lanes), lambda v, g, m: (0, g)),
                pl.BlockSpec((depth, lanes), lambda v, g, m: (0, g)),
                pl.BlockSpec((depth, depth), whole),
            ]
            + [untouched] * len(meanwhile),
            out_specs=pl.BlockSpec((3 * depth, lanes), lambda v, g, m: (0, v * groups + g)),
        ),
        out_shape=shape((3 * depth, tile_cols), bf16),
        compiler_params=params(2),
        name="factor_at_columns",
        cost_estimate=about(10),
    )(meta, own, other, inverse, *meanwhile)

    share = depth // cols
    factor = None
    tile = token = None
    diag_view = front_diag.reshape(2, child_slots, sources, 1, BLK)
    mine_of = lambda m: info.row(m) // half
    square = pl.BlockSpec((depth, depth), whole)
    few = min(2, width)
    counts = [1] + [halves] * (sources - 1)
    row_parts = [[] for _ in counts]

    order_of_work = [("rows", 0, 0), ("rows", 1, 0), ("tile", 0)]
    order_of_work += [("rows", turn, n) for turn in range(1, sources) for n in range(counts[turn]) if (turn, n) != (1, 0)]
    order_of_work += [("tile", turn) for turn in range(1, sources)]
    for work, turn, *rest in order_of_work:
        parts_count = counts[turn]
        if work == "rows":
            (at_half,) = rest
            used = sorted({int(n) for n in np.take_along_axis(where, turns[turn : turn + 1], 0).ravel()})
            steps_here = child_slots // few // parts_count
            first = at_half * steps_here

            def piece(n, turn=turn, first=first, at_half=at_half):
                base = first if len(held[n]) == 1 else 0
                return held[n][-1 if base else min(at_half, len(held[n]) - 1)], pl.BlockSpec(
                    (2 * depth, few * BLK),
                    lambda g, m: (0, jnp.where(info.held(m, info.source(m, turn)) == n, base + g, 0)),
                )

            operands = [piece(n)[0] for n in used] + [lower, inverse_t]
            in_specs = [piece(n)[1] for n in used] + [square, square]
            if factor is None:
                factor, aliases = jnp.zeros((2, 1, sources, BLK, BLK), f32), {}
            else:
                aliases = {len(operands) + 1: 0}
            operands += [factor, meta if token is None else token]
            in_specs += [untouched] * 2
            factor, row_part = pl.pallas_call(
                functools.partial(rows_kernel, info, rows, cols, few, share, turn, first, used),
                grid_spec=pltpu.PrefetchScalarGridSpec(
                    num_scalar_prefetch=1,
                    grid=(steps_here,),
                    in_specs=in_specs,
                    out_specs=[
                        pl.BlockSpec(
                            (2, few, 1, BLK, BLK),
                            lambda g, m, turn=turn, first=first: (0, first + g, info.source(m, turn), 0, 0),
                        ),
                        pl.BlockSpec((2, few, BLK, 3 * depth), lambda g, m: (0, g, 0, 0)),
                    ],
                    scratch_shapes=[pltpu.VMEM((BLK, depth), f32)],
                ),
                out_shape=[
                    shape((2, child_slots, sources, BLK, BLK), f32),
                    shape((2, child_slots // parts_count, BLK, 3 * depth), bf16),
                ],
                input_output_aliases=aliases,
                compiler_params=params(1, 40),
                name="factor_rows",
                cost_estimate=about(3.0 * steps_here * (LATE if turn else 1.0)),
            )(meta, *operands)
            row_parts[turn].append(row_part)
            continue

        for first, part in [(first, part) for at_turn, first, part in received if at_turn == turn]:
            at = first // ROWS_AT_ONCE
            row_part = row_parts[turn][first * parts_count // child_slots]
            left_at = at % (child_slots // parts_count // ROWS_AT_ONCE)
            source_of = functools.partial(info.source, turn=turn)
            in_specs = [
                pl.BlockSpec(
                    (ROWS_AT_ONCE, 1, 1, BLK, child_width),
                    lambda t, v, m, at=at, source_of=source_of: (at + t, source_of(m), mine_of(m), 0, 0),
                ),
                pl.BlockSpec((ROWS_AT_ONCE, BLK, child_width), lambda t, v, m: (t, 0, 0)),
                pl.BlockSpec((2, ROWS_AT_ONCE, BLK, 3 * depth), lambda t, v, m, at=left_at: (0, at + t, 0, 0)),
                pl.BlockSpec((3 * depth, tile_cols), whole),
                pl.BlockSpec(
                    (2, ROWS_AT_ONCE, 1, 1, BLK),
                    lambda t, v, m, at=at, source_of=source_of: (0, at + t, source_of(m), 0, 0),
                ),
            ]
            operands = [own_view, part, row_part, col_parts, diag_view]
            aliases = {}
            if tile is None:
                in_specs.append(untouched)
                operands.append(row_parts[1][0])
            else:
                in_specs.append(untouched)
                operands.append(tile)
                aliases = {len(operands): 0}
            tile, token = pl.pallas_call(
                functools.partial(update_kernel, info, rows, cols, child_slots, width, turn, first),
                grid_spec=pltpu.PrefetchScalarGridSpec(
                    num_scalar_prefetch=1,
                    grid=(part.shape[0] // ROWS_AT_ONCE, 2),
                    in_specs=in_specs,
                    out_specs=[
                        pl.BlockSpec(
                            (2, ROWS_AT_ONCE, 1, BLK, child_width),
                            lambda t, v, m, at=at, source_of=source_of: (0, at + t, source_of(m), 0, v),
                        ),
                        pl.BlockSpec((8, BLK), lambda t, v, m: (0, 0)),
                    ],
                ),
                out_shape=[shape((2, child_slots, sources, BLK, tile_cols), f32), shape((8, BLK), f32)],
                input_output_aliases=aliases,
                compiler_params=params(2, 36),
                name="update_tile",
                cost_estimate=about(3.0 * part.shape[0] * (LATE if turn else 1.0)),
            )(meta, *operands)
    factor = factor.reshape(local_rows, BLK)
    if share < BLK:
        factor = lax.dynamic_slice_in_dim(factor, q * share % BLK, share, 1)

    return factor, tile.reshape(local_rows, tile_cols)


def solution(mesh):
    placed = (P(("front", "row"), "col"), P(("front", "row")), P("front", None), P("front"))
    return jax.shard_map(
        per_device,
        mesh=mesh,
        in_specs=placed,
        out_specs=(P(("front", "row"), "col"), P(("front", "row"), "col")),
        check_vma=False,
    )
```

time: 335 us -> 303 us (0.904)
  waiting for transfers between devices: 107 us -> 65.8 us
  local copies, waits for them, and re-layouts: 17.7 us -> 37.8 us
  Pallas kernels: 158 us -> 147 us
  starting transfers between devices: 43.1 us -> 33 us
  between operations: 0.83 us -> 9.22 us
  other arithmetic: 1.33 us -> 5.7 us
    ppermute x8 -> x6, waiting for transfers between devices: 54.3 us -> 22.9 us  [per_device(): held.append([lax.ppermute(part, ('row', 'col'), pairs) for part in sent])]
    ppermute x7, waiting for transfers between devices: 53.1 us -> 43 us  [swapped(): lax.ppermute(shard, axis, [(i, i ^ 1 << bit) for i in range(lax.axis_size...]
    ppermute x7, starting transfers between devices: 31.6 us -> 22.2 us  [swapped(): lax.ppermute(shard, axis, [(i, i ^ 1 << bit) for i in range(lax.axis_size...]
    split x0 -> x2, local copies, waits for them, and re-layouts: none -> 9.23 us  [per_device(): sent = jnp.split(sent, halves, axis=1)]
    unnamed x24 -> x44, local copies, waits for them, and re-layouts: 6.07 us -> 12.6 us
    mul x0 -> x2, other arithmetic: none -> 4.42 us  [the longest x1 4.35 us: per_device(): both = jnp.concatenate([own, other]) * one_after(across).astype(f32)]
    pallas_call x3, Pallas kernels: 49.8 us -> 45.8 us  [per_device(): pl.pallas_call(functools.partial(update_kernel, info, rows, cols, child_s...]
    slice x0 -> x6, local copies, waits for them, and re-layouts: none -> 3.9 us  [the longest x5 3.24 us: one_after(): first = [array[(0,) * array.ndim] for array in arrays]]
  transfers between devices with their start and end apart: 15 -> 13, of which waited for: 5 -> 6; matrix products, arithmetic and copies ran while one was open for 3% -> 10% of each run, Pallas kernels for 44% -> 45%
where the time goes in v3:
time: 303 us; the launch traced here: 299 us
  Pallas kernels  147 us (49%)
  waiting for transfers between devices  65.8 us (22%)
  local copies, waits for them, and re-layouts  37.8 us (12%)
  starting transfers between devices  33 us (11%)
  between operations  9.22 us (3%)
  other arithmetic  5.7 us (2%)
    pallas_call x1, Pallas kernels, per_device(): pl.pallas_call(functools.partial(cholesky_kernel, pivot_count), out_shape...  58.9 us
    pallas_call x3, Pallas kernels, per_device(): pl.pallas_call(functools.partial(update_kernel, info, rows, cols, child_s...  45.8 us
    ppermute x7, waiting for transfers between devices, swapped(): lax.ppermute(shard, axis, [(i, i ^ 1 << bit) for i in range(lax.axis_size...  43 us
    pallas_call x3, Pallas kernels, per_device(): pl.pallas_call(functools.partial(rows_kernel, info, rows, cols, few, shar...  31.3 us
    ppermute x6, waiting for transfers between devices, per_device(): held.append([lax.ppermute(part, ('row', 'col'), pairs) for part in sent])  22.9 us
    ppermute x7, starting transfers between devices, swapped(): lax.ppermute(shard, axis, [(i, i ^ 1 << bit) for i in range(lax.axis_size...  22.2 us
    unnamed x44, local copies, waits for them, and re-layouts  12.6 us
    ppermute x6, starting transfers between devices, per_device(): held.append([lax.ppermute(part, ('row', 'col'), pairs) for part in sent])  10.9 us
  transfers between devices with their start and end apart: 13, of which 6 were waited for; matrix products, arithmetic and copies ran while one was open for 10% of the time, Pallas kernels for 45%

profile of v3, /device:TPU:6, one launch (start us, length us, event | category | flops | bytes accessed | tf_op | source)
XLA Modules:
  0.0 298.9 jit_solution(17523743948306651131)
XLA Ops:
  0.6 0.8 reshape.64
  1.4 0.7 fusion
  2.1 0.7 concatenate.6.meta.refs_6_
  2.8 5.8 %copy-done = f32[4096,1024]{1,0:T(8,128)S(1)} copy-done((f32[4096,1024]{1,0:T(8,128)S(1)}, f32[4096,1024]{1,0:T(8,128)}, u32[]{:S(2)}) %copy-start) | copy-done | bytes 16777240
  8.6 0.7 copy-done.5
  9.3 1.2 pick.1
  10.5 0.6 collective-permute-start
  11.1 1.6 collective-permute-start.1
  12.6 14.6 %collective-permute-done.1 = f32[10,128,128]{2,1,0:T(8,128)S(1)} collective-permute-done((f32[10,128,128]{2,1,0:T(8,128)S(1)}, f32[10,128,128]{2,1,0:T(8,128)S(1)}, u32[]{:S(2)}, u32[]{:S(2)}) %collective-permute-start.1) | collective-permute-done | bytes 655392 | tf_op jit(solution)/shard_map/ppermute | solution.py:23
  27.3 2.7 collective-permute-start.2
  30.0 27.9 %collective-permute-done.other = f32[512,1024]{1,0:T(8,128)S(1)} collective-permute-done((f32[512,1024]{1,0:T(8,128)S(1)}, f32[512,1024]{1,0:T(8,128)S(1)}, u32[]{:S(2)}, u32[]{:S(2)}) %collective-permute-start) | collective-permute-done | bytes 2097184 | tf_op jit(solution)/shard_map/ppermute | solution.py:23
  57.9 1.4 copy-done.3
  61.2 0.6 collective-permute-start.6
  61.8 0.7 fusion.3
  62.4 0.5 slice.31
  64.2 4.3 %maximum_multiply_fusion.refs_0_ = f32[1024,1024]{1,0:T(8,128)} fusion(f32[512,1024]{1,0:T(8,128)} %copy-done.3, f32[512,1024]{1,0:T(8,128)S(1)} %bitcast.32, f32[]{:T(128)} %bitcast.6), kind=kLoop, calls=%fused_computation | loop fusion | flops 2097152 | bytes 8388612 | tf_op jit(solution)/shard_map/mul | solution.py:401
  68.6 2.7 collective-permute-start.9
  71.3 1.3 collective-permute-start.3
  72.6 4.6 %fusion.2 = (f32[1024,512]{1,0:T(8,128)}, f32[1024,512]{1,0:T(8,128)}) fusion(f32[1024,1024]{1,0:T(8,128)} %maximum_multiply_fusion.refs_0_), kind=kLoop, calls=%fused_computation.9 | loop fusion | bytes 8388608 | tf_op jit(solution)/shard_map/split | solution.py:407
  77.2 2.1 collective-permute-start.7
  79.3 2.0 collective-permute-start.4
  81.3 1.2 add.39.blocks
  82.5 0.5 slice.33
  85.0 4.9 %dynamic-slice_bitcast_fusion = f32[8,128,1024]{2,1,0:T(8,128)} fusion(f32[8,2,2,128,1024]{4,3,2,1,0:T(8,128)} %bitcast.23, s32[]{:T(128)S(6)} %select_n.58, s32[]{:T(128)S(6)} %select_n.59), kind=kLoop, calls=%fused_computation.1 | loop fusion | bytes 8388616 | tf_op jit(solution)/shard_map/reshape | solution.py:444
  89.8 8.2 %collective-permute-start.10 = (f32[8,128,1024]{2,1,0:T(8,128)}, f32[8,128,1024]{2,1,0:T(8,128)}, u32[]{:S(2)}, u32[]{:S(2)}) collective-permute-start(f32[8,128,1024]{2,1,0:T(8,128)} %dynamic-slice_bitcast_fusion), channel_id=1, source_target_pairs={{0,4},{4,0},{1,5},{5,1},{2,6},{6,2},{3,7},{7,3},{8,12},{12,8},{9,1... | collective-permute-start | bytes 12582920 | tf_op jit(solution)/shard_map/ppermute | solution.py:23
  98.1 58.9 %factor_pivots.1 = (f32[512,512]{1,0:T(8,128)S(1)}, f32[512,512]{1,0:T(8,128)S(1)}, f32[512,512]{1,0:T(8,128)S(1)}) custom-call(f32[10,128,128]{2,1,0:T(8,128)S(1)} %add.39.blocks), custom_call_target="tpu_custom_call" | custom-call | flops 67849998336 | bytes 217710000 | tf_op jit(solution)/shard_map/factor_pivots/pallas_call | solution.py:415
  157.0 1.0 copy-done.9
  158.0 1.0 copy-done.13
  158.9 0.5 slice.30
  159.5 1.0 copy-done.7
  162.4 4.6 %collective-permute-done.3.refs_1_.refs_0_ = f32[1024,1024]{1,0:T(8,128)} collective-permute-done((f32[1024,1024]{1,0:T(8,128)}, f32[1024,1024]{1,0:T(8,128)}, u32[]{:S(2)}, u32[]{:S(2)}) %collective-permute-start.3) | collective-permute-done | bytes 4194336 | tf_op jit(solution)/shard_map/ppermute | solution.py:410
  167.1 4.6 %fusion.1 = (f32[1024,512]{1,0:T(8,128)}, f32[1024,512]{1,0:T(8,128)}) fusion(f32[1024,1024]{1,0:T(8,128)} %collective-permute-done.3.refs_1_.refs_0_), kind=kLoop, calls=%fused_computation.8 | loop fusion | bytes 8388608 | tf_op jit(solution)/shard_map/split | solution.py:407
  171.7 1.3 collective-permute-start.8
  173.0 1.5 collective-permute-start.5
  174.5 14.0 %factor_rows.3 = (f32[2,8,2,128,128]{4,3,2,1,0:T(8,128)}, bf16[2,8,128,1536]{3,2,1,0:T(8,128)(2,1)}) custom-call(s32[74]{0:T(128)S(1)} %concatenate.6.meta.refs_6_, f32[1024,1024]{1,0:T(8,128)} %maximum_multiply_fusion.refs_0_, f32[1024,1024]{1,0:T(8,128)} %collective-permute-done.3.refs_1_.refs_0_, f32[1024,1024]{1,0:T(8,128)} %collective-permute-done.9.refs_2_.refs_1_, ...), custom_call_target="tpu_custom_call" | custom-call | flops 13799999488 | bytes 44280000 | tf_op jit(solution)/shard_map/factor_rows/pallas_call | solution.py:508
  188.5 1.2 slice.34
  191.5 5.1 %dynamic-slice_bitcast_fusion.1 = (f32[4,128,1024]{2,1,0:T(8,128)}, f32[4,128,1024]{2,1,0:T(8,128)}) fusion(f32[8,2,2,128,1024]{4,3,2,1,0:T(8,128)} %bitcast.24, s32[]{:T(128)S(6)} %select_n.65, s32[]{:T(128)S(6)} %select_n.59, s32[]{:T(128)S(6)} %select_n.62), kind=kLoop, calls=%fused_computation.2 | loop fusion | bytes 8388620 | tf_op jit(solution)/shard_map/reshape | solution.py:444
  196.6 4.6 %collective-permute-start.12 = (f32[4,128,1024]{2,1,0:T(8,128)}, f32[4,128,1024]{2,1,0:T(8,128)}, u32[]{:S(2)}, u32[]{:S(2)}) collective-permute-start(f32[4,128,1024]{2,1,0:T(8,128)} %get-tuple-element.32), channel_id=1, source_target_pairs={{0,4},{4,0},{1,5},{5,1},{2,6},{6,2},{3,7},{7,3},{8,12},{12,8},{9,1... | collective-permute-start | bytes 6291464 | tf_op jit(solution)/shard_map/ppermute | solution.py:23
  201.2 10.1 %factor_at_columns.1.refs_3_ = bf16[1536,2048]{1,0:T(8,128)(2,1)} custom-call(s32[74]{0:T(128)S(1)} %concatenate.6.meta.refs_6_, f32[512,1024]{1,0:T(8,128)S(1)} %bitcast.33, f32[512,1024]{1,0:T(8,128)S(1)} %copy-done.4, f32[512,512]{1,0:T(8,128)S(1)} %copy-done.8, f32[1024,1024]{1,0:T(8,128)} %collective-permute-done.3.refs_1_.refs_0_, ...), custom_call_target="tpu_custom_call" | custom-call | flops 11500000256 | bytes 36900000 | tf_op jit(solution)/shard_map/factor_at_columns/pallas_call | solution.py:453
  211.3 4.0 %collective-permute-start.11 = (f32[4,128,1024]{2,1,0:T(8,128)}, f32[4,128,1024]{2,1,0:T(8,128)}, u32[]{:S(2)}, u32[]{:S(2)}) collective-permute-start(f32[4,128,1024]{2,1,0:T(8,128)} %get-tuple-element.33), channel_id=1, source_target_pairs={{0,4},{4,0},{1,5},{5,1},{2,6},{6,2},{3,7},{7,3},{8,12},{12,8},{9,1... | collective-permute-start | bytes 6291464 | tf_op jit(solution)/shard_map/ppermute | solution.py:23
  215.3 9.8 %collective-permute-done.8.refs_2_ = f32[1024,512]{1,0:T(8,128)} collective-permute-done((f32[1024,512]{1,0:T(8,128)}, f32[1024,512]{1,0:T(8,128)}, u32[]{:S(2)}, u32[]{:S(2)}) %collective-permute-start.8) | collective-permute-done | bytes 2097184 | tf_op jit(solution)/shard_map/ppermute | solution.py:410
  225.1 8.4 %factor_rows.4 = (f32[2,8,2,128,128]{4,3,2,1,0:T(8,128)}, bf16[2,4,128,1536]{3,2,1,0:T(8,128)(2,1)S(1)}) custom-call(s32[74]{0:T(128)S(1)} %concatenate.6.meta.refs_6_, f32[1024,1024]{1,0:T(8,128)} %collective-permute-done.3.refs_1_.refs_0_, f32[1024,512]{1,0:T(8,128)} %collective-permute-done.7.refs_1_, ...), custom_call_target="tpu_custom_call", output_to_operand_aliasing={{0}: (6, {})} | custom-call | flops 6899999744 | bytes 22140000 | tf_op jit(solution)/shard_map/factor_rows/pallas_call | solution.py:508
  233.5 22.2 %update_tile.3 = (f32[2,8,2,128,2048]{4,3,2,1,0:T(8,128)}, f32[8,128]{1,0:T(8,128)S(1)}) custom-call(s32[74]{0:T(128)S(1)} %concatenate.6.meta.refs_6_, f32[8,2,2,128,1024]{4,3,2,1,0:T(8,128)} %bitcast.25, f32[8,128,1024]{2,1,0:T(8,128)} %collective-permute-done.10.refs_2_.refs_1_, bf16[2,8,128,1536]{3,2,1,0:T(8,128)(2,1)S(1)} %bitcast.39, ...), custom_call_target="tpu_custom_call" | custom-call | flops 27599998976 | bytes 88560000 | tf_op jit(solution)/shard_map/update_tile/pallas_call | solution.py:562
  255.6 8.5 %collective-permute-done.5.refs_2_ = f32[1024,512]{1,0:T(8,128)} collective-permute-done((f32[1024,512]{1,0:T(8,128)}, f32[1024,512]{1,0:T(8,128)}, u32[]{:S(2)}, u32[]{:S(2)}) %collective-permute-start.5) | collective-permute-done | bytes 2097184 | tf_op jit(solution)/shard_map/ppermute | solution.py:410
  264.1 9.0 %factor_rows.5 = (f32[2,8,2,128,128]{4,3,2,1,0:T(8,128)}, bf16[2,4,128,1536]{3,2,1,0:T(8,128)(2,1)S(1)}) custom-call(s32[74]{0:T(128)S(1)} %concatenate.6.meta.refs_6_, f32[1024,1024]{1,0:T(8,128)} %collective-permute-done.3.refs_1_.refs_0_, f32[1024,512]{1,0:T(8,128)} %collective-permute-done.4.refs_1_, ...), custom_call_target="tpu_custom_call", output_to_operand_aliasing={{0}: (6, {})} | custom-call | flops 6899999744 | bytes 22140000 | tf_op jit(solution)/shard_map/factor_rows/pallas_call | solution.py:508
  273.1 1.7 copy-done.1
  274.8 12.0 %update_tile.4 = (f32[2,8,2,128,2048]{4,3,2,1,0:T(8,128)}, f32[8,128]{1,0:T(8,128)}) custom-call(s32[74]{0:T(128)S(1)} %concatenate.6.meta.refs_6_, f32[8,2,2,128,1024]{4,3,2,1,0:T(8,128)} %bitcast.26, f32[4,128,1024]{2,1,0:T(8,128)} %collective-permute-done.12.refs_1_, ...), custom_call_target="tpu_custom_call", output_to_operand_aliasing={{0}: (6, {})} | custom-call | flops 13799999488 | bytes 44280000 | tf_op jit(solution)/shard_map/update_tile/pallas_call | solution.py:562
  287.2 11.7 %update_tile.5 = (f32[2,8,2,128,2048]{4,3,2,1,0:T(8,128)}, f32[8,128]{1,0:T(8,128)}) custom-call(s32[74]{0:T(128)S(1)} %concatenate.6.meta.refs_6_, f32[8,2,2,128,1024]{4,3,2,1,0:T(8,128)} %bitcast.27, f32[4,128,1024]{2,1,0:T(8,128)} %collective-permute-done.11.refs_1_, bf16[2,4,128,1536]{3,2,1,0:T(8,128)(2,1)S(1)} %copy-done.2, ...), custom_call_target="tpu_custom_call", output_to_operand_aliasing={{0}: (6, {})} | custom-call | flops 13799999488 | bytes 44280000 | tf_op jit(solution)/shard_map/update_tile/pallas_call | solution.py:562
  (51 shorter events, 1.2 us)
Async XLA Ops:
  2.8 5.8 %copy-start = (f32[4096,1024]{1,0:T(8,128)S(1)}, f32[4096,1024]{1,0:T(8,128)}, u32[]{:S(2)}) copy-start(f32[4096,1024]{1,0:T(8,128)} %param.6) | copy-start | bytes 50331652
  8.6 0.7 copy-start.5
  10.5 51.3 %copy-start.17 = (s32[2,2,4]{2,1,0:T(2,128)S(1)}, s32[2,2,4]{2,1,0:T(2,128)}, u32[]{:S(2)}) copy-start(s32[2,2,4]{2,1,0:T(2,128)} %constant.50.clone) | copy-start | bytes 196
  10.5 47.4 %collective-permute-start = (f32[512,1024]{1,0:T(8,128)S(1)}, f32[512,1024]{1,0:T(8,128)S(1)}, u32[]{:S(2)}, u32[]{:S(2)}) collective-permute-start(f32[512,1024]{1,0:T(8,128)S(1)} %bitcast.31), channel_id=1, source_target_pairs={{0,4},{4,0},{1,5},{5,1},{2,6},{6,2},{3,7},{7,3},{8,12},{12,8},{9,1... | collective-permute-start | bytes 6291464 | tf_op jit(solution)/shard_map/ppermute | solution.py:23
  11.1 16.2 %collective-permute-start.1 = (f32[10,128,128]{2,1,0:T(8,128)S(1)}, f32[10,128,128]{2,1,0:T(8,128)S(1)}, u32[]{:S(2)}, u32[]{:S(2)}) collective-permute-start(f32[10,128,128]{2,1,0:T(8,128)S(1)} %get-tuple-element.18), channel_id=1, source_target_pairs={{0,1},{1,0},{2,3},{3,2},{4,5},{5,4},{6,7},{7,6},{8,9},{9,8},{10,11... | collective-permute-start | bytes 1966088 | tf_op jit(solution)/shard_map/ppermute | solution.py:23
  27.3 33.8 %collective-permute-start.2 = (f32[10,128,128]{2,1,0:T(8,128)S(1)}, f32[10,128,128]{2,1,0:T(8,128)S(1)}, u32[]{:S(2)}, u32[]{:S(2)}) collective-permute-start(f32[10,128,128]{2,1,0:T(8,128)S(1)} %add.37), channel_id=1, source_target_pairs={{0,2},{1,3},{2,0},{3,1},{4,6},{5,7},{6,4},{7,5},{8,10},{9,11},{10,... | collective-permute-start | bytes 1966088 | tf_op jit(solution)/shard_map/ppermute | solution.py:23
  57.9 1.4 copy-start.3
  61.2 20.1 %collective-permute-start.6 = (f32[10,128,128]{2,1,0:T(8,128)S(1)}, f32[10,128,128]{2,1,0:T(8,128)}, u32[]{:S(2)}, u32[]{:S(2)}) collective-permute-start(f32[10,128,128]{2,1,0:T(8,128)S(1)} %add_multiply_fusion), channel_id=1, source_target_pairs={{0,4},{4,0},{1,5},{5,1},{2,6},{6,2},{3,7},{7,3},{8,12},{12,8},{9,1... | collective-permute-start | bytes 1966088 | tf_op jit(solution)/shard_map/ppermute | solution.py:23
  68.6 104.4 %collective-permute-start.9 = (f32[1024,1024]{1,0:T(8,128)}, f32[1024,1024]{1,0:T(8,128)}, u32[]{:S(2)}, u32[]{:S(2)}) collective-permute-start(f32[1024,1024]{1,0:T(8,128)} %maximum_multiply_fusion.refs_0_), channel_id=1, source_target_pairs={{2,1},{5,6},{10,9},{13,14},{18,17},{21,22},{26,25},{29,30}} | collective-permute-start | bytes 12582920 | tf_op jit(solution)/shard_map/ppermute | solution.py:410
  71.3 95.8 %collective-permute-start.3 = (f32[1024,1024]{1,0:T(8,128)}, f32[1024,1024]{1,0:T(8,128)}, u32[]{:S(2)}, u32[]{:S(2)}) collective-permute-start(f32[1024,1024]{1,0:T(8,128)} %maximum_multiply_fusion.refs_0_), channel_id=1, source_target_pairs={{2,3},{0,2},{5,4},{7,5},{10,11},{8,10},{13,12},{15,13},{18,19},{16... | collective-permute-start | bytes 12582920 | tf_op jit(solution)/shard_map/ppermute | solution.py:410
  77.2 134.1 %collective-permute-start.7 = (f32[1024,512]{1,0:T(8,128)}, f32[1024,512]{1,0:T(8,128)}, u32[]{:S(2)}, u32[]{:S(2)}) collective-permute-start(f32[1024,512]{1,0:T(8,128)} %get-tuple-element.36), channel_id=1, source_target_pairs={{2,0},{0,1},{5,7},{7,6},{10,8},{8,9},{13,15},{15,14},{18,16},{16,1... | collective-permute-start | bytes 6291464 | tf_op jit(solution)/shard_map/ppermute | solution.py:410
  79.3 176.4 %collective-permute-start.4 = (f32[1024,512]{1,0:T(8,128)}, f32[1024,512]{1,0:T(8,128)}, u32[]{:S(2)}, u32[]{:S(2)}) collective-permute-start(f32[1024,512]{1,0:T(8,128)} %get-tuple-element.37), channel_id=1, source_target_pairs={{2,0},{0,1},{5,7},{7,6},{10,8},{8,9},{13,15},{15,14},{18,16},{16,1... | collective-permute-start | bytes 6291464 | tf_op jit(solution)/shard_map/ppermute | solution.py:410
  89.8 98.6 %collective-permute-start.10 = (f32[8,128,1024]{2,1,0:T(8,128)}, f32[8,128,1024]{2,1,0:T(8,128)}, u32[]{:S(2)}, u32[]{:S(2)}) collective-permute-start(f32[8,128,1024]{2,1,0:T(8,128)} %dynamic-slice_bitcast_fusion), channel_id=1, source_target_pairs={{0,4},{4,0},{1,5},{5,1},{2,6},{6,2},{3,7},{7,3},{8,12},{12,8},{9,1... | collective-permute-start | bytes 12582920 | tf_op jit(solution)/shard_map/ppermute | solution.py:23
  157.0 1.0 copy-start.9
  158.0 1.0 copy-start.13
  159.5 1.0 copy-start.7
  162.4 12.0 %copy-start.10 = (f32[512,512]{1,0:T(8,128)S(1)}, f32[512,512]{1,0:T(8,128)}, u32[]{:S(2)}) copy-start(f32[512,512]{1,0:T(8,128)} %copy-done.9) | copy-start | bytes 3145732
  162.4 12.0 %copy-start.14 = (f32[512,512]{1,0:T(8,128)S(1)}, f32[512,512]{1,0:T(8,128)}, u32[]{:S(2)}) copy-start(f32[512,512]{1,0:T(8,128)} %copy-done.13) | copy-start | bytes 3145732
  171.7 53.4 %collective-permute-start.8 = (f32[1024,512]{1,0:T(8,128)}, f32[1024,512]{1,0:T(8,128)}, u32[]{:S(2)}, u32[]{:S(2)}) collective-permute-start(f32[1024,512]{1,0:T(8,128)} %get-tuple-element.34), channel_id=1, source_target_pairs={{2,3},{5,4},{10,11},{13,12},{18,19},{21,20},{26,27},{29,28}} | collective-permute-start | bytes 6291464 | tf_op jit(solution)/shard_map/ppermute | solution.py:410
  173.0 91.1 %collective-permute-start.5 = (f32[1024,512]{1,0:T(8,128)}, f32[1024,512]{1,0:T(8,128)}, u32[]{:S(2)}, u32[]{:S(2)}) collective-permute-start(f32[1024,512]{1,0:T(8,128)} %get-tuple-element.35), channel_id=1, source_target_pairs={{2,3},{5,4},{10,11},{13,12},{18,19},{21,20},{26,27},{29,28}} | collective-permute-start | bytes 6291464 | tf_op jit(solution)/shard_map/ppermute | solution.py:410
  191.5 9.7 %copy-start.4 = (f32[512,1024]{1,0:T(8,128)S(1)}, f32[512,1024]{1,0:T(8,128)}, u32[]{:S(2)}) copy-start(f32[512,1024]{1,0:T(8,128)} %copy-done.3) | copy-start | bytes 6291460
  191.5 9.7 %copy-start.8 = (f32[512,512]{1,0:T(8,128)S(1)}, f32[512,512]{1,0:T(8,128)}, u32[]{:S(2)}) copy-start(f32[512,512]{1,0:T(8,128)} %copy-done.7) | copy-start | bytes 3145732
  191.5 41.9 %slice-start.2 = ((s8[6291456]{0:T(1024)(128)(4,1)}), s8[4194304]{0:T(1024)(128)(4,1)S(1)}, s32[]{:S(2)}) async-start(s8[6291456]{0:T(1024)(128)(4,1)} %bitcast.38), calls=%async_computation.2 | async-start | bytes 8388608
  196.6 28.5 %copy-start.11 = (f32[512,512]{1,0:T(8,128)S(1)}, f32[512,512]{1,0:T(8,128)}, u32[]{:S(2)}) copy-start(f32[512,512]{1,0:T(8,128)} %copy-done.9) | copy-start | bytes 3145732
  196.6 28.5 %copy-start.15 = (f32[512,512]{1,0:T(8,128)S(1)}, f32[512,512]{1,0:T(8,128)}, u32[]{:S(2)}) copy-start(f32[512,512]{1,0:T(8,128)} %copy-done.13) | copy-start | bytes 3145732
  196.6 36.9 %slice-start.3 = ((s8[6291456]{0:T(1024)(128)(4,1)}), s8[2097152]{0:T(1024)(128)(4,1)S(1)}, s32[]{:S(2)}) async-start(s8[6291456]{0:T(1024)(128)(4,1)} %bitcast.38), calls=%async_computation.3 | async-start | bytes 4194304
  196.6 78.2 %collective-permute-start.12 = (f32[4,128,1024]{2,1,0:T(8,128)}, f32[4,128,1024]{2,1,0:T(8,128)}, u32[]{:S(2)}, u32[]{:S(2)}) collective-permute-start(f32[4,128,1024]{2,1,0:T(8,128)} %get-tuple-element.32), channel_id=1, source_target_pairs={{0,4},{4,0},{1,5},{5,1},{2,6},{6,2},{3,7},{7,3},{8,12},{12,8},{9,1... | collective-permute-start | bytes 6291464 | tf_op jit(solution)/shard_map/ppermute | solution.py:23
  211.3 75.9 %collective-permute-start.11 = (f32[4,128,1024]{2,1,0:T(8,128)}, f32[4,128,1024]{2,1,0:T(8,128)}, u32[]{:S(2)}, u32[]{:S(2)}) collective-permute-start(f32[4,128,1024]{2,1,0:T(8,128)} %get-tuple-element.33), channel_id=1, source_target_pairs={{0,4},{4,0},{1,5},{5,1},{2,6},{6,2},{3,7},{7,3},{8,12},{12,8},{9,1... | collective-permute-start | bytes 6291464 | tf_op jit(solution)/shard_map/ppermute | solution.py:23
  225.1 8.4 %copy-start.6 = (f32[4096]{0:T(1024)S(1)}, f32[4096]{0:T(1024)}, u32[]{:S(2)}) copy-start(f32[4096]{0:T(1024)} %param.7) | copy-start | bytes 49156
  233.5 30.7 %copy-start.12 = (f32[512,512]{1,0:T(8,128)S(1)}, f32[512,512]{1,0:T(8,128)}, u32[]{:S(2)}) copy-start(f32[512,512]{1,0:T(8,128)} %copy-done.9) | copy-start | bytes 3145732
  233.5 30.6 %copy-start.16 = (f32[512,512]{1,0:T(8,128)S(1)}, f32[512,512]{1,0:T(8,128)}, u32[]{:S(2)}) copy-start(f32[512,512]{1,0:T(8,128)} %copy-done.13) | copy-start | bytes 3145732
  264.1 10.7 %slice-start = ((s8[6291456]{0:T(1024)(128)(4,1)}), s8[4194304]{0:T(1024)(128)(4,1)S(1)}, s32[]{:S(2)}) async-start(s8[6291456]{0:T(1024)(128)(4,1)} %bitcast.29), calls=%async_computation | async-start | bytes 8388608
  264.1 10.7 %slice-start.1 = ((s8[6291456]{0:T(1024)(128)(4,1)}), s8[2097152]{0:T(1024)(128)(4,1)S(1)}, s32[]{:S(2)}) async-start(s8[6291456]{0:T(1024)(128)(4,1)} %bitcast.29), calls=%async_computation.1 | async-start | bytes 4194304
  273.1 1.7 copy-start.1
  274.8 12.4 %copy-start.2 = (bf16[2,4,128,1536]{3,2,1,0:T(8,128)(2,1)S(1)}, bf16[2,4,128,1536]{3,2,1,0:T(8,128)(2,1)}, u32[]{:S(2)}) copy-start(bf16[2,4,128,1536]{3,2,1,0:T(8,128)(2,1)} %copy-done.1) | copy-start | bytes 9437188

commit v4 on v3

--- a/solution.py
+++ b/solution.py
@@ -11,6 +11,11 @@
 NF = 8192
 BLK = 128
 HALVES = 2
+ORDER = 1
+B0 = 1
+GATE3 = 0
+MAGNET = 50
+BOTH = 0
 CHUNKS = (4, 4)
 ROWS_AT_ONCE = 2
 PACE = 1.0
@@ -324,6 +329,21 @@
     return pl.CostEstimate(flops=int(micros * 1.15e9), bytes_accessed=int(micros * 3.69e6), transcendentals=0)
 
 
+def pause_kernel(*refs):
+    refs[-1][...] = jnp.ones_like(refs[-1])
+
+
+def pause(micros, *after):
+    ones = pl.pallas_call(
+        pause_kernel,
+        in_specs=[pl.BlockSpec(memory_space=pl.ANY)] * len(after),
+        out_shape=jax.ShapeDtypeStruct((8, BLK), jnp.float32),
+        cost_estimate=about(micros),
+        name="pause",
+    )(*after)
+    return ones[0, 0]
+
+
 def per_device(contrib, front_diag, child_map, pivots):
     rows, cols = lax.axis_size("row"), lax.axis_size("col")
     r, q = lax.axis_index("row"), lax.axis_index("col")
@@ -395,10 +415,11 @@
         across = swapped(pivot_blocks, "col", bit)
         pivot_blocks = pivot_blocks + across
     pivot_blocks = gated(pivot_blocks, other)
+    behind = pause(50, across, other).astype(jnp.int32) if B0 == 3 else None
     for bit in range(half_bit, -1, -1):
         pivot_blocks = pivot_blocks + swapped(pivot_blocks, "row", bit)
 
-    both = jnp.concatenate([own, other]) * one_after(across).astype(f32)
+    both = jnp.concatenate([own, other]) * one_after([across, other, pivot_blocks][BOTH]).astype(f32)
     halves = HALVES if child_slots // ROWS_AT_ONCE % HALVES == 0 and order is None else 1
     held = [[both]]
     for n, (buffer, pairs) in enumerate(steps):
@@ -432,11 +453,11 @@
         first = 0
         for chunk in chunks:
             if not received:
-                start = one_after(pivot_blocks)
+                start = behind if B0 == 3 else one_after([pivot_blocks, other, across][B0])
             elif len(received) == 1:
                 start = one_after(inverse)
             else:
-                start = one_after(*[part for _, _, part in received[:-1]])
+                start = one_after(inverse) if len(received) == 1 else pause(MAGNET, inverse, part).astype(jnp.int32)
             part = lax.dynamic_slice(
                 own_view,
                 (first, partner_turns[turn] * start, 1 - mine, 0, 0),
@@ -480,8 +501,13 @@
     row_parts = [[] for _ in counts]
 
     order_of_work = [("rows", 0, 0), ("rows", 1, 0), ("tile", 0)]
-    order_of_work += [("rows", turn, n) for turn in range(1, sources) for n in range(counts[turn]) if (turn, n) != (1, 0)]
-    order_of_work += [("tile", turn) for turn in range(1, sources)]
+    chunks_of = [[(first, part) for at_turn, first, part in received if at_turn == turn] for turn in range(sources)]
+    order_of_work = [("rows", 0, 0), ("rows", 1, 0), ("tile", 0, 0)]
+    for turn in range(1, sources):
+        ahead = len(chunks_of[turn]) // 2 if counts[turn] == 2 and ORDER else 0
+        order_of_work += [("tile", turn, n) for n in range(ahead)]
+        order_of_work += [("rows", turn, n) for n in range(counts[turn]) if (turn, n) != (1, 0)]
+        order_of_work += [("tile", turn, n) for n in range(ahead, len(chunks_of[turn]))]
     for work, turn, *rest in order_of_work:
         parts_count = counts[turn]
         if work == "rows":
@@ -503,7 +529,7 @@
                 factor, aliases = jnp.zeros((2, 1, sources, BLK, BLK), f32), {}
             else:
                 aliases = {len(operands) + 1: 0}
-            operands += [factor, meta if token is None else token]
+            operands += [factor, [meta, received[0][2]][GATE3] if token is None else token]
             in_specs += [untouched] * 2
             factor, row_part = pl.pallas_call(
                 functools.partial(rows_kernel, info, rows, cols, few, share, turn, first, used),
@@ -532,7 +558,7 @@
             row_parts[turn].append(row_part)
             continue
 
-        for first, part in [(first, part) for at_turn, first, part in received if at_turn == turn]:
+        for first, part in [chunks_of[turn][rest[0]]]:
             at = first // ROWS_AT_ONCE
             row_part = row_parts[turn][first * parts_count // child_slots]
             left_at = at % (child_slots // parts_count // ROWS_AT_ONCE)

time: 303 us -> 306 us (level)
  waiting for transfers between devices: 65.8 us -> 78.7 us
  starting transfers between devices: 33 us -> 27.2 us
    ppermute x7, waiting for transfers between devices: 43 us -> 53.6 us  [swapped(): lax.ppermute(shard, axis, [(i, i ^ 1 << bit) for i in range(lax.axis_size...]
    ppermute x7, starting transfers between devices: 22.2 us -> 15.9 us  [swapped(): lax.ppermute(shard, axis, [(i, i ^ 1 << bit) for i in range(lax.axis_size...]
    reshape x2 -> x3, local copies, waits for them, and re-layouts: 9.91 us -> 11.1 us  [per_device(): part = lax.dynamic_slice(own_view, (first, partner_turns[turn] * start, 1...]
    unnamed x44 -> x32, local copies, waits for them, and re-layouts: 12.6 us -> 12.6 us
  transfers between devices with their start and end apart: 13 -> 13, of which waited for: 6 -> 4; matrix products, arithmetic and copies ran while one was open for 10% -> 9% of each run, Pallas kernels for 45% -> 44%
where the time goes in v4:
time: 306 us; the launch traced here: 305 us
  Pallas kernels  147 us (48%)
  waiting for transfers between devices  78.7 us (26%)
  local copies, waits for them, and re-layouts  38.8 us (13%)
  starting transfers between devices  27.2 us (9%)
  between operations  7.17 us (2%)
  other arithmetic  5.98 us (2%)
    pallas_call x1, Pallas kernels, per_device(): pl.pallas_call(functools.partial(cholesky_kernel, pivot_count), out_shape...  58.9 us
    ppermute x7, waiting for transfers between devices, swapped(): lax.ppermute(shard, axis, [(i, i ^ 1 << bit) for i in range(lax.axis_size...  53.6 us
    pallas_call x3, Pallas kernels, per_device(): pl.pallas_call(functools.partial(update_kernel, info, rows, cols, child_s...  45.5 us
    pallas_call x3, Pallas kernels, per_device(): pl.pallas_call(functools.partial(rows_kernel, info, rows, cols, few, shar...  29.8 us
    ppermute x6, waiting for transfers between devices, per_device(): held.append([lax.ppermute(part, ('row', 'col'), pairs) for part in sent])  25.1 us
    ppermute x7, starting transfers between devices, swapped(): lax.ppermute(shard, axis, [(i, i ^ 1 << bit) for i in range(lax.axis_size...  15.9 us
    unnamed x32, local copies, waits for them, and re-layouts  12.6 us
    ppermute x6, starting transfers between devices, per_device(): held.append([lax.ppermute(part, ('row', 'col'), pairs) for part in sent])  11.3 us
  transfers between devices with their start and end apart: 13, of which 4 were waited for; matrix products, arithmetic and copies ran while one was open for 9% of the time, Pallas kernels for 44%

profile of v4, /device:TPU:6, one launch (start us, length us, event | category | flops | bytes accessed | tf_op | source)
XLA Modules:
  0.0 304.7 jit_solution(9488194031380366613)
XLA Ops:
  0.6 0.8 reshape.55
  1.4 0.7 fusion
  2.1 0.7 concatenate.6.meta.refs_6_
  2.8 5.8 %copy-done = f32[4096,1024]{1,0:T(8,128)S(1)} copy-done((f32[4096,1024]{1,0:T(8,128)S(1)}, f32[4096,1024]{1,0:T(8,128)}, u32[]{:S(2)}) %copy-start) | copy-done | bytes 16777240
  8.6 0.7 copy-done.2
  9.3 1.2 pick.1
  10.5 0.6 collective-permute-start
  11.1 1.6 collective-permute-start.1
  12.6 14.6 %collective-permute-done.1 = f32[10,128,128]{2,1,0:T(8,128)S(1)} collective-permute-done((f32[10,128,128]{2,1,0:T(8,128)S(1)}, f32[10,128,128]{2,1,0:T(8,128)S(1)}, u32[]{:S(2)}, u32[]{:S(2)}) %collective-permute-start.1) | collective-permute-done | bytes 655392 | tf_op jit(solution)/shard_map/ppermute | solution.py:28
  27.3 0.1 add.37
  27.3 2.7 collective-permute-start.2
  30.0 0.6 constant_dynamic-slice_fusion
  30.6 27.1 %collective-permute-done.2 = f32[10,128,128]{2,1,0:T(8,128)S(1)} collective-permute-done((f32[10,128,128]{2,1,0:T(8,128)S(1)}, f32[10,128,128]{2,1,0:T(8,128)S(1)}, u32[]{:S(2)}, u32[]{:S(2)}) %collective-permute-start.2) | collective-permute-done | bytes 655392 | tf_op jit(solution)/shard_map/ppermute | solution.py:28
  57.7 0.5 slice.28
  59.6 1.2 slice.29
  62.1 1.2 add_multiply_fusion
  63.3 1.6 collective-permute-start.6
  64.9 4.6 %maximum_multiply_fusion.refs_0_ = f32[1024,1024]{1,0:T(8,128)} fusion(f32[512,1024]{1,0:T(8,128)} %collective-permute-done.other, f32[512,1024]{1,0:T(8,128)S(1)} %bitcast.33, f32[]{:T(128)} %bitcast.6), kind=kLoop, calls=%fused_computation | loop fusion | flops 2097152 | bytes 8388612 | tf_op jit(solution)/shard_map/mul | solution.py:422
  70.1 2.7 collective-permute-start.9
  72.9 1.3 collective-permute-start.3
  74.1 4.7 %fusion.2 = (f32[1024,512]{1,0:T(8,128)}, f32[1024,512]{1,0:T(8,128)}) fusion(f32[1024,1024]{1,0:T(8,128)} %maximum_multiply_fusion.refs_0_), kind=kLoop, calls=%fused_computation.9 | loop fusion | bytes 8388608 | tf_op jit(solution)/shard_map/split | solution.py:428
  78.9 2.0 collective-permute-start.7
  80.9 2.0 collective-permute-start.4
  82.9 4.7 %dynamic-slice_bitcast_fusion = f32[8,128,1024]{2,1,0:T(8,128)} fusion(f32[8,2,2,128,1024]{4,3,2,1,0:T(8,128)} %bitcast.23, s32[]{:T(128)S(6)} %select_n.55, s32[]{:T(128)S(6)} %select_n.54), kind=kLoop, calls=%fused_computation.1 | loop fusion | bytes 8388616 | tf_op jit(solution)/shard_map/reshape | solution.py:465
  87.7 6.4 %collective-permute-start.11 = (f32[8,128,1024]{2,1,0:T(8,128)}, f32[8,128,1024]{2,1,0:T(8,128)}, u32[]{:S(2)}, u32[]{:S(2)}) collective-permute-start(f32[8,128,1024]{2,1,0:T(8,128)} %dynamic-slice_bitcast_fusion), channel_id=1, source_target_pairs={{0,4},{4,0},{1,5},{5,1},{2,6},{6,2},{3,7},{7,3},{8,12},{12,8},{9,1... | collective-permute-start | bytes 12582920 | tf_op jit(solution)/shard_map/ppermute | solution.py:28
  94.2 58.9 %factor_pivots.1 = (f32[512,512]{1,0:T(8,128)S(1)}, f32[512,512]{1,0:T(8,128)S(1)}, f32[512,512]{1,0:T(8,128)S(1)}) custom-call(f32[10,128,128]{2,1,0:T(8,128)S(1)} %add.39.blocks), custom_call_target="tpu_custom_call" | custom-call | flops 67849998336 | bytes 217710000 | tf_op jit(solution)/shard_map/factor_pivots/pallas_call | solution.py:436
  153.1 1.0 copy-done.6
  154.0 1.0 copy-done.8
  155.0 0.6 slice.25
  157.4 3.2 %dynamic-slice_bitcast_fusion.2.refs_1_ = f32[4,128,1024]{2,1,0:T(8,128)} fusion(f32[8,2,2,128,1024]{4,3,2,1,0:T(8,128)} %bitcast.24, s32[]{:T(128)S(6)} %select_n.53, s32[]{:T(128)S(6)} %select_n.54), kind=kLoop, calls=%fused_computation.3 | loop fusion | bytes 4194312 | tf_op jit(solution)/shard_map/reshape | solution.py:465
  160.5 0.6 pause.1
  161.1 1.3 slice.27
  163.7 3.2 %dynamic-slice_bitcast_fusion.1 = f32[4,128,1024]{2,1,0:T(8,128)} fusion(f32[8,2,2,128,1024]{4,3,2,1,0:T(8,128)} %bitcast.25, s32[]{:T(128)S(6)} %select_n.56, s32[]{:T(128)S(6)} %select_n.54), kind=kLoop, calls=%fused_computation.2 | loop fusion | bytes 4194312 | tf_op jit(solution)/shard_map/reshape | solution.py:465
  166.9 3.1 %collective-permute-start.10 = (f32[4,128,1024]{2,1,0:T(8,128)}, f32[4,128,1024]{2,1,0:T(8,128)S(1)}, u32[]{:S(2)}, u32[]{:S(2)}) collective-permute-start(f32[4,128,1024]{2,1,0:T(8,128)} %dynamic-slice_bitcast_fusion.2.refs_1_), channel_id=1, source_target_pairs={{0,4},{4,0},{1,5},{5,1},{2,6},{6,2},{3,7},{7,3},{8,12},{12,8},{9,1... | collective-permute-start | bytes 6291464 | tf_op jit(solution)/shard_map/ppermute | solution.py:28
  170.0 4.0 %fusion.1 = (f32[1024,512]{1,0:T(8,128)S(1)}, f32[1024,512]{1,0:T(8,128)}) fusion(f32[1024,1024]{1,0:T(8,128)} %collective-permute-done.3.refs_1_.refs_0_), kind=kLoop, calls=%fused_computation.8 | loop fusion | bytes 8388608 | tf_op jit(solution)/shard_map/split | solution.py:428
  174.0 11.9 %collective-permute-done.11.refs_2_.refs_1_ = f32[8,128,1024]{2,1,0:T(8,128)} collective-permute-done((f32[8,128,1024]{2,1,0:T(8,128)}, f32[8,128,1024]{2,1,0:T(8,128)}, u32[]{:S(2)}, u32[]{:S(2)}) %collective-permute-start.11) | collective-permute-done | bytes 4194336 | tf_op jit(solution)/shard_map/ppermute | solution.py:28
  185.9 1.7 collective-permute-start.8
  187.6 10.9 %factor_at_columns.1.refs_3_ = bf16[1536,2048]{1,0:T(8,128)(2,1)} custom-call(s32[74]{0:T(128)S(1)} %concatenate.6.meta.refs_6_, f32[512,1024]{1,0:T(8,128)S(1)} %bitcast.34, f32[512,1024]{1,0:T(8,128)} %collective-permute-done.other, f32[512,512]{1,0:T(8,128)S(1)} %copy-done.5, f32[1024,1024]{1,0:T(8,128)} %collective-permute-done.3.refs_1_.refs_0_, ...), custom_call_target="tpu_custom_call" | custom-call | flops 11500000256 | bytes 36900000 | tf_op jit(solution)/shard_map/factor_at_columns/pallas_call | solution.py:474
  198.6 13.7 %factor_rows.3 = (f32[2,8,2,128,128]{4,3,2,1,0:T(8,128)}, bf16[2,8,128,1536]{3,2,1,0:T(8,128)(2,1)}) custom-call(s32[74]{0:T(128)S(1)} %concatenate.6.meta.refs_6_, f32[1024,1024]{1,0:T(8,128)S(1)} %copy-done.1, f32[1024,1024]{1,0:T(8,128)} %collective-permute-done.3.refs_1_.refs_0_, f32[1024,1024]{1,0:T(8,128)} %collective-permute-done.9.refs_2_.refs_1_, ...), custom_call_target="tpu_custom_call" | custom-call | flops 13799999488 | bytes 44280000 | tf_op jit(solution)/shard_map/factor_rows/pallas_call | solution.py:534
  212.3 1.5 collective-permute-start.5
  213.9 25.1 %collective-permute-done.8.refs_2_ = f32[1024,512]{1,0:T(8,128)S(1)} collective-permute-done((f32[1024,512]{1,0:T(8,128)S(1)}, f32[1024,512]{1,0:T(8,128)S(1)}, u32[]{:S(2)}, u32[]{:S(2)}) %collective-permute-start.8) | collective-permute-done | bytes 2097184 | tf_op jit(solution)/shard_map/ppermute | solution.py:431
  238.9 8.1 %factor_rows.4 = (f32[2,8,2,128,128]{4,3,2,1,0:T(8,128)}, bf16[2,4,128,1536]{3,2,1,0:T(8,128)(2,1)S(1)}) custom-call(s32[74]{0:T(128)S(1)} %concatenate.6.meta.refs_6_, f32[1024,1024]{1,0:T(8,128)} %collective-permute-done.3.refs_1_.refs_0_, f32[1024,512]{1,0:T(8,128)} %collective-permute-done.7.refs_1_, ...), custom_call_target="tpu_custom_call", output_to_operand_aliasing={{0}: (6, {})} | custom-call | flops 6899999744 | bytes 22140000 | tf_op jit(solution)/shard_map/factor_rows/pallas_call | solution.py:534
  247.0 2.9 copy-done.11
  250.0 22.2 %update_tile.3 = (f32[2,8,2,128,2048]{4,3,2,1,0:T(8,128)}, f32[8,128]{1,0:T(8,128)}) custom-call(s32[74]{0:T(128)S(1)} %concatenate.6.meta.refs_6_, f32[8,2,2,128,1024]{4,3,2,1,0:T(8,128)} %bitcast.26, f32[8,128,1024]{2,1,0:T(8,128)} %collective-permute-done.11.refs_2_.refs_1_, bf16[2,8,128,1536]{3,2,1,0:T(8,128)(2,1)S(1)} %copy-done.11, ...), custom_call_target="tpu_custom_call" | custom-call | flops 27599998976 | bytes 88560000 | tf_op jit(solution)/shard_map/update_tile/pallas_call | solution.py:588
  272.2 11.6 %update_tile.4 = (f32[2,8,2,128,2048]{4,3,2,1,0:T(8,128)}, f32[8,128]{1,0:T(8,128)S(1)}) custom-call(s32[74]{0:T(128)S(1)} %concatenate.6.meta.refs_6_, f32[8,2,2,128,1024]{4,3,2,1,0:T(8,128)} %bitcast.27, f32[4,128,1024]{2,1,0:T(8,128)S(1)} %collective-permute-done.10.refs_1_, ...), custom_call_target="tpu_custom_call", output_to_operand_aliasing={{0}: (6, {})} | custom-call | flops 13799999488 | bytes 44280000 | tf_op jit(solution)/shard_map/update_tile/pallas_call | solution.py:588
  283.8 1.2 copy-done.10
  285.0 8.0 %factor_rows.5 = (f32[2,8,2,128,128]{4,3,2,1,0:T(8,128)}, bf16[2,4,128,1536]{3,2,1,0:T(8,128)(2,1)S(1)}) custom-call(s32[74]{0:T(128)S(1)} %concatenate.6.meta.refs_6_, f32[1024,1024]{1,0:T(8,128)} %collective-permute-done.3.refs_1_.refs_0_, f32[1024,512]{1,0:T(8,128)} %collective-permute-done.4.refs_1_, ...), custom_call_target="tpu_custom_call", output_to_operand_aliasing={{0}: (6, {})} | custom-call | flops 6899999744 | bytes 22140000 | tf_op jit(solution)/shard_map/factor_rows/pallas_call | solution.py:534
  293.0 11.6 %update_tile.5 = (f32[2,8,2,128,2048]{4,3,2,1,0:T(8,128)}, f32[8,128]{1,0:T(8,128)}) custom-call(s32[74]{0:T(128)S(1)} %concatenate.6.meta.refs_6_, f32[8,2,2,128,1024]{4,3,2,1,0:T(8,128)} %bitcast.28, f32[4,128,1024]{2,1,0:T(8,128)} %collective-permute-done.12.refs_1_, ...), custom_call_target="tpu_custom_call", output_to_operand_aliasing={{0}: (6, {})} | custom-call | flops 13799999488 | bytes 44280000 | tf_op jit(solution)/shard_map/update_tile/pallas_call | solution.py:588
  (39 shorter events, 0.2 us)
Async XLA Ops:
  2.8 5.8 %copy-start = (f32[4096,1024]{1,0:T(8,128)S(1)}, f32[4096,1024]{1,0:T(8,128)}, u32[]{:S(2)}) copy-start(f32[4096,1024]{1,0:T(8,128)} %param.6) | copy-start | bytes 50331652
  8.6 0.7 copy-start.2
  9.3 20.7 %copy-start.13 = (s32[2,2,4]{2,1,0:T(2,128)S(1)}, s32[2,2,4]{2,1,0:T(2,128)}, u32[]{:S(2)}) copy-start(s32[2,2,4]{2,1,0:T(2,128)} %constant.46.clone) | copy-start | bytes 196
  10.5 49.1 %collective-permute-start = (f32[512,1024]{1,0:T(8,128)S(1)}, f32[512,1024]{1,0:T(8,128)}, u32[]{:S(2)}, u32[]{:S(2)}) collective-permute-start(f32[512,1024]{1,0:T(8,128)S(1)} %bitcast.32), channel_id=1, source_target_pairs={{0,4},{4,0},{1,5},{5,1},{2,6},{6,2},{3,7},{7,3},{8,12},{12,8},{9,1... | collective-permute-start | bytes 6291464 | tf_op jit(solution)/shard_map/ppermute | solution.py:28
  11.1 16.2 %collective-permute-start.1 = (f32[10,128,128]{2,1,0:T(8,128)S(1)}, f32[10,128,128]{2,1,0:T(8,128)S(1)}, u32[]{:S(2)}, u32[]{:S(2)}) collective-permute-start(f32[10,128,128]{2,1,0:T(8,128)S(1)} %get-tuple-element.18), channel_id=1, source_target_pairs={{0,1},{1,0},{2,3},{3,2},{4,5},{5,4},{6,7},{7,6},{8,9},{9,8},{10,11... | collective-permute-start | bytes 1966088 | tf_op jit(solution)/shard_map/ppermute | solution.py:28
  27.3 30.4 %collective-permute-start.2 = (f32[10,128,128]{2,1,0:T(8,128)S(1)}, f32[10,128,128]{2,1,0:T(8,128)S(1)}, u32[]{:S(2)}, u32[]{:S(2)}) collective-permute-start(f32[10,128,128]{2,1,0:T(8,128)S(1)} %add.37), channel_id=1, source_target_pairs={{0,2},{1,3},{2,0},{3,1},{4,6},{5,7},{6,4},{7,5},{8,10},{9,11},{10,... | collective-permute-start | bytes 1966088 | tf_op jit(solution)/shard_map/ppermute | solution.py:28
  57.7 4.3 %copy-start.12 = (f32[10,128,128]{2,1,0:T(8,128)}, f32[10,128,128]{2,1,0:T(8,128)S(1)}, u32[]{:S(2)}) copy-start(f32[10,128,128]{2,1,0:T(8,128)S(1)} %collective-permute-done.2) | copy-start | bytes 1966084
  63.3 24.4 %collective-permute-start.6 = (f32[10,128,128]{2,1,0:T(8,128)S(1)}, f32[10,128,128]{2,1,0:T(8,128)S(1)}, u32[]{:S(2)}, u32[]{:S(2)}) collective-permute-start(f32[10,128,128]{2,1,0:T(8,128)S(1)} %add_multiply_fusion), channel_id=1, source_target_pairs={{0,4},{4,0},{1,5},{5,1},{2,6},{6,2},{3,7},{7,3},{8,12},{12,8},{9,1... | collective-permute-start | bytes 1966088 | tf_op jit(solution)/shard_map/ppermute | solution.py:28
  70.1 103.9 %collective-permute-start.9 = (f32[1024,1024]{1,0:T(8,128)}, f32[1024,1024]{1,0:T(8,128)}, u32[]{:S(2)}, u32[]{:S(2)}) collective-permute-start(f32[1024,1024]{1,0:T(8,128)} %maximum_multiply_fusion.refs_0_), channel_id=1, source_target_pairs={{2,1},{5,6},{10,9},{13,14},{18,17},{21,22},{26,25},{29,30}} | collective-permute-start | bytes 12582920 | tf_op jit(solution)/shard_map/ppermute | solution.py:431
  72.9 94.1 %collective-permute-start.3 = (f32[1024,1024]{1,0:T(8,128)}, f32[1024,1024]{1,0:T(8,128)}, u32[]{:S(2)}, u32[]{:S(2)}) collective-permute-start(f32[1024,1024]{1,0:T(8,128)} %maximum_multiply_fusion.refs_0_), channel_id=1, source_target_pairs={{2,3},{0,2},{5,4},{7,5},{10,11},{8,10},{13,12},{15,13},{18,19},{16... | collective-permute-start | bytes 12582920 | tf_op jit(solution)/shard_map/ppermute | solution.py:431
  78.9 133.5 %collective-permute-start.7 = (f32[1024,512]{1,0:T(8,128)}, f32[1024,512]{1,0:T(8,128)}, u32[]{:S(2)}, u32[]{:S(2)}) collective-permute-start(f32[1024,512]{1,0:T(8,128)} %get-tuple-element.34), channel_id=1, source_target_pairs={{2,0},{0,1},{5,7},{7,6},{10,8},{8,9},{13,15},{15,14},{18,16},{16,1... | collective-permute-start | bytes 6291464 | tf_op jit(solution)/shard_map/ppermute | solution.py:431
  80.9 202.9 %collective-permute-start.4 = (f32[1024,512]{1,0:T(8,128)}, f32[1024,512]{1,0:T(8,128)}, u32[]{:S(2)}, u32[]{:S(2)}) collective-permute-start(f32[1024,512]{1,0:T(8,128)} %get-tuple-element.35), channel_id=1, source_target_pairs={{2,0},{0,1},{5,7},{7,6},{10,8},{8,9},{13,15},{15,14},{18,16},{16,1... | collective-permute-start | bytes 6291464 | tf_op jit(solution)/shard_map/ppermute | solution.py:431
  87.7 98.2 %collective-permute-start.11 = (f32[8,128,1024]{2,1,0:T(8,128)}, f32[8,128,1024]{2,1,0:T(8,128)}, u32[]{:S(2)}, u32[]{:S(2)}) collective-permute-start(f32[8,128,1024]{2,1,0:T(8,128)} %dynamic-slice_bitcast_fusion), channel_id=1, source_target_pairs={{0,4},{4,0},{1,5},{5,1},{2,6},{6,2},{3,7},{7,3},{8,12},{12,8},{9,1... | collective-permute-start | bytes 12582920 | tf_op jit(solution)/shard_map/ppermute | solution.py:28
  153.1 1.0 copy-start.6
  154.0 1.0 copy-start.8
  155.0 5.5 %copy-start.4 = (f32[512,512]{1,0:T(8,128)}, f32[512,512]{1,0:T(8,128)S(1)}, u32[]{:S(2)}) copy-start(f32[512,512]{1,0:T(8,128)S(1)} %get-tuple-element.23.inverse.refs_0_) | copy-start | bytes 3145732
  166.9 20.7 %copy-start.5 = (f32[512,512]{1,0:T(8,128)S(1)}, f32[512,512]{1,0:T(8,128)}, u32[]{:S(2)}) copy-start(f32[512,512]{1,0:T(8,128)} %copy-done.4) | copy-start | bytes 3145732
  166.9 105.3 %collective-permute-start.10 = (f32[4,128,1024]{2,1,0:T(8,128)}, f32[4,128,1024]{2,1,0:T(8,128)S(1)}, u32[]{:S(2)}, u32[]{:S(2)}) collective-permute-start(f32[4,128,1024]{2,1,0:T(8,128)} %dynamic-slice_bitcast_fusion.2.refs_1_), channel_id=1, source_target_pairs={{0,4},{4,0},{1,5},{5,1},{2,6},{6,2},{3,7},{7,3},{8,12},{12,8},{9,1... | collective-permute-start | bytes 6291464 | tf_op jit(solution)/shard_map/ppermute | solution.py:28
  174.0 119.0 %collective-permute-start.12 = (f32[4,128,1024]{2,1,0:T(8,128)}, f32[4,128,1024]{2,1,0:T(8,128)}, u32[]{:S(2)}, u32[]{:S(2)}) collective-permute-start(f32[4,128,1024]{2,1,0:T(8,128)} %dynamic-slice_bitcast_fusion.1), channel_id=1, source_target_pairs={{0,4},{4,0},{1,5},{5,1},{2,6},{6,2},{3,7},{7,3},{8,12},{12,8},{9,1... | collective-permute-start | bytes 6291464 | tf_op jit(solution)/shard_map/ppermute | solution.py:28
  185.9 12.7 %copy-start.1 = (f32[1024,1024]{1,0:T(8,128)S(1)}, f32[1024,1024]{1,0:T(8,128)}, u32[]{:S(2)}) copy-start(f32[1024,1024]{1,0:T(8,128)} %maximum_multiply_fusion.refs_0_) | copy-start | bytes 12582916
  185.9 12.7 %copy-start.7 = (f32[512,512]{1,0:T(8,128)S(1)}, f32[512,512]{1,0:T(8,128)}, u32[]{:S(2)}) copy-start(f32[512,512]{1,0:T(8,128)} %copy-done.6) | copy-start | bytes 3145732
  185.9 12.7 %copy-start.9 = (f32[512,512]{1,0:T(8,128)S(1)}, f32[512,512]{1,0:T(8,128)}, u32[]{:S(2)}) copy-start(f32[512,512]{1,0:T(8,128)} %copy-done.8) | copy-start | bytes 3145732
  185.9 53.0 %collective-permute-start.8 = (f32[1024,512]{1,0:T(8,128)S(1)}, f32[1024,512]{1,0:T(8,128)S(1)}, u32[]{:S(2)}, u32[]{:S(2)}) collective-permute-start(f32[1024,512]{1,0:T(8,128)S(1)} %get-tuple-element.32), channel_id=1, source_target_pairs={{2,3},{5,4},{10,11},{13,12},{18,19},{21,20},{26,27},{29,28}} | collective-permute-start | bytes 6291464 | tf_op jit(solution)/shard_map/ppermute | solution.py:431
  212.3 71.5 %collective-permute-start.5 = (f32[1024,512]{1,0:T(8,128)}, f32[1024,512]{1,0:T(8,128)S(1)}, u32[]{:S(2)}, u32[]{:S(2)}) collective-permute-start(f32[1024,512]{1,0:T(8,128)} %get-tuple-element.33), channel_id=1, source_target_pairs={{2,3},{5,4},{10,11},{13,12},{18,19},{21,20},{26,27},{29,28}} | collective-permute-start | bytes 6291464 | tf_op jit(solution)/shard_map/ppermute | solution.py:431
  238.9 8.1 %copy-start.3 = (f32[4096]{0:T(1024)S(1)}, f32[4096]{0:T(1024)}, u32[]{:S(2)}) copy-start(f32[4096]{0:T(1024)} %param.7) | copy-start | bytes 49156
  247.0 25.2 %slice-start = ((s8[6291456]{0:T(1024)(128)(4,1)}), s8[4194304]{0:T(1024)(128)(4,1)S(1)}, s32[]{:S(2)}) async-start(s8[6291456]{0:T(1024)(128)(4,1)} %bitcast.30), calls=%async_computation | async-start | bytes 8388608
  247.0 2.9 copy-start.11
  250.0 22.3 %slice-start.1 = ((s8[6291456]{0:T(1024)(128)(4,1)}), s8[2097152]{0:T(1024)(128)(4,1)S(1)}, s32[]{:S(2)}) async-start(s8[6291456]{0:T(1024)(128)(4,1)} %bitcast.30), calls=%async_computation.1 | async-start | bytes 4194304
  283.8 1.2 copy-start.10

commit v5 on v4

--- a/solution.py
+++ b/solution.py
@@ -12,9 +12,11 @@
 BLK = 128
 HALVES = 2
 ORDER = 1
-B0 = 1
+B0 = 3
 GATE3 = 0
 MAGNET = 50
+G5 = 0
+G6 = 0
 BOTH = 0
 CHUNKS = (4, 4)
 ROWS_AT_ONCE = 2
@@ -413,9 +415,9 @@
     pivot_blocks = pivot_part
     for bit in range(cols.bit_length() - 1):
         across = swapped(pivot_blocks, "col", bit)
+        across_first = across if bit == 0 else across_first
         pivot_blocks = pivot_blocks + across
     pivot_blocks = gated(pivot_blocks, other)
-    behind = pause(50, across, other).astype(jnp.int32) if B0 == 3 else None
     for bit in range(half_bit, -1, -1):
         pivot_blocks = pivot_blocks + swapped(pivot_blocks, "row", bit)
 
@@ -453,11 +455,20 @@
         first = 0
         for chunk in chunks:
             if not received:
-                start = behind if B0 == 3 else one_after([pivot_blocks, other, across][B0])
+                start = one_after([pivot_blocks, other, across, across_first][B0])
             elif len(received) == 1:
                 start = one_after(inverse)
             else:
-                start = one_after(inverse) if len(received) == 1 else pause(MAGNET, inverse, part).astype(jnp.int32)
+                if len(received) == 1:
+                    start = one_after(inverse)
+                elif G5 == 0:
+                    start = pause(MAGNET, inverse, part).astype(jnp.int32)
+                elif G5 == 1:
+                    start = one_after(inverse, received[0][2])
+                elif G5 == 2:
+                    start = pause(MAGNET, received[0][2], part).astype(jnp.int32)
+                else:
+                    start = pause(MAGNET, inverse, part, *[held[n][0] for n in early]).astype(jnp.int32)
             part = lax.dynamic_slice(
                 own_view,
                 (first, partner_turns[turn] * start, 1 - mine, 0, 0),
@@ -502,7 +513,7 @@
 
     order_of_work = [("rows", 0, 0), ("rows", 1, 0), ("tile", 0)]
     chunks_of = [[(first, part) for at_turn, first, part in received if at_turn == turn] for turn in range(sources)]
-    order_of_work = [("rows", 0, 0), ("rows", 1, 0), ("tile", 0, 0)]
+    order_of_work = [("rows", 0, 0), ("rows", 1, 0), ("tile", 0, 0)] if G6 else [("rows", 0, 0), ("tile", 0, 0), ("rows", 1, 0)]
     for turn in range(1, sources):
         ahead = len(chunks_of[turn]) // 2 if counts[turn] == 2 and ORDER else 0
         order_of_work += [("tile", turn, n) for n in range(ahead)]
@@ -578,10 +589,10 @@
             ]
             operands = [own_view, part, row_part, col_parts, diag_view]
             aliases = {}
-            if tile is None:
+            if tile is None and G6:
                 in_specs.append(untouched)
                 operands.append(row_parts[1][0])
-            else:
+            elif tile is not None:
                 in_specs.append(untouched)
                 operands.append(tile)
                 aliases = {len(operands): 0}

time: 306 us -> 290 us (0.948)
  waiting for transfers between devices: 78.7 us -> 67.8 us
  starting transfers between devices: 27.2 us -> 21.6 us
    ppermute x7, waiting for transfers between devices: 53.6 us -> 38 us  [swapped(): lax.ppermute(shard, axis, [(i, i ^ 1 << bit) for i in range(lax.axis_size...]
    ppermute x7, starting transfers between devices: 15.9 us -> 10.7 us  [swapped(): lax.ppermute(shard, axis, [(i, i ^ 1 << bit) for i in range(lax.axis_size...]
    ppermute x6, waiting for transfers between devices: 25.1 us -> 29.8 us  [per_device(): held.append([lax.ppermute(part, ('row', 'col'), pairs) for part in sent])]
    unnamed x32 -> x28, local copies, waits for them, and re-layouts: 12.6 us -> 12 us
  transfers between devices with their start and end apart: 13 -> 13, of which waited for: 4 -> 4; matrix products, arithmetic and copies ran while one was open for 9% -> 11% of each run, Pallas kernels for 44% -> 46%
where the time goes in v5:
time: 290 us; the launch traced here: 289 us
  Pallas kernels  146 us (50%)
  waiting for transfers between devices  67.8 us (23%)
  local copies, waits for them, and re-layouts  40 us (14%)
  starting transfers between devices  21.6 us (7%)
  between operations  8.58 us (3%)
  other arithmetic  4.81 us (2%)
    pallas_call x1, Pallas kernels, per_device(): pl.pallas_call(functools.partial(cholesky_kernel, pivot_count), out_shape...  58.9 us
    pallas_call x3, Pallas kernels, per_device(): pl.pallas_call(functools.partial(update_kernel, info, rows, cols, child_s...  43.5 us
    ppermute x7, waiting for transfers between devices, swapped(): lax.ppermute(shard, axis, [(i, i ^ 1 << bit) for i in range(lax.axis_size...  38 us
    pallas_call x3, Pallas kernels, per_device(): pl.pallas_call(functools.partial(rows_kernel, info, rows, cols, few, shar...  31.1 us
    ppermute x6, waiting for transfers between devices, per_device(): held.append([lax.ppermute(part, ('row', 'col'), pairs) for part in sent])  29.8 us
    unnamed x28, local copies, waits for them, and re-layouts  12 us
    reshape x3, local copies, waits for them, and re-layouts, per_device(): part = lax.dynamic_slice(own_view, (first, partner_turns[turn] * start, 1...  11.1 us
    pallas_call x1, Pallas kernels, per_device(): pl.pallas_call(functools.partial(columns_kernel, info, rows, cols, child_...  10.9 us
  transfers between devices with their start and end apart: 13, of which 4 were waited for; matrix products, arithmetic and copies ran while one was open for 11% of the time, Pallas kernels for 46%

profile of v5, /device:TPU:6, one launch (start us, length us, event | category | flops | bytes accessed | tf_op | source)
XLA Modules:
  0.0 289.0 jit_solution(3567287006388876576)
XLA Ops:
  0.6 0.8 reshape.61
  1.4 0.7 fusion
  2.1 0.7 concatenate.6.meta.refs_6_
  2.8 5.8 %copy-done = f32[4096,1024]{1,0:T(8,128)S(1)} copy-done((f32[4096,1024]{1,0:T(8,128)S(1)}, f32[4096,1024]{1,0:T(8,128)}, u32[]{:S(2)}) %copy-start) | copy-done | bytes 16777240
  8.6 0.7 copy-done.2
  9.3 1.2 pick.1
  10.5 0.6 collective-permute-start
  11.1 1.6 collective-permute-start.1
  12.6 14.6 %collective-permute-done.1 = f32[10,128,128]{2,1,0:T(8,128)S(1)} collective-permute-done((f32[10,128,128]{2,1,0:T(8,128)S(1)}, f32[10,128,128]{2,1,0:T(8,128)S(1)}, u32[]{:S(2)}, u32[]{:S(2)}) %collective-permute-start.1) | collective-permute-done | bytes 655392 | tf_op jit(solution)/shard_map/ppermute | solution.py:30
  27.3 0.8 copy-done.12
  28.1 2.6 collective-permute-start.2
  30.7 0.6 fusion.3
  31.3 1.3 slice.33
  34.6 23.4 %collective-permute-done.other = f32[512,1024]{1,0:T(8,128)} collective-permute-done((f32[512,1024]{1,0:T(8,128)S(1)}, f32[512,1024]{1,0:T(8,128)}, u32[]{:S(2)}, u32[]{:S(2)}) %collective-permute-start) | collective-permute-done | bytes 2097184 | tf_op jit(solution)/shard_map/ppermute | solution.py:30
  58.0 1.2 slice.32
  60.6 0.6 collective-permute-start.6
  61.2 4.8 %dynamic-slice_bitcast_fusion = f32[8,128,1024]{2,1,0:T(8,128)} fusion(f32[8,2,2,128,1024]{4,3,2,1,0:T(8,128)} %bitcast.23, s32[]{:T(128)S(6)} %select_n.52, s32[]{:T(128)S(6)} %select_n.53), kind=kLoop, calls=%fused_computation.1 | loop fusion | bytes 8388616 | tf_op jit(solution)/shard_map/reshape | solution.py:476
  66.0 1.5 collective-permute-start.10
  67.5 0.5 slice.31
  69.3 4.6 %maximum_multiply_fusion.refs_0_ = f32[1024,1024]{1,0:T(8,128)} fusion(f32[512,1024]{1,0:T(8,128)} %collective-permute-done.other, f32[512,1024]{1,0:T(8,128)S(1)} %bitcast.31, f32[]{:T(128)} %bitcast.6), kind=kLoop, calls=%fused_computation | loop fusion | flops 2097152 | bytes 8388612 | tf_op jit(solution)/shard_map/mul | solution.py:424
  73.9 2.7 collective-permute-start.9
  76.5 1.3 collective-permute-start.3
  77.8 4.7 %fusion.2 = (f32[1024,512]{1,0:T(8,128)}, f32[1024,512]{1,0:T(8,128)}) fusion(f32[1024,1024]{1,0:T(8,128)} %maximum_multiply_fusion.refs_0_), kind=kLoop, calls=%fused_computation.9 | loop fusion | bytes 8388608 | tf_op jit(solution)/shard_map/split | solution.py:430
  82.5 2.0 collective-permute-start.7
  84.5 2.1 collective-permute-start.4
  86.6 58.9 %factor_pivots.1 = (f32[512,512]{1,0:T(8,128)S(1)}, f32[512,512]{1,0:T(8,128)S(1)}, f32[512,512]{1,0:T(8,128)S(1)}) custom-call(f32[10,128,128]{2,1,0:T(8,128)S(1)} %add.39.blocks), custom_call_target="tpu_custom_call" | custom-call | flops 67849998336 | bytes 217710000 | tf_op jit(solution)/shard_map/factor_pivots/pallas_call | solution.py:438
  145.5 1.0 copy-done.6
  146.5 1.0 copy-done.8
  147.5 0.6 slice.29
  149.9 3.2 %dynamic-slice_bitcast_fusion.2.refs_1_ = f32[4,128,1024]{2,1,0:T(8,128)} fusion(f32[8,2,2,128,1024]{4,3,2,1,0:T(8,128)} %bitcast.24, s32[]{:T(128)S(6)} %select_n.56, s32[]{:T(128)S(6)} %select_n.53), kind=kLoop, calls=%fused_computation.3 | loop fusion | bytes 4194312 | tf_op jit(solution)/shard_map/reshape | solution.py:476
  153.0 0.6 pause.1
  153.6 1.2 slice.30
  156.1 3.2 %dynamic-slice_bitcast_fusion.1 = f32[4,128,1024]{2,1,0:T(8,128)} fusion(f32[8,2,2,128,1024]{4,3,2,1,0:T(8,128)} %bitcast.25, s32[]{:T(128)S(6)} %select_n.57, s32[]{:T(128)S(6)} %select_n.53), kind=kLoop, calls=%fused_computation.2 | loop fusion | bytes 4194312 | tf_op jit(solution)/shard_map/reshape | solution.py:476
  159.3 12.7 %collective-permute-done.3.refs_1_.refs_0_ = f32[1024,1024]{1,0:T(8,128)} collective-permute-done((f32[1024,1024]{1,0:T(8,128)}, f32[1024,1024]{1,0:T(8,128)}, u32[]{:S(2)}, u32[]{:S(2)}) %collective-permute-start.3) | collective-permute-done | bytes 4194336 | tf_op jit(solution)/shard_map/ppermute | solution.py:433
  172.0 2.6 collective-permute-start.11
  174.6 4.7 %fusion.1 = (f32[1024,512]{1,0:T(8,128)}, f32[1024,512]{1,0:T(8,128)}) fusion(f32[1024,1024]{1,0:T(8,128)} %collective-permute-done.3.refs_1_.refs_0_), kind=kLoop, calls=%fused_computation.8 | loop fusion | bytes 8388608 | tf_op jit(solution)/shard_map/split | solution.py:430
  179.2 1.3 collective-permute-start.8
  180.5 1.6 collective-permute-start.5
  182.2 10.9 %factor_at_columns.1.refs_3_ = bf16[1536,2048]{1,0:T(8,128)(2,1)} custom-call(s32[74]{0:T(128)S(1)} %concatenate.6.meta.refs_6_, f32[512,1024]{1,0:T(8,128)S(1)} %bitcast.32, f32[512,1024]{1,0:T(8,128)} %collective-permute-done.other, f32[512,512]{1,0:T(8,128)S(1)} %copy-done.5, f32[1024,1024]{1,0:T(8,128)} %collective-permute-done.3.refs_1_.refs_0_, ...), custom_call_target="tpu_custom_call" | custom-call | flops 11500000256 | bytes 36900000 | tf_op jit(solution)/shard_map/factor_at_columns/pallas_call | solution.py:485
  193.2 14.2 %factor_rows.3 = (f32[2,8,2,128,128]{4,3,2,1,0:T(8,128)}, bf16[2,8,128,1536]{3,2,1,0:T(8,128)(2,1)}) custom-call(s32[74]{0:T(128)S(1)} %concatenate.6.meta.refs_6_, f32[1024,1024]{1,0:T(8,128)} %maximum_multiply_fusion.refs_0_, f32[1024,1024]{1,0:T(8,128)} %collective-permute-done.3.refs_1_.refs_0_, f32[1024,1024]{1,0:T(8,128)} %collective-permute-done.9.refs_2_.refs_1_, ...), custom_call_target="tpu_custom_call" | custom-call | flops 13799999488 | bytes 44280000 | tf_op jit(solution)/shard_map/factor_rows/pallas_call | solution.py:545
  207.4 2.8 copy-done.11
  210.2 20.2 %update_tile.3 = (f32[2,8,2,128,2048]{4,3,2,1,0:T(8,128)}, f32[8,128]{1,0:T(8,128)S(1)}) custom-call(s32[74]{0:T(128)S(1)} %concatenate.6.meta.refs_6_, f32[8,2,2,128,1024]{4,3,2,1,0:T(8,128)} %bitcast.26, f32[8,128,1024]{2,1,0:T(8,128)} %collective-permute-done.10.refs_2_.refs_1_, bf16[2,8,128,1536]{3,2,1,0:T(8,128)(2,1)S(1)} %copy-done.11, ...), custom_call_target="tpu_custom_call" | custom-call | flops 27599998976 | bytes 88560000 | tf_op jit(solution)/shard_map/update_tile/pallas_call | solution.py:599
  230.4 1.3 collective-permute-start.12
  231.7 8.3 %factor_rows.4 = (f32[2,8,2,128,128]{4,3,2,1,0:T(8,128)}, bf16[2,4,128,1536]{3,2,1,0:T(8,128)(2,1)S(1)}) custom-call(s32[74]{0:T(128)S(1)} %concatenate.6.meta.refs_6_, f32[1024,1024]{1,0:T(8,128)} %collective-permute-done.3.refs_1_.refs_0_, f32[1024,512]{1,0:T(8,128)} %collective-permute-done.7.refs_1_, ...), custom_call_target="tpu_custom_call", output_to_operand_aliasing={{0}: (6, {})} | custom-call | flops 6899999744 | bytes 22140000 | tf_op jit(solution)/shard_map/factor_rows/pallas_call | solution.py:545
  240.1 11.6 %update_tile.4 = (f32[2,8,2,128,2048]{4,3,2,1,0:T(8,128)}, f32[8,128]{1,0:T(8,128)S(1)}) custom-call(s32[74]{0:T(128)S(1)} %concatenate.6.meta.refs_6_, f32[8,2,2,128,1024]{4,3,2,1,0:T(8,128)} %bitcast.27, f32[4,128,1024]{2,1,0:T(8,128)} %collective-permute-done.11.refs_1_, ...), custom_call_target="tpu_custom_call", output_to_operand_aliasing={{0}: (6, {})} | custom-call | flops 13799999488 | bytes 44280000 | tf_op jit(solution)/shard_map/update_tile/pallas_call | solution.py:599
  251.7 17.1 %collective-permute-done.5.refs_2_ = f32[1024,512]{1,0:T(8,128)} collective-permute-done((f32[1024,512]{1,0:T(8,128)}, f32[1024,512]{1,0:T(8,128)}, u32[]{:S(2)}, u32[]{:S(2)}) %collective-permute-start.5) | collective-permute-done | bytes 2097184 | tf_op jit(solution)/shard_map/ppermute | solution.py:433
  268.8 8.6 %factor_rows.5 = (f32[2,8,2,128,128]{4,3,2,1,0:T(8,128)}, bf16[2,4,128,1536]{3,2,1,0:T(8,128)(2,1)S(1)}) custom-call(s32[74]{0:T(128)S(1)} %concatenate.6.meta.refs_6_, f32[1024,1024]{1,0:T(8,128)} %collective-permute-done.3.refs_1_.refs_0_, f32[1024,512]{1,0:T(8,128)} %collective-permute-done.4.refs_1_, ...), custom_call_target="tpu_custom_call", output_to_operand_aliasing={{0}: (6, {})} | custom-call | flops 6899999744 | bytes 22140000 | tf_op jit(solution)/shard_map/factor_rows/pallas_call | solution.py:545
  277.4 11.6 %update_tile.5 = (f32[2,8,2,128,2048]{4,3,2,1,0:T(8,128)}, f32[8,128]{1,0:T(8,128)}) custom-call(s32[74]{0:T(128)S(1)} %concatenate.6.meta.refs_6_, f32[8,2,2,128,1024]{4,3,2,1,0:T(8,128)} %bitcast.28, f32[4,128,1024]{2,1,0:T(8,128)} %collective-permute-done.12.refs_1_, ...), custom_call_target="tpu_custom_call", output_to_operand_aliasing={{0}: (6, {})} | custom-call | flops 13799999488 | bytes 44280000 | tf_op jit(solution)/shard_map/update_tile/pallas_call | solution.py:599
  (35 shorter events, 0.3 us)
Async XLA Ops:
  2.8 5.8 %copy-start = (f32[4096,1024]{1,0:T(8,128)S(1)}, f32[4096,1024]{1,0:T(8,128)}, u32[]{:S(2)}) copy-start(f32[4096,1024]{1,0:T(8,128)} %param.6) | copy-start | bytes 50331652
  8.6 0.7 copy-start.2
  9.3 21.4 %copy-start.13 = (s32[2,2,4]{2,1,0:T(2,128)S(1)}, s32[2,2,4]{2,1,0:T(2,128)}, u32[]{:S(2)}) copy-start(s32[2,2,4]{2,1,0:T(2,128)} %constant.48.clone) | copy-start | bytes 196
  10.5 47.5 %collective-permute-start = (f32[512,1024]{1,0:T(8,128)S(1)}, f32[512,1024]{1,0:T(8,128)}, u32[]{:S(2)}, u32[]{:S(2)}) collective-permute-start(f32[512,1024]{1,0:T(8,128)S(1)} %bitcast.30), channel_id=1, source_target_pairs={{0,4},{4,0},{1,5},{5,1},{2,6},{6,2},{3,7},{7,3},{8,12},{12,8},{9,1... | collective-permute-start | bytes 6291464 | tf_op jit(solution)/shard_map/ppermute | solution.py:30
  11.1 16.2 %collective-permute-start.1 = (f32[10,128,128]{2,1,0:T(8,128)S(1)}, f32[10,128,128]{2,1,0:T(8,128)S(1)}, u32[]{:S(2)}, u32[]{:S(2)}) collective-permute-start(f32[10,128,128]{2,1,0:T(8,128)S(1)} %get-tuple-element.19), channel_id=1, source_target_pairs={{0,1},{1,0},{2,3},{3,2},{4,5},{5,4},{6,7},{7,6},{8,9},{9,8},{10,11... | collective-permute-start | bytes 1966088 | tf_op jit(solution)/shard_map/ppermute | solution.py:30
  27.2 0.8 copy-start.12
  28.1 32.4 %collective-permute-start.2 = (f32[10,128,128]{2,1,0:T(8,128)S(1)}, f32[10,128,128]{2,1,0:T(8,128)S(1)}, u32[]{:S(2)}, u32[]{:S(2)}) collective-permute-start(f32[10,128,128]{2,1,0:T(8,128)S(1)} %add.37), channel_id=1, source_target_pairs={{0,2},{1,3},{2,0},{3,1},{4,6},{5,7},{6,4},{7,5},{8,10},{9,11},{10,... | collective-permute-start | bytes 1966088 | tf_op jit(solution)/shard_map/ppermute | solution.py:30
  60.6 23.9 %collective-permute-start.6 = (f32[10,128,128]{2,1,0:T(8,128)S(1)}, f32[10,128,128]{2,1,0:T(8,128)S(1)}, u32[]{:S(2)}, u32[]{:S(2)}) collective-permute-start(f32[10,128,128]{2,1,0:T(8,128)S(1)} %add_multiply_fusion), channel_id=1, source_target_pairs={{0,4},{4,0},{1,5},{5,1},{2,6},{6,2},{3,7},{7,3},{8,12},{12,8},{9,1... | collective-permute-start | bytes 1966088 | tf_op jit(solution)/shard_map/ppermute | solution.py:30
  66.0 113.3 %collective-permute-start.10 = (f32[8,128,1024]{2,1,0:T(8,128)}, f32[8,128,1024]{2,1,0:T(8,128)}, u32[]{:S(2)}, u32[]{:S(2)}) collective-permute-start(f32[8,128,1024]{2,1,0:T(8,128)} %dynamic-slice_bitcast_fusion), channel_id=1, source_target_pairs={{0,4},{4,0},{1,5},{5,1},{2,6},{6,2},{3,7},{7,3},{8,12},{12,8},{9,1... | collective-permute-start | bytes 12582920 | tf_op jit(solution)/shard_map/ppermute | solution.py:30
  73.9 106.6 %collective-permute-start.9 = (f32[1024,1024]{1,0:T(8,128)}, f32[1024,1024]{1,0:T(8,128)}, u32[]{:S(2)}, u32[]{:S(2)}) collective-permute-start(f32[1024,1024]{1,0:T(8,128)} %maximum_multiply_fusion.refs_0_), channel_id=1, source_target_pairs={{2,1},{5,6},{10,9},{13,14},{18,17},{21,22},{26,25},{29,30}} | collective-permute-start | bytes 12582920 | tf_op jit(solution)/shard_map/ppermute | solution.py:433
  76.5 95.5 %collective-permute-start.3 = (f32[1024,1024]{1,0:T(8,128)}, f32[1024,1024]{1,0:T(8,128)}, u32[]{:S(2)}, u32[]{:S(2)}) collective-permute-start(f32[1024,1024]{1,0:T(8,128)} %maximum_multiply_fusion.refs_0_), channel_id=1, source_target_pairs={{2,3},{0,2},{5,4},{7,5},{10,11},{8,10},{13,12},{15,13},{18,19},{16... | collective-permute-start | bytes 12582920 | tf_op jit(solution)/shard_map/ppermute | solution.py:433
  82.5 147.9 %collective-permute-start.7 = (f32[1024,512]{1,0:T(8,128)}, f32[1024,512]{1,0:T(8,128)}, u32[]{:S(2)}, u32[]{:S(2)}) collective-permute-start(f32[1024,512]{1,0:T(8,128)} %get-tuple-element.36), channel_id=1, source_target_pairs={{2,0},{0,1},{5,7},{7,6},{10,8},{8,9},{13,15},{15,14},{18,16},{16,1... | collective-permute-start | bytes 6291464 | tf_op jit(solution)/shard_map/ppermute | solution.py:433
  84.5 167.2 %collective-permute-start.4 = (f32[1024,512]{1,0:T(8,128)}, f32[1024,512]{1,0:T(8,128)}, u32[]{:S(2)}, u32[]{:S(2)}) collective-permute-start(f32[1024,512]{1,0:T(8,128)} %get-tuple-element.37), channel_id=1, source_target_pairs={{2,0},{0,1},{5,7},{7,6},{10,8},{8,9},{13,15},{15,14},{18,16},{16,1... | collective-permute-start | bytes 6291464 | tf_op jit(solution)/shard_map/ppermute | solution.py:433
  145.5 1.0 copy-start.6
  146.5 1.0 copy-start.8
  147.5 5.6 %copy-start.4 = (f32[512,512]{1,0:T(8,128)}, f32[512,512]{1,0:T(8,128)S(1)}, u32[]{:S(2)}) copy-start(f32[512,512]{1,0:T(8,128)S(1)} %get-tuple-element.24.inverse.refs_0_) | copy-start | bytes 3145732
  159.3 22.8 %copy-start.5 = (f32[512,512]{1,0:T(8,128)S(1)}, f32[512,512]{1,0:T(8,128)}, u32[]{:S(2)}) copy-start(f32[512,512]{1,0:T(8,128)} %copy-done.4) | copy-start | bytes 3145732
  172.0 68.1 %collective-permute-start.11 = (f32[4,128,1024]{2,1,0:T(8,128)}, f32[4,128,1024]{2,1,0:T(8,128)}, u32[]{:S(2)}, u32[]{:S(2)}) collective-permute-start(f32[4,128,1024]{2,1,0:T(8,128)} %dynamic-slice_bitcast_fusion.2.refs_1_), channel_id=1, source_target_pairs={{0,4},{4,0},{1,5},{5,1},{2,6},{6,2},{3,7},{7,3},{8,12},{12,8},{9,1... | collective-permute-start | bytes 6291464 | tf_op jit(solution)/shard_map/ppermute | solution.py:30
  179.2 52.5 %collective-permute-start.8 = (f32[1024,512]{1,0:T(8,128)}, f32[1024,512]{1,0:T(8,128)}, u32[]{:S(2)}, u32[]{:S(2)}) collective-permute-start(f32[1024,512]{1,0:T(8,128)} %get-tuple-element.34), channel_id=1, source_target_pairs={{2,3},{5,4},{10,11},{13,12},{18,19},{21,20},{26,27},{29,28}} | collective-permute-start | bytes 6291464 | tf_op jit(solution)/shard_map/ppermute | solution.py:433
  180.5 12.6 %copy-start.7 = (f32[512,512]{1,0:T(8,128)S(1)}, f32[512,512]{1,0:T(8,128)}, u32[]{:S(2)}) copy-start(f32[512,512]{1,0:T(8,128)} %copy-done.6) | copy-start | bytes 3145732
  180.5 12.6 %copy-start.9 = (f32[512,512]{1,0:T(8,128)S(1)}, f32[512,512]{1,0:T(8,128)}, u32[]{:S(2)}) copy-start(f32[512,512]{1,0:T(8,128)} %copy-done.8) | copy-start | bytes 3145732
  180.5 88.3 %collective-permute-start.5 = (f32[1024,512]{1,0:T(8,128)}, f32[1024,512]{1,0:T(8,128)}, u32[]{:S(2)}, u32[]{:S(2)}) collective-permute-start(f32[1024,512]{1,0:T(8,128)} %get-tuple-element.35), channel_id=1, source_target_pairs={{2,3},{5,4},{10,11},{13,12},{18,19},{21,20},{26,27},{29,28}} | collective-permute-start | bytes 6291464 | tf_op jit(solution)/shard_map/ppermute | solution.py:433
  193.2 14.3 %copy-start.1 = (bf16[1536,2048]{1,0:T(8,128)(2,1)S(1)}, bf16[1536,2048]{1,0:T(8,128)(2,1)}, u32[]{:S(2)}) copy-start(bf16[1536,2048]{1,0:T(8,128)(2,1)} %factor_at_columns.1.refs_3_) | copy-start | bytes 18874372
  193.2 14.2 %copy-start.3 = (f32[4096]{0:T(1024)S(1)}, f32[4096]{0:T(1024)}, u32[]{:S(2)}) copy-start(f32[4096]{0:T(1024)} %param.7) | copy-start | bytes 49156
  207.4 2.8 copy-start.11
  210.2 21.5 %copy-start.10 = (f32[512,512]{1,0:T(8,128)S(1)}, f32[512,512]{1,0:T(8,128)}, u32[]{:S(2)}) copy-start(f32[512,512]{1,0:T(8,128)} %copy-done.8) | copy-start | bytes 3145732
  230.4 47.0 %collective-permute-start.12 = (f32[4,128,1024]{2,1,0:T(8,128)}, f32[4,128,1024]{2,1,0:T(8,128)}, u32[]{:S(2)}, u32[]{:S(2)}) collective-permute-start(f32[4,128,1024]{2,1,0:T(8,128)} %dynamic-slice_bitcast_fusion.1), channel_id=1, source_target_pairs={{0,4},{4,0},{1,5},{5,1},{2,6},{6,2},{3,7},{7,3},{8,12},{12,8},{9,1... | collective-permute-start | bytes 6291464 | tf_op jit(solution)/shard_map/ppermute | solution.py:30

commit v6 on v5

--- a/solution.py
+++ b/solution.py
@@ -17,6 +17,7 @@
 MAGNET = 50
 G5 = 0
 G6 = 0
+PIECES = 1
 BOTH = 0
 CHUNKS = (4, 4)
 ROWS_AT_ONCE = 2
@@ -279,7 +280,7 @@
     token[...] = jnp.zeros_like(token)
     r, q = info.row(meta), info.col(meta)
     mine = r // (rows // 2)
-    step, v = pl.program_id(0), pl.program_id(1)
+    v, step = pl.program_id(0), pl.program_id(1)
     left_rows = left[...].reshape(2 * ROWS_AT_ONCE * BLK, left.shape[-1])
 
     def takes(block, front_block):
@@ -295,8 +296,8 @@
         for j in range(ROWS_AT_ONCE)
     }
     for start in range(0, child_slots, width):
-        at = pl.multiple_of((v * child_slots + start) * BLK, BLK)
-        change = jnp.dot(left_rows, right[:, pl.ds(at, width * BLK)], preferred_element_type=jnp.float32)
+        lanes = slice(start * BLK, (start + width) * BLK)
+        change = jnp.dot(left_rows, right[:, lanes], preferred_element_type=jnp.float32)
         for i in range(width):
             block = (start + i) * cols + q
             col_takes = takes(block, block + v * info.child_blocks)
@@ -394,7 +395,7 @@
             shape((pivot_count, BLK, child_width), f32),
             shape((lower_count, BLK, BLK), f32),
         ],
-        compiler_params=params(1),
+        compiler_params=params(1, 60),
         name="pick",
         cost_estimate=about(5),
     )(meta, contrib.reshape(child_rows, BLK, child_width), front_diag.reshape(row_slots, 1, BLK))
@@ -512,8 +513,12 @@
     row_parts = [[] for _ in counts]
 
     order_of_work = [("rows", 0, 0), ("rows", 1, 0), ("tile", 0)]
-    chunks_of = [[(first, part) for at_turn, first, part in received if at_turn == turn] for turn in range(sources)]
-    order_of_work = [("rows", 0, 0), ("rows", 1, 0), ("tile", 0, 0)] if G6 else [("rows", 0, 0), ("tile", 0, 0), ("rows", 1, 0)]
+    chunks_of = [[] for _ in range(sources)]
+    for turn, first, part in received:
+        pieces = PIECES if turn == 0 and part.shape[0] % (PIECES * ROWS_AT_ONCE) == 0 else 1
+        count = part.shape[0] // pieces
+        chunks_of[turn] += [(first + n * count, part, n * count, count) for n in range(pieces)]
+    order_of_work = [("rows", 0, 0)] + [("tile", 0, n) for n in range(len(chunks_of[0]))] + [("rows", 1, 0)]
     for turn in range(1, sources):
         ahead = len(chunks_of[turn]) // 2 if counts[turn] == 2 and ORDER else 0
         order_of_work += [("tile", turn, n) for n in range(ahead)]
@@ -569,7 +574,7 @@
             row_parts[turn].append(row_part)
             continue
 
-        for first, part in [chunks_of[turn][rest[0]]]:
+        for first, part, offset, count in [chunks_of[turn][rest[0]]]:
             at = first // ROWS_AT_ONCE
             row_part = row_parts[turn][first * parts_count // child_slots]
             left_at = at % (child_slots // parts_count // ROWS_AT_ONCE)
@@ -577,14 +582,14 @@
             in_specs = [
                 pl.BlockSpec(
                     (ROWS_AT_ONCE, 1, 1, BLK, child_width),
-                    lambda t, v, m, at=at, source_of=source_of: (at + t, source_of(m), mine_of(m), 0, 0),
+                    lambda v, t, m, at=at, source_of=source_of: (at + t, source_of(m), mine_of(m), 0, 0),
                 ),
-                pl.BlockSpec((ROWS_AT_ONCE, BLK, child_width), lambda t, v, m: (t, 0, 0)),
-                pl.BlockSpec((2, ROWS_AT_ONCE, BLK, 3 * depth), lambda t, v, m, at=left_at: (0, at + t, 0, 0)),
-                pl.BlockSpec((3 * depth, tile_cols), whole),
+                pl.BlockSpec((ROWS_AT_ONCE, BLK, child_width), lambda v, t, m, at=offset // ROWS_AT_ONCE: (at + t, 0, 0)),
+                pl.BlockSpec((2, ROWS_AT_ONCE, BLK, 3 * depth), lambda v, t, m, at=left_at: (0, at + t, 0, 0)),
+                pl.BlockSpec((3 * depth, child_width), lambda v, t, m: (0, v)),
                 pl.BlockSpec(
                     (2, ROWS_AT_ONCE, 1, 1, BLK),
-                    lambda t, v, m, at=at, source_of=source_of: (0, at + t, source_of(m), 0, 0),
+                    lambda v, t, m, at=at, source_of=source_of: (0, at + t, source_of(m), 0, 0),
                 ),
             ]
             operands = [own_view, part, row_part, col_parts, diag_view]
@@ -600,21 +605,21 @@
                 functools.partial(update_kernel, info, rows, cols, child_slots, width, turn, first),
                 grid_spec=pltpu.PrefetchScalarGridSpec(
                     num_scalar_prefetch=1,
-                    grid=(part.shape[0] // ROWS_AT_ONCE, 2),
+                    grid=(2, count // ROWS_AT_ONCE),
                     in_specs=in_specs,
                     out_specs=[
                         pl.BlockSpec(
                             (2, ROWS_AT_ONCE, 1, BLK, child_width),
-                            lambda t, v, m, at=at, source_of=source_of: (0, at + t, source_of(m), 0, v),
+                            lambda v, t, m, at=at, source_of=source_of: (0, at + t, source_of(m), 0, v),
                         ),
-                        pl.BlockSpec((8, BLK), lambda t, v, m: (0, 0)),
+                        pl.BlockSpec((8, BLK), lambda v, t, m: (0, 0)),
                     ],
                 ),
                 out_shape=[shape((2, child_slots, sources, BLK, tile_cols), f32), shape((8, BLK), f32)],
                 input_output_aliases=aliases,
                 compiler_params=params(2, 36),
                 name="update_tile",
-                cost_estimate=about(3.0 * part.shape[0] * (LATE if turn else 1.0)),
+                cost_estimate=about(3.0 * count * (LATE if turn else 1.0)),
             )(meta, *operands)
     factor = factor.reshape(local_rows, BLK)
     if share < BLK:

time: 290 us -> 285 us (0.983)
  local copies, waits for them, and re-layouts: 40 us -> 33 us
  Pallas kernels: 146 us -> 149 us
    unnamed x28 -> x34, local copies, waits for them, and re-layouts: 12 us -> 5.61 us
    pallas_call x1, Pallas kernels: 1.17 us -> 5.01 us  [per_device(): pl.pallas_call(functools.partial(pick_kernel, info, rows, cols), grid_spe...]
  transfers between devices with their start and end apart: 13 -> 13, of which waited for: 4 -> 4; matrix products, arithmetic and copies ran while one was open for 11% -> 10% of each run, Pallas kernels for 46% -> 47%
where the time goes in v6:
time: 285 us; the launch traced here: 284 us
  Pallas kernels  149 us (52%)
  waiting for transfers between devices  68 us (24%)
  local copies, waits for them, and re-layouts  33 us (12%)
  starting transfers between devices  21.6 us (8%)
  between operations  8.26 us (3%)
  other arithmetic  3.74 us (1%)
    pallas_call x1, Pallas kernels, per_device(): pl.pallas_call(functools.partial(cholesky_kernel, pivot_count), out_shape...  58.9 us
    pallas_call x3, Pallas kernels, per_device(): pl.pallas_call(functools.partial(update_kernel, info, rows, cols, child_s...  43.8 us
    ppermute x7, waiting for transfers between devices, swapped(): lax.ppermute(shard, axis, [(i, i ^ 1 << bit) for i in range(lax.axis_size...  37.1 us
    pallas_call x3, Pallas kernels, per_device(): pl.pallas_call(functools.partial(rows_kernel, info, rows, cols, few, shar...  31.2 us
    ppermute x6, waiting for transfers between devices, per_device(): held.append([lax.ppermute(part, ('row', 'col'), pairs) for part in sent])  31 us
    reshape x3, local copies, waits for them, and re-layouts, per_device(): part = lax.dynamic_slice(own_view, (first, partner_turns[turn] * start, 1...  11.3 us
    ppermute x6, starting transfers between devices, per_device(): held.append([lax.ppermute(part, ('row', 'col'), pairs) for part in sent])  10.9 us
    ppermute x7, starting transfers between devices, swapped(): lax.ppermute(shard, axis, [(i, i ^ 1 << bit) for i in range(lax.axis_size...  10.8 us
  transfers between devices with their start and end apart: 13, of which 4 were waited for; matrix products, arithmetic and copies ran while one was open for 10% of the time, Pallas kernels for 47%

profile of v6, /device:TPU:6, one launch (start us, length us, event | category | flops | bytes accessed | tf_op | source)
XLA Modules:
  0.0 284.2 jit_solution(9455573287065483225)
XLA Ops:
  0.6 0.8 reshape.61
  1.4 0.7 fusion
  2.1 1.3 concatenate.6.meta.refs_6_
  3.4 5.0 %pick.1 = (f32[4,128,1024]{2,1,0:T(8,128)}, f32[10,128,128]{2,1,0:T(8,128)}) custom-call(s32[74]{0:T(128)} %concatenate.6.meta.refs_6_, f32[32,128,1024]{2,1,0:T(8,128)} %bitcast.31, f32[32,1,128]{2,1,0:T(1,128)} %bitcast.26), custom_call_target="tpu_custom_call" | custom-call | flops 5750000128 | bytes 18450000 | tf_op jit(solution)/shard_map/pick/pallas_call | solution.py:378
  8.4 0.5 collective-permute-start
  8.9 1.6 collective-permute-start.1
  10.5 14.8 %collective-permute-done.1 = f32[10,128,128]{2,1,0:T(8,128)S(1)} collective-permute-done((f32[10,128,128]{2,1,0:T(8,128)}, f32[10,128,128]{2,1,0:T(8,128)S(1)}, u32[]{:S(2)}, u32[]{:S(2)}) %collective-permute-start.1) | collective-permute-done | bytes 655392 | tf_op jit(solution)/shard_map/ppermute | solution.py:31
  25.3 0.9 copy-done.15
  26.2 1.2 add.37
  27.3 2.7 collective-permute-start.2
  30.0 0.6 fusion.3
  30.6 1.2 slice.33
  33.7 22.3 %collective-permute-done.other = f32[512,1024]{1,0:T(8,128)S(1)} collective-permute-done((f32[512,1024]{1,0:T(8,128)}, f32[512,1024]{1,0:T(8,128)S(1)}, u32[]{:S(2)}, u32[]{:S(2)}) %collective-permute-start) | collective-permute-done | bytes 2097184 | tf_op jit(solution)/shard_map/ppermute | solution.py:31
  56.0 0.5 slice.32
  57.8 0.1 add_multiply_fusion
  57.9 1.3 collective-permute-start.6
  59.2 4.9 %dynamic-slice_bitcast_fusion = f32[8,128,1024]{2,1,0:T(8,128)} fusion(f32[8,2,2,128,1024]{4,3,2,1,0:T(8,128)} %bitcast.32, s32[]{:T(128)S(6)} %select_n.52, s32[]{:T(128)S(6)} %select_n.53), kind=kLoop, calls=%fused_computation.1 | loop fusion | bytes 8388616 | tf_op jit(solution)/shard_map/reshape | solution.py:477
  64.2 0.8 collective-permute-start.10
  65.0 0.5 slice.31
  66.7 2.4 maximum_multiply_fusion.refs_0_
  69.1 2.7 collective-permute-start.9
  71.7 1.3 collective-permute-start.3
  73.0 4.7 %fusion.2 = (f32[1024,512]{1,0:T(8,128)}, f32[1024,512]{1,0:T(8,128)}) fusion(f32[1024,1024]{1,0:T(8,128)} %maximum_multiply_fusion.refs_0_), kind=kLoop, calls=%fused_computation.9 | loop fusion | bytes 8388608 | tf_op jit(solution)/shard_map/split | solution.py:431
  77.7 2.0 collective-permute-start.7
  79.7 2.1 collective-permute-start.4
  81.8 58.9 %factor_pivots.1 = (f32[512,512]{1,0:T(8,128)S(1)}, f32[512,512]{1,0:T(8,128)S(1)}, f32[512,512]{1,0:T(8,128)S(1)}) custom-call(f32[10,128,128]{2,1,0:T(8,128)S(1)} %add.39.blocks), custom_call_target="tpu_custom_call" | custom-call | flops 67849998336 | bytes 217710000 | tf_op jit(solution)/shard_map/factor_pivots/pallas_call | solution.py:439
  140.8 1.0 copy-done.9
  141.7 1.0 copy-done.11
  142.7 0.6 slice.29
  145.0 3.2 %dynamic-slice_bitcast_fusion.2.refs_1_ = f32[4,128,1024]{2,1,0:T(8,128)} fusion(f32[8,2,2,128,1024]{4,3,2,1,0:T(8,128)} %bitcast.33, s32[]{:T(128)S(6)} %select_n.56, s32[]{:T(128)S(6)} %select_n.53), kind=kLoop, calls=%fused_computation.3 | loop fusion | bytes 4194312 | tf_op jit(solution)/shard_map/reshape | solution.py:477
  148.2 0.6 pause.1
  148.8 1.2 slice.30
  151.2 3.2 %dynamic-slice_bitcast_fusion.1 = f32[4,128,1024]{2,1,0:T(8,128)} fusion(f32[8,2,2,128,1024]{4,3,2,1,0:T(8,128)} %bitcast.34, s32[]{:T(128)S(6)} %select_n.57, s32[]{:T(128)S(6)} %select_n.53), kind=kLoop, calls=%fused_computation.2 | loop fusion | bytes 4194312 | tf_op jit(solution)/shard_map/reshape | solution.py:477
  154.4 12.7 %collective-permute-done.3.refs_1_.refs_0_ = f32[1024,1024]{1,0:T(8,128)} collective-permute-done((f32[1024,1024]{1,0:T(8,128)}, f32[1024,1024]{1,0:T(8,128)}, u32[]{:S(2)}, u32[]{:S(2)}) %collective-permute-start.3) | collective-permute-done | bytes 4194336 | tf_op jit(solution)/shard_map/ppermute | solution.py:434
  167.1 2.6 collective-permute-start.11
  169.8 4.0 %fusion.1 = (f32[1024,512]{1,0:T(8,128)S(1)}, f32[1024,512]{1,0:T(8,128)}) fusion(f32[1024,1024]{1,0:T(8,128)} %collective-permute-done.3.refs_1_.refs_0_), kind=kLoop, calls=%fused_computation.8 | loop fusion | bytes 8388608 | tf_op jit(solution)/shard_map/split | solution.py:431
  173.7 1.3 collective-permute-start.8
  175.1 1.6 collective-permute-start.5
  176.7 10.1 %factor_at_columns.1.refs_3_ = bf16[1536,2048]{1,0:T(8,128)(2,1)} custom-call(s32[74]{0:T(128)S(1)} %copy-done.6, f32[512,1024]{1,0:T(8,128)S(1)} %bitcast.25, f32[512,1024]{1,0:T(8,128)S(1)} %copy-done.4, f32[512,512]{1,0:T(8,128)S(1)} %copy-done.8, f32[1024,1024]{1,0:T(8,128)} %collective-permute-done.3.refs_1_.refs_0_, ...), custom_call_target="tpu_custom_call" | custom-call | flops 11500000256 | bytes 36900000 | tf_op jit(solution)/shard_map/factor_at_columns/pallas_call | solution.py:486
  186.8 14.2 %factor_rows.3 = (f32[2,8,2,128,128]{4,3,2,1,0:T(8,128)}, bf16[2,8,128,1536]{3,2,1,0:T(8,128)(2,1)}) custom-call(s32[74]{0:T(128)S(1)} %copy-done.6, f32[1024,1024]{1,0:T(8,128)} %maximum_multiply_fusion.refs_0_, f32[1024,1024]{1,0:T(8,128)} %collective-permute-done.3.refs_1_.refs_0_, f32[1024,1024]{1,0:T(8,128)} %collective-permute-done.9.refs_2_.refs_1_, ...), custom_call_target="tpu_custom_call" | custom-call | flops 13799999488 | bytes 44280000 | tf_op jit(solution)/shard_map/factor_rows/pallas_call | solution.py:550
  201.1 2.8 copy-done.14
  203.9 20.3 %update_tile.3 = (f32[2,8,2,128,2048]{4,3,2,1,0:T(8,128)}, f32[8,128]{1,0:T(8,128)S(1)}) custom-call(s32[74]{0:T(128)S(1)} %copy-done.6, f32[8,2,2,128,1024]{4,3,2,1,0:T(8,128)} %bitcast.35, f32[8,128,1024]{2,1,0:T(8,128)} %collective-permute-done.10.refs_2_.refs_1_, bf16[2,8,128,1536]{3,2,1,0:T(8,128)(2,1)S(1)} %copy-done.14, ...), custom_call_target="tpu_custom_call" | custom-call | flops 27599998976 | bytes 88560000 | tf_op jit(solution)/shard_map/update_tile/pallas_call | solution.py:604
  224.2 1.3 collective-permute-start.12
  225.5 8.4 %factor_rows.4 = (f32[2,8,2,128,128]{4,3,2,1,0:T(8,128)}, bf16[2,4,128,1536]{3,2,1,0:T(8,128)(2,1)S(1)}) custom-call(s32[74]{0:T(128)S(1)} %copy-done.6, f32[1024,1024]{1,0:T(8,128)} %collective-permute-done.3.refs_1_.refs_0_, f32[1024,512]{1,0:T(8,128)} %collective-permute-done.7.refs_1_, ...), custom_call_target="tpu_custom_call", output_to_operand_aliasing={{0}: (6, {})} | custom-call | flops 6899999744 | bytes 22140000 | tf_op jit(solution)/shard_map/factor_rows/pallas_call | solution.py:550
  233.9 11.8 %update_tile.4 = (f32[2,8,2,128,2048]{4,3,2,1,0:T(8,128)}, f32[8,128]{1,0:T(8,128)S(1)}) custom-call(s32[74]{0:T(128)S(1)} %copy-done.6, f32[8,2,2,128,1024]{4,3,2,1,0:T(8,128)} %bitcast.36, f32[4,128,1024]{2,1,0:T(8,128)} %collective-permute-done.11.refs_1_, ...), custom_call_target="tpu_custom_call", output_to_operand_aliasing={{0}: (6, {})} | custom-call | flops 13799999488 | bytes 44280000 | tf_op jit(solution)/shard_map/update_tile/pallas_call | solution.py:604
  245.8 18.2 %collective-permute-done.5.refs_2_ = f32[1024,512]{1,0:T(8,128)} collective-permute-done((f32[1024,512]{1,0:T(8,128)}, f32[1024,512]{1,0:T(8,128)}, u32[]{:S(2)}, u32[]{:S(2)}) %collective-permute-start.5) | collective-permute-done | bytes 2097184 | tf_op jit(solution)/shard_map/ppermute | solution.py:434
  264.0 8.6 %factor_rows.5 = (f32[2,8,2,128,128]{4,3,2,1,0:T(8,128)}, bf16[2,4,128,1536]{3,2,1,0:T(8,128)(2,1)S(1)}) custom-call(s32[74]{0:T(128)S(1)} %copy-done.6, f32[1024,1024]{1,0:T(8,128)} %collective-permute-done.3.refs_1_.refs_0_, f32[1024,512]{1,0:T(8,128)} %collective-permute-done.4.refs_1_, ...), custom_call_target="tpu_custom_call", output_to_operand_aliasing={{0}: (6, {})} | custom-call | flops 6899999744 | bytes 22140000 | tf_op jit(solution)/shard_map/factor_rows/pallas_call | solution.py:550
  272.6 11.6 %update_tile.5 = (f32[2,8,2,128,2048]{4,3,2,1,0:T(8,128)}, f32[8,128]{1,0:T(8,128)}) custom-call(s32[74]{0:T(128)S(1)} %copy-done.6, f32[8,2,2,128,1024]{4,3,2,1,0:T(8,128)} %bitcast.37, f32[4,128,1024]{2,1,0:T(8,128)S(1)} %collective-permute-done.12.refs_1_, ...), custom_call_target="tpu_custom_call", output_to_operand_aliasing={{0}: (6, {})} | custom-call | flops 13799999488 | bytes 44280000 | tf_op jit(solution)/shard_map/update_tile/pallas_call | solution.py:604
  (41 shorter events, 0.2 us)
Async XLA Ops:
  3.4 26.6 %copy-start.16 = (s32[2,2,4]{2,1,0:T(2,128)S(1)}, s32[2,2,4]{2,1,0:T(2,128)}, u32[]{:S(2)}) copy-start(s32[2,2,4]{2,1,0:T(2,128)} %constant.48.clone) | copy-start | bytes 196
  8.4 47.5 %collective-permute-start = (f32[512,1024]{1,0:T(8,128)}, f32[512,1024]{1,0:T(8,128)S(1)}, u32[]{:S(2)}, u32[]{:S(2)}) collective-permute-start(f32[512,1024]{1,0:T(8,128)} %bitcast.23), channel_id=1, source_target_pairs={{0,4},{4,0},{1,5},{5,1},{2,6},{6,2},{3,7},{7,3},{8,12},{12,8},{9,1... | collective-permute-start | bytes 6291464 | tf_op jit(solution)/shard_map/ppermute | solution.py:31
  8.9 16.4 %collective-permute-start.1 = (f32[10,128,128]{2,1,0:T(8,128)}, f32[10,128,128]{2,1,0:T(8,128)S(1)}, u32[]{:S(2)}, u32[]{:S(2)}) collective-permute-start(f32[10,128,128]{2,1,0:T(8,128)} %get-tuple-element.19), channel_id=1, source_target_pairs={{0,1},{1,0},{2,3},{3,2},{4,5},{5,4},{6,7},{7,6},{8,9},{9,8},{10,11... | collective-permute-start | bytes 1966088 | tf_op jit(solution)/shard_map/ppermute | solution.py:31
  25.3 0.9 copy-start.15
  27.3 30.5 %collective-permute-start.2 = (f32[10,128,128]{2,1,0:T(8,128)S(1)}, f32[10,128,128]{2,1,0:T(8,128)S(1)}, u32[]{:S(2)}, u32[]{:S(2)}) collective-permute-start(f32[10,128,128]{2,1,0:T(8,128)S(1)} %add.37), channel_id=1, source_target_pairs={{0,2},{1,3},{2,0},{3,1},{4,6},{5,7},{6,4},{7,5},{8,10},{9,11},{10,... | collective-permute-start | bytes 1966088 | tf_op jit(solution)/shard_map/ppermute | solution.py:31
  56.0 3.3 %copy-start.2 = (f32[512,1024]{1,0:T(8,128)}, f32[512,1024]{1,0:T(8,128)S(1)}, u32[]{:S(2)}) copy-start(f32[512,1024]{1,0:T(8,128)S(1)} %collective-permute-done.other) | copy-start | bytes 6291460
  57.9 21.8 %collective-permute-start.6 = (f32[10,128,128]{2,1,0:T(8,128)S(1)}, f32[10,128,128]{2,1,0:T(8,128)S(1)}, u32[]{:S(2)}, u32[]{:S(2)}) collective-permute-start(f32[10,128,128]{2,1,0:T(8,128)S(1)} %add_multiply_fusion), channel_id=1, source_target_pairs={{0,4},{4,0},{1,5},{5,1},{2,6},{6,2},{3,7},{7,3},{8,12},{12,8},{9,1... | collective-permute-start | bytes 1966088 | tf_op jit(solution)/shard_map/ppermute | solution.py:31
  59.2 7.4 %copy-start.1 = (f32[4,128,1024]{2,1,0:T(8,128)S(1)}, f32[4,128,1024]{2,1,0:T(8,128)}, u32[]{:S(2)}) copy-start(f32[4,128,1024]{2,1,0:T(8,128)} %get-tuple-element.18) | copy-start | bytes 6291460
  59.2 7.4 %copy-start.3 = (f32[512,1024]{1,0:T(8,128)S(1)}, f32[512,1024]{1,0:T(8,128)}, u32[]{:S(2)}) copy-start(f32[512,1024]{1,0:T(8,128)} %copy-done.2) | copy-start | bytes 6291460
  64.2 109.6 %collective-permute-start.10 = (f32[8,128,1024]{2,1,0:T(8,128)}, f32[8,128,1024]{2,1,0:T(8,128)}, u32[]{:S(2)}, u32[]{:S(2)}) collective-permute-start(f32[8,128,1024]{2,1,0:T(8,128)} %dynamic-slice_bitcast_fusion), channel_id=1, source_target_pairs={{0,4},{4,0},{1,5},{5,1},{2,6},{6,2},{3,7},{7,3},{8,12},{12,8},{9,1... | collective-permute-start | bytes 12582920 | tf_op jit(solution)/shard_map/ppermute | solution.py:31
  69.1 106.0 %collective-permute-start.9 = (f32[1024,1024]{1,0:T(8,128)}, f32[1024,1024]{1,0:T(8,128)}, u32[]{:S(2)}, u32[]{:S(2)}) collective-permute-start(f32[1024,1024]{1,0:T(8,128)} %maximum_multiply_fusion.refs_0_), channel_id=1, source_target_pairs={{2,1},{5,6},{10,9},{13,14},{18,17},{21,22},{26,25},{29,30}} | collective-permute-start | bytes 12582920 | tf_op jit(solution)/shard_map/ppermute | solution.py:434
  71.7 95.4 %collective-permute-start.3 = (f32[1024,1024]{1,0:T(8,128)}, f32[1024,1024]{1,0:T(8,128)}, u32[]{:S(2)}, u32[]{:S(2)}) collective-permute-start(f32[1024,1024]{1,0:T(8,128)} %maximum_multiply_fusion.refs_0_), channel_id=1, source_target_pairs={{2,3},{0,2},{5,4},{7,5},{10,11},{8,10},{13,12},{15,13},{18,19},{16... | collective-permute-start | bytes 12582920 | tf_op jit(solution)/shard_map/ppermute | solution.py:434
  77.7 146.4 %collective-permute-start.7 = (f32[1024,512]{1,0:T(8,128)}, f32[1024,512]{1,0:T(8,128)}, u32[]{:S(2)}, u32[]{:S(2)}) collective-permute-start(f32[1024,512]{1,0:T(8,128)} %get-tuple-element.36), channel_id=1, source_target_pairs={{2,0},{0,1},{5,7},{7,6},{10,8},{8,9},{13,15},{15,14},{18,16},{16,1... | collective-permute-start | bytes 6291464 | tf_op jit(solution)/shard_map/ppermute | solution.py:434
  79.7 166.1 %collective-permute-start.4 = (f32[1024,512]{1,0:T(8,128)}, f32[1024,512]{1,0:T(8,128)}, u32[]{:S(2)}, u32[]{:S(2)}) collective-permute-start(f32[1024,512]{1,0:T(8,128)} %get-tuple-element.37), channel_id=1, source_target_pairs={{2,0},{0,1},{5,7},{7,6},{10,8},{8,9},{13,15},{15,14},{18,16},{16,1... | collective-permute-start | bytes 6291464 | tf_op jit(solution)/shard_map/ppermute | solution.py:434
  140.7 1.0 copy-start.9
  141.7 1.0 copy-start.11
  142.7 5.6 %copy-start.7 = (f32[512,512]{1,0:T(8,128)}, f32[512,512]{1,0:T(8,128)S(1)}, u32[]{:S(2)}) copy-start(f32[512,512]{1,0:T(8,128)S(1)} %get-tuple-element.24.inverse.refs_0_) | copy-start | bytes 3145732
  154.4 22.3 %copy-start.4 = (f32[512,1024]{1,0:T(8,128)S(1)}, f32[512,1024]{1,0:T(8,128)}, u32[]{:S(2)}) copy-start(f32[512,1024]{1,0:T(8,128)} %copy-done.2) | copy-start | bytes 6291460
  154.4 22.3 %copy-start.6 = (s32[74]{0:T(128)S(1)}, s32[74]{0:T(128)}, u32[]{:S(2)}) copy-start(s32[74]{0:T(128)} %concatenate.6.meta.refs_6_) | copy-start | bytes 892
  154.4 22.3 %copy-start.8 = (f32[512,512]{1,0:T(8,128)S(1)}, f32[512,512]{1,0:T(8,128)}, u32[]{:S(2)}) copy-start(f32[512,512]{1,0:T(8,128)} %copy-done.7) | copy-start | bytes 3145732
  167.1 66.8 %collective-permute-start.11 = (f32[4,128,1024]{2,1,0:T(8,128)}, f32[4,128,1024]{2,1,0:T(8,128)}, u32[]{:S(2)}, u32[]{:S(2)}) collective-permute-start(f32[4,128,1024]{2,1,0:T(8,128)} %dynamic-slice_bitcast_fusion.2.refs_1_), channel_id=1, source_target_pairs={{0,4},{4,0},{1,5},{5,1},{2,6},{6,2},{3,7},{7,3},{8,12},{12,8},{9,1... | collective-permute-start | bytes 6291464 | tf_op jit(solution)/shard_map/ppermute | solution.py:31
  173.7 51.8 %collective-permute-start.8 = (f32[1024,512]{1,0:T(8,128)S(1)}, f32[1024,512]{1,0:T(8,128)}, u32[]{:S(2)}, u32[]{:S(2)}) collective-permute-start(f32[1024,512]{1,0:T(8,128)S(1)} %get-tuple-element.34), channel_id=1, source_target_pairs={{2,3},{5,4},{10,11},{13,12},{18,19},{21,20},{26,27},{29,28}} | collective-permute-start | bytes 6291464 | tf_op jit(solution)/shard_map/ppermute | solution.py:434
  175.0 11.8 %copy-start.10 = (f32[512,512]{1,0:T(8,128)S(1)}, f32[512,512]{1,0:T(8,128)}, u32[]{:S(2)}) copy-start(f32[512,512]{1,0:T(8,128)} %copy-done.9) | copy-start | bytes 3145732
  175.0 11.8 %copy-start.12 = (f32[512,512]{1,0:T(8,128)S(1)}, f32[512,512]{1,0:T(8,128)}, u32[]{:S(2)}) copy-start(f32[512,512]{1,0:T(8,128)} %copy-done.11) | copy-start | bytes 3145732
  175.1 88.9 %collective-permute-start.5 = (f32[1024,512]{1,0:T(8,128)}, f32[1024,512]{1,0:T(8,128)}, u32[]{:S(2)}, u32[]{:S(2)}) collective-permute-start(f32[1024,512]{1,0:T(8,128)} %get-tuple-element.35), channel_id=1, source_target_pairs={{2,3},{5,4},{10,11},{13,12},{18,19},{21,20},{26,27},{29,28}} | collective-permute-start | bytes 6291464 | tf_op jit(solution)/shard_map/ppermute | solution.py:434
  186.8 14.2 %copy-start = (bf16[1536,2048]{1,0:T(8,128)(2,1)S(1)}, bf16[1536,2048]{1,0:T(8,128)(2,1)}, u32[]{:S(2)}) copy-start(bf16[1536,2048]{1,0:T(8,128)(2,1)} %factor_at_columns.1.refs_3_) | copy-start | bytes 18874372
  186.8 14.2 %copy-start.5 = (f32[4096]{0:T(1024)S(1)}, f32[4096]{0:T(1024)}, u32[]{:S(2)}) copy-start(f32[4096]{0:T(1024)} %param.7) | copy-start | bytes 49156
  201.1 2.8 copy-start.14
  203.9 21.7 %copy-start.13 = (f32[512,512]{1,0:T(8,128)S(1)}, f32[512,512]{1,0:T(8,128)}, u32[]{:S(2)}) copy-start(f32[512,512]{1,0:T(8,128)} %copy-done.11) | copy-start | bytes 3145732
  224.2 48.4 %collective-permute-start.12 = (f32[4,128,1024]{2,1,0:T(8,128)}, f32[4,128,1024]{2,1,0:T(8,128)S(1)}, u32[]{:S(2)}, u32[]{:S(2)}) collective-permute-start(f32[4,128,1024]{2,1,0:T(8,128)} %dynamic-slice_bitcast_fusion.1), channel_id=1, source_target_pairs={{0,4},{4,0},{1,5},{5,1},{2,6},{6,2},{3,7},{7,3},{8,12},{12,8},{9,1... | collective-permute-start | bytes 6291464 | tf_op jit(solution)/shard_map/ppermute | solution.py:31

commit v7 on v6

--- a/solution.py
+++ b/solution.py
@@ -145,31 +145,29 @@
     return jnp.dot(a, b, precision=highest, preferred_element_type=jnp.float32)
 
 
-def pick_kernel(info, rows, cols, meta, child, diag, panel, pivot_part):
+def pick_kernel(info, rows, cols, meta, *refs):
+    count = info.pivot_count
+    children, diags = refs[:count], refs[count : 2 * count]
+    panel, pivot_part = refs[2 * count :]
     half = rows // 2
     r, q = info.row(meta), info.col(meta)
     mine, within = r // half, r % half
-    p = pl.program_id(0)
-    front_block = info.pivot(meta, p)
-    block = front_block % info.child_blocks
-    present = jnp.logical_and(info.has(meta, mine, block, front_block), block % half == within)
-    panel[0] = child[0] * as_float(present)
-    first = p * (p + 1) // 2
-    for t in range(info.pivot_count):
-        other = info.pivot(meta, t)
-        other_block = other % info.child_blocks
-        here = jnp.logical_and(info.has(meta, mine, other_block, other), other_block % cols == q)
-
-        @pl.when(t <= p)
+    for p in range(count):
+        front_block = info.pivot(meta, p)
+        block = front_block % info.child_blocks
+        present = jnp.logical_and(info.has(meta, mine, block, front_block), block % half == within)
+        panel[p] = children[p][0] * as_float(present)
+        first = p * (p + 1) // 2
+        for t in range(p + 1):
+            other = info.pivot(meta, t)
+            other_block = other % info.child_blocks
+            here = jnp.logical_and(info.has(meta, mine, other_block, other), other_block % cols == q)
+            at = pl.multiple_of(other_block // cols * BLK, BLK)
+            pivot_part[first + t] = panel[p, :, pl.ds(at, BLK)] * as_float(here)
+
+        @pl.when(jnp.logical_and(front_block % rows == r, front_block % cols == q))
         def _():
-            at = pl.multiple_of(other_block // cols * BLK, BLK)
-            pivot_part[first + t] = panel[0, :, pl.ds(at, BLK)] * as_float(here)
-
-    on_diagonal = jnp.logical_and(front_block % rows == r, front_block % cols == q)
-
-    @pl.when(on_diagonal)
-    def _():
-        pivot_part[first + p] += jnp.where(eye_mask(), diag[0], 0.0)
+            pivot_part[first + p] += jnp.where(eye_mask(), diags[p][0], 0.0)
 
 
 def cholesky_kernel(count, blocks, lower, inverse, inverse_t, work, rest):
@@ -375,20 +373,20 @@
     shape = jax.ShapeDtypeStruct
 
     lower_count = pivot_count * (pivot_count + 1) // 2
+    child_spec = lambda p: pl.BlockSpec(
+        (1, BLK, child_width), lambda g, m: (info.pivot(m, p) % child_blocks // half, 0, 0)
+    )
+    diag_spec = lambda p: pl.BlockSpec((1, 1, BLK), lambda g, m: (info.pivot(m, p) // rows, 0, 0))
+    child_view = contrib.reshape(child_rows, BLK, child_width)
     panel, pivot_part = pl.pallas_call(
         functools.partial(pick_kernel, info, rows, cols),
         grid_spec=pltpu.PrefetchScalarGridSpec(
             num_scalar_prefetch=1,
-            grid=(pivot_count,),
-            in_specs=[
-                pl.BlockSpec(
-                    (1, BLK, child_width), lambda p, m: (info.pivot(m, p) % child_blocks // half, 0, 0)
-                ),
-                pl.BlockSpec((1, 1, BLK), lambda p, m: (info.pivot(m, p) // rows, 0, 0)),
-            ],
+            grid=(1,),
+            in_specs=[child_spec(p) for p in range(pivot_count)] + [diag_spec(p) for p in range(pivot_count)],
             out_specs=[
-                pl.BlockSpec((1, BLK, child_width), lambda p, m: (p, 0, 0)),
-                pl.BlockSpec((lower_count, BLK, BLK), lambda p, m: (0, 0, 0)),
+                pl.BlockSpec((pivot_count, BLK, child_width), lambda g, m: (0, 0, 0)),
+                pl.BlockSpec((lower_count, BLK, BLK), lambda g, m: (0, 0, 0)),
             ],
         ),
         out_shape=[
@@ -398,7 +396,7 @@
         compiler_params=params(1, 60),
         name="pick",
         cost_estimate=about(5),
-    )(meta, contrib.reshape(child_rows, BLK, child_width), front_diag.reshape(row_slots, 1, BLK))
+    )(meta, *[child_view] * pivot_count, *[front_diag.reshape(row_slots, 1, BLK)] * pivot_count)
     own = panel.reshape(depth, child_width)
     for bit in range(half_bit):
         own = own + swapped(own, "row", bit)

time: 285 us -> 285 us (level)
  local copies, waits for them, and re-layouts: 33 us -> 36.6 us
    unnamed x34 -> x40, local copies, waits for them, and re-layouts: 5.61 us -> 8.49 us
where the time goes in v7:
time: 285 us; the launch traced here: 284 us
  Pallas kernels  149 us (52%)
  waiting for transfers between devices  66.2 us (23%)
  local copies, waits for them, and re-layouts  36.6 us (13%)
  starting transfers between devices  20.5 us (7%)
  between operations  8.57 us (3%)
  other arithmetic  3.74 us (1%)
    pallas_call x1, Pallas kernels, per_device(): pl.pallas_call(functools.partial(cholesky_kernel, pivot_count), out_shape...  58.9 us
    pallas_call x3, Pallas kernels, per_device(): pl.pallas_call(functools.partial(update_kernel, info, rows, cols, child_s...  44.1 us
    ppermute x7, waiting for transfers between devices, swapped(): lax.ppermute(shard, axis, [(i, i ^ 1 << bit) for i in range(lax.axis_size...  37 us
    pallas_call x3, Pallas kernels, per_device(): pl.pallas_call(functools.partial(rows_kernel, info, rows, cols, few, shar...  30.8 us
    ppermute x6, waiting for transfers between devices, per_device(): held.append([lax.ppermute(part, ('row', 'col'), pairs) for part in sent])  29.2 us
    reshape x3, local copies, waits for them, and re-layouts, per_device(): part = lax.dynamic_slice(own_view, (first, partner_turns[turn] * start, 1...  11.4 us
    ppermute x6, starting transfers between devices, per_device(): held.append([lax.ppermute(part, ('row', 'col'), pairs) for part in sent])  11 us
    pallas_call x1, Pallas kernels, per_device(): pl.pallas_call(functools.partial(columns_kernel, info, rows, cols, child_...  10.1 us
  transfers between devices with their start and end apart: 13, of which 4 were waited for; matrix products, arithmetic and copies ran while one was open for 10% of the time, Pallas kernels for 47%

profile of v7, /device:TPU:6, one launch (start us, length us, event | category | flops | bytes accessed | tf_op | source)
XLA Modules:
  0.0 284.3 jit_solution(369409202663521631)
XLA Ops:
  0.6 0.8 reshape.61
  1.4 0.7 fusion
  2.1 1.2 concatenate.6.meta.refs_6_
  3.3 4.2 %pick.1 = (f32[4,128,1024]{2,1,0:T(8,128)}, f32[10,128,128]{2,1,0:T(8,128)}) custom-call(s32[74]{0:T(128)} %concatenate.6.meta.refs_6_, f32[32,128,1024]{2,1,0:T(8,128)} %bitcast.33, f32[32,128,1024]{2,1,0:T(8,128)} %bitcast.34, f32[32,128,1024]{2,1,0:T(8,128)} %bitcast.35, f32[32,128,1024]{2,1,0:T(8,128)} %bitcast.36, f32[32,1,128]{2,1,0:T(1,128)} %bitcast.26, ...), custom_call_target="tpu_custom_call" | custom-call | flops 5750000128 | bytes 18450000 | tf_op jit(solution)/shard_map/pick/pallas_call | solution.py:381
  7.5 0.5 collective-permute-start
  8.0 1.6 collective-permute-start.1
  9.5 14.8 %collective-permute-done.1 = f32[10,128,128]{2,1,0:T(8,128)S(1)} collective-permute-done((f32[10,128,128]{2,1,0:T(8,128)}, f32[10,128,128]{2,1,0:T(8,128)S(1)}, u32[]{:S(2)}, u32[]{:S(2)}) %collective-permute-start.1) | collective-permute-done | bytes 655392 | tf_op jit(solution)/shard_map/ppermute | solution.py:31
  24.4 0.8 copy-done.18
  25.2 1.2 add.37
  26.4 2.7 collective-permute-start.2
  29.1 0.6 fusion.3
  29.7 1.2 slice.33
  32.9 22.2 %collective-permute-done.other = f32[512,1024]{1,0:T(8,128)S(1)} collective-permute-done((f32[512,1024]{1,0:T(8,128)}, f32[512,1024]{1,0:T(8,128)S(1)}, u32[]{:S(2)}, u32[]{:S(2)}) %collective-permute-start) | collective-permute-done | bytes 2097184 | tf_op jit(solution)/shard_map/ppermute | solution.py:31
  55.0 0.5 slice.32
  57.0 1.3 collective-permute-start.6
  58.3 4.9 %dynamic-slice_bitcast_fusion = f32[8,128,1024]{2,1,0:T(8,128)} fusion(f32[8,2,2,128,1024]{4,3,2,1,0:T(8,128)} %bitcast.37, s32[]{:T(128)S(6)} %select_n.52, s32[]{:T(128)S(6)} %select_n.53), kind=kLoop, calls=%fused_computation.1 | loop fusion | bytes 8388616 | tf_op jit(solution)/shard_map/reshape | solution.py:475
  63.3 0.7 collective-permute-start.10
  64.0 0.5 slice.31
  65.9 2.4 maximum_multiply_fusion.refs_0_
  68.3 2.7 collective-permute-start.9
  71.0 1.3 collective-permute-start.3
  72.3 4.7 %fusion.2 = (f32[1024,512]{1,0:T(8,128)}, f32[1024,512]{1,0:T(8,128)}) fusion(f32[1024,1024]{1,0:T(8,128)} %maximum_multiply_fusion.refs_0_), kind=kLoop, calls=%fused_computation.9 | loop fusion | bytes 8388608 | tf_op jit(solution)/shard_map/split | solution.py:429
  76.9 2.0 collective-permute-start.7
  79.0 2.1 collective-permute-start.4
  81.1 58.9 %factor_pivots.1 = (f32[512,512]{1,0:T(8,128)S(1)}, f32[512,512]{1,0:T(8,128)S(1)}, f32[512,512]{1,0:T(8,128)S(1)}) custom-call(f32[10,128,128]{2,1,0:T(8,128)S(1)} %add.39.blocks), custom_call_target="tpu_custom_call" | custom-call | flops 67849998336 | bytes 217710000 | tf_op jit(solution)/shard_map/factor_pivots/pallas_call | solution.py:437
  140.0 1.0 copy-done.11
  141.0 1.0 copy-done.13
  141.9 0.6 slice.29
  144.4 3.2 %dynamic-slice_bitcast_fusion.2.refs_1_ = f32[4,128,1024]{2,1,0:T(8,128)} fusion(f32[8,2,2,128,1024]{4,3,2,1,0:T(8,128)} %bitcast.38, s32[]{:T(128)S(6)} %select_n.56, s32[]{:T(128)S(6)} %select_n.53), kind=kLoop, calls=%fused_computation.3 | loop fusion | bytes 4194312 | tf_op jit(solution)/shard_map/reshape | solution.py:475
  147.6 0.6 pause.1
  148.2 1.3 slice.30
  150.7 3.2 %dynamic-slice_bitcast_fusion.1 = f32[4,128,1024]{2,1,0:T(8,128)} fusion(f32[8,2,2,128,1024]{4,3,2,1,0:T(8,128)} %bitcast.39, s32[]{:T(128)S(6)} %select_n.57, s32[]{:T(128)S(6)} %select_n.53), kind=kLoop, calls=%fused_computation.2 | loop fusion | bytes 4194312 | tf_op jit(solution)/shard_map/reshape | solution.py:475
  154.0 12.4 %collective-permute-done.3.refs_1_.refs_0_ = f32[1024,1024]{1,0:T(8,128)} collective-permute-done((f32[1024,1024]{1,0:T(8,128)}, f32[1024,1024]{1,0:T(8,128)}, u32[]{:S(2)}, u32[]{:S(2)}) %collective-permute-start.3) | collective-permute-done | bytes 4194336 | tf_op jit(solution)/shard_map/ppermute | solution.py:432
  166.4 2.6 collective-permute-start.11
  169.0 4.7 %fusion.1 = (f32[1024,512]{1,0:T(8,128)}, f32[1024,512]{1,0:T(8,128)}) fusion(f32[1024,1024]{1,0:T(8,128)} %collective-permute-done.3.refs_1_.refs_0_), kind=kLoop, calls=%fused_computation.8 | loop fusion | bytes 8388608 | tf_op jit(solution)/shard_map/split | solution.py:429
  173.7 1.3 collective-permute-start.8
  175.0 1.6 collective-permute-start.5
  176.6 10.1 %factor_at_columns.1.refs_3_ = bf16[1536,2048]{1,0:T(8,128)(2,1)} custom-call(s32[74]{0:T(128)S(1)} %copy-done.6, f32[512,1024]{1,0:T(8,128)S(1)} %bitcast.25, f32[512,1024]{1,0:T(8,128)S(1)} %copy-done.4, f32[512,512]{1,0:T(8,128)S(1)} %copy-done.10, f32[1024,1024]{1,0:T(8,128)} %collective-permute-done.3.refs_1_.refs_0_, ...), custom_call_target="tpu_custom_call" | custom-call | flops 11500000256 | bytes 36900000 | tf_op jit(solution)/shard_map/factor_at_columns/pallas_call | solution.py:484
  186.8 14.3 %factor_rows.3 = (f32[2,8,2,128,128]{4,3,2,1,0:T(8,128)}, bf16[2,8,128,1536]{3,2,1,0:T(8,128)(2,1)}) custom-call(s32[74]{0:T(128)S(1)} %copy-done.6, f32[1024,1024]{1,0:T(8,128)} %maximum_multiply_fusion.refs_0_, f32[1024,1024]{1,0:T(8,128)} %collective-permute-done.3.refs_1_.refs_0_, f32[1024,1024]{1,0:T(8,128)} %collective-permute-done.9.refs_2_.refs_1_, ...), custom_call_target="tpu_custom_call" | custom-call | flops 13799999488 | bytes 44280000 | tf_op jit(solution)/shard_map/factor_rows/pallas_call | solution.py:548
  201.1 2.8 copy-done.16
  203.8 20.7 %update_tile.3 = (f32[2,8,2,128,2048]{4,3,2,1,0:T(8,128)}, f32[8,128]{1,0:T(8,128)S(1)}) custom-call(s32[74]{0:T(128)S(1)} %copy-done.6, f32[8,2,2,128,1024]{4,3,2,1,0:T(8,128)} %bitcast.40, f32[8,128,1024]{2,1,0:T(8,128)} %collective-permute-done.10.refs_2_.refs_1_, bf16[2,8,128,1536]{3,2,1,0:T(8,128)(2,1)S(1)} %copy-done.16, ...), custom_call_target="tpu_custom_call" | custom-call | flops 27599998976 | bytes 88560000 | tf_op jit(solution)/shard_map/update_tile/pallas_call | solution.py:602
  224.7 1.3 copy-done.7
  226.0 1.6 copy-done.8
  227.6 8.0 %factor_rows.4 = (f32[2,8,2,128,128]{4,3,2,1,0:T(8,128)}, bf16[2,4,128,1536]{3,2,1,0:T(8,128)(2,1)S(1)}) custom-call(s32[74]{0:T(128)S(1)} %copy-done.6, f32[1024,1024]{1,0:T(8,128)} %collective-permute-done.3.refs_1_.refs_0_, f32[1024,512]{1,0:T(8,128)} %collective-permute-done.7.refs_1_, ...), custom_call_target="tpu_custom_call", output_to_operand_aliasing={{0}: (6, {})} | custom-call | flops 6899999744 | bytes 22140000 | tf_op jit(solution)/shard_map/factor_rows/pallas_call | solution.py:548
  235.6 11.8 %update_tile.4 = (f32[2,8,2,128,2048]{4,3,2,1,0:T(8,128)}, f32[8,128]{1,0:T(8,128)S(1)}) custom-call(s32[74]{0:T(128)S(1)} %copy-done.6, f32[8,2,2,128,1024]{4,3,2,1,0:T(8,128)} %bitcast.41, f32[4,128,1024]{2,1,0:T(8,128)} %collective-permute-done.11.refs_1_, ...), custom_call_target="tpu_custom_call", output_to_operand_aliasing={{0}: (6, {})} | custom-call | flops 13799999488 | bytes 44280000 | tf_op jit(solution)/shard_map/update_tile/pallas_call | solution.py:602
  247.4 16.8 %collective-permute-done.5.refs_2_ = f32[1024,512]{1,0:T(8,128)} collective-permute-done((f32[1024,512]{1,0:T(8,128)}, f32[1024,512]{1,0:T(8,128)}, u32[]{:S(2)}, u32[]{:S(2)}) %collective-permute-start.5) | collective-permute-done | bytes 2097184 | tf_op jit(solution)/shard_map/ppermute | solution.py:432
  264.2 8.6 %factor_rows.5 = (f32[2,8,2,128,128]{4,3,2,1,0:T(8,128)}, bf16[2,4,128,1536]{3,2,1,0:T(8,128)(2,1)S(1)}) custom-call(s32[74]{0:T(128)S(1)} %copy-done.6, f32[1024,1024]{1,0:T(8,128)} %collective-permute-done.3.refs_1_.refs_0_, f32[1024,512]{1,0:T(8,128)} %collective-permute-done.4.refs_1_, ...), custom_call_target="tpu_custom_call", output_to_operand_aliasing={{0}: (6, {})} | custom-call | flops 6899999744 | bytes 22140000 | tf_op jit(solution)/shard_map/factor_rows/pallas_call | solution.py:548
  272.8 11.6 %update_tile.5 = (f32[2,8,2,128,2048]{4,3,2,1,0:T(8,128)}, f32[8,128]{1,0:T(8,128)}) custom-call(s32[74]{0:T(128)S(1)} %copy-done.6, f32[8,2,2,128,1024]{4,3,2,1,0:T(8,128)} %bitcast.42, f32[4,128,1024]{2,1,0:T(8,128)S(1)} %collective-permute-done.12.refs_1_, ...), custom_call_target="tpu_custom_call", output_to_operand_aliasing={{0}: (6, {})} | custom-call | flops 13799999488 | bytes 44280000 | tf_op jit(solution)/shard_map/update_tile/pallas_call | solution.py:602
  (47 shorter events, 0.4 us)
Async XLA Ops:
  3.3 25.8 %copy-start.19 = (s32[2,2,4]{2,1,0:T(2,128)S(1)}, s32[2,2,4]{2,1,0:T(2,128)}, u32[]{:S(2)}) copy-start(s32[2,2,4]{2,1,0:T(2,128)} %constant.48.clone) | copy-start | bytes 196
  7.5 47.6 %collective-permute-start = (f32[512,1024]{1,0:T(8,128)}, f32[512,1024]{1,0:T(8,128)S(1)}, u32[]{:S(2)}, u32[]{:S(2)}) collective-permute-start(f32[512,1024]{1,0:T(8,128)} %bitcast.23), channel_id=1, source_target_pairs={{0,4},{4,0},{1,5},{5,1},{2,6},{6,2},{3,7},{7,3},{8,12},{12,8},{9,1... | collective-permute-start | bytes 6291464 | tf_op jit(solution)/shard_map/ppermute | solution.py:31
  8.0 16.4 %collective-permute-start.1 = (f32[10,128,128]{2,1,0:T(8,128)}, f32[10,128,128]{2,1,0:T(8,128)S(1)}, u32[]{:S(2)}, u32[]{:S(2)}) collective-permute-start(f32[10,128,128]{2,1,0:T(8,128)} %get-tuple-element.19), channel_id=1, source_target_pairs={{0,1},{1,0},{2,3},{3,2},{4,5},{5,4},{6,7},{7,6},{8,9},{9,8},{10,11... | collective-permute-start | bytes 1966088 | tf_op jit(solution)/shard_map/ppermute | solution.py:31
  24.4 0.8 copy-start.18
  26.4 30.5 %collective-permute-start.2 = (f32[10,128,128]{2,1,0:T(8,128)S(1)}, f32[10,128,128]{2,1,0:T(8,128)S(1)}, u32[]{:S(2)}, u32[]{:S(2)}) collective-permute-start(f32[10,128,128]{2,1,0:T(8,128)S(1)} %add.37), channel_id=1, source_target_pairs={{0,2},{1,3},{2,0},{3,1},{4,6},{5,7},{6,4},{7,5},{8,10},{9,11},{10,... | collective-permute-start | bytes 1966088 | tf_op jit(solution)/shard_map/ppermute | solution.py:31
  55.0 3.3 %copy-start.2 = (f32[512,1024]{1,0:T(8,128)}, f32[512,1024]{1,0:T(8,128)S(1)}, u32[]{:S(2)}) copy-start(f32[512,1024]{1,0:T(8,128)S(1)} %collective-permute-done.other) | copy-start | bytes 6291460
  57.0 22.0 %collective-permute-start.6 = (f32[10,128,128]{2,1,0:T(8,128)S(1)}, f32[10,128,128]{2,1,0:T(8,128)S(1)}, u32[]{:S(2)}, u32[]{:S(2)}) collective-permute-start(f32[10,128,128]{2,1,0:T(8,128)S(1)} %add_multiply_fusion), channel_id=1, source_target_pairs={{0,4},{4,0},{1,5},{5,1},{2,6},{6,2},{3,7},{7,3},{8,12},{12,8},{9,1... | collective-permute-start | bytes 1966088 | tf_op jit(solution)/shard_map/ppermute | solution.py:31
  58.3 7.5 %copy-start.1 = (f32[4,128,1024]{2,1,0:T(8,128)S(1)}, f32[4,128,1024]{2,1,0:T(8,128)}, u32[]{:S(2)}) copy-start(f32[4,128,1024]{2,1,0:T(8,128)} %get-tuple-element.18) | copy-start | bytes 6291460
  58.3 7.5 %copy-start.3 = (f32[512,1024]{1,0:T(8,128)S(1)}, f32[512,1024]{1,0:T(8,128)}, u32[]{:S(2)}) copy-start(f32[512,1024]{1,0:T(8,128)} %copy-done.2) | copy-start | bytes 6291460
  63.3 110.4 %collective-permute-start.10 = (f32[8,128,1024]{2,1,0:T(8,128)}, f32[8,128,1024]{2,1,0:T(8,128)}, u32[]{:S(2)}, u32[]{:S(2)}) collective-permute-start(f32[8,128,1024]{2,1,0:T(8,128)} %dynamic-slice_bitcast_fusion), channel_id=1, source_target_pairs={{0,4},{4,0},{1,5},{5,1},{2,6},{6,2},{3,7},{7,3},{8,12},{12,8},{9,1... | collective-permute-start | bytes 12582920 | tf_op jit(solution)/shard_map/ppermute | solution.py:31
  68.3 106.7 %collective-permute-start.9 = (f32[1024,1024]{1,0:T(8,128)}, f32[1024,1024]{1,0:T(8,128)}, u32[]{:S(2)}, u32[]{:S(2)}) collective-permute-start(f32[1024,1024]{1,0:T(8,128)} %maximum_multiply_fusion.refs_0_), channel_id=1, source_target_pairs={{2,1},{5,6},{10,9},{13,14},{18,17},{21,22},{26,25},{29,30}} | collective-permute-start | bytes 12582920 | tf_op jit(solution)/shard_map/ppermute | solution.py:432
  71.0 95.5 %collective-permute-start.3 = (f32[1024,1024]{1,0:T(8,128)}, f32[1024,1024]{1,0:T(8,128)}, u32[]{:S(2)}, u32[]{:S(2)}) collective-permute-start(f32[1024,1024]{1,0:T(8,128)} %maximum_multiply_fusion.refs_0_), channel_id=1, source_target_pairs={{2,3},{0,2},{5,4},{7,5},{10,11},{8,10},{13,12},{15,13},{18,19},{16... | collective-permute-start | bytes 12582920 | tf_op jit(solution)/shard_map/ppermute | solution.py:432
  76.9 147.6 %collective-permute-start.7 = (f32[1024,512]{1,0:T(8,128)}, f32[1024,512]{1,0:T(8,128)}, u32[]{:S(2)}, u32[]{:S(2)}) collective-permute-start(f32[1024,512]{1,0:T(8,128)} %get-tuple-element.36), channel_id=1, source_target_pairs={{2,0},{0,1},{5,7},{7,6},{10,8},{8,9},{13,15},{15,14},{18,16},{16,1... | collective-permute-start | bytes 6291464 | tf_op jit(solution)/shard_map/ppermute | solution.py:432
  79.0 168.5 %collective-permute-start.4 = (f32[1024,512]{1,0:T(8,128)}, f32[1024,512]{1,0:T(8,128)}, u32[]{:S(2)}, u32[]{:S(2)}) collective-permute-start(f32[1024,512]{1,0:T(8,128)} %get-tuple-element.37), channel_id=1, source_target_pairs={{2,0},{0,1},{5,7},{7,6},{10,8},{8,9},{13,15},{15,14},{18,16},{16,1... | collective-permute-start | bytes 6291464 | tf_op jit(solution)/shard_map/ppermute | solution.py:432
  140.0 1.0 copy-start.11
  141.0 1.0 copy-start.13
  141.9 5.7 %copy-start.9 = (f32[512,512]{1,0:T(8,128)}, f32[512,512]{1,0:T(8,128)S(1)}, u32[]{:S(2)}) copy-start(f32[512,512]{1,0:T(8,128)S(1)} %get-tuple-element.24.inverse.refs_0_) | copy-start | bytes 3145732
  154.0 22.6 %copy-start.4 = (f32[512,1024]{1,0:T(8,128)S(1)}, f32[512,1024]{1,0:T(8,128)}, u32[]{:S(2)}) copy-start(f32[512,1024]{1,0:T(8,128)} %copy-done.2) | copy-start | bytes 6291460
  154.0 22.6 %copy-start.6 = (s32[74]{0:T(128)S(1)}, s32[74]{0:T(128)}, u32[]{:S(2)}) copy-start(s32[74]{0:T(128)} %concatenate.6.meta.refs_6_) | copy-start | bytes 892
  154.0 22.6 %copy-start.10 = (f32[512,512]{1,0:T(8,128)S(1)}, f32[512,512]{1,0:T(8,128)}, u32[]{:S(2)}) copy-start(f32[512,512]{1,0:T(8,128)} %copy-done.9) | copy-start | bytes 3145732
  166.4 69.1 %collective-permute-start.11 = (f32[4,128,1024]{2,1,0:T(8,128)}, f32[4,128,1024]{2,1,0:T(8,128)}, u32[]{:S(2)}, u32[]{:S(2)}) collective-permute-start(f32[4,128,1024]{2,1,0:T(8,128)} %dynamic-slice_bitcast_fusion.2.refs_1_), channel_id=1, source_target_pairs={{0,4},{4,0},{1,5},{5,1},{2,6},{6,2},{3,7},{7,3},{8,12},{12,8},{9,1... | collective-permute-start | bytes 6291464 | tf_op jit(solution)/shard_map/ppermute | solution.py:31
  173.7 51.0 %collective-permute-start.8 = (f32[1024,512]{1,0:T(8,128)}, f32[1024,512]{1,0:T(8,128)S(1)}, u32[]{:S(2)}, u32[]{:S(2)}) collective-permute-start(f32[1024,512]{1,0:T(8,128)} %get-tuple-element.34), channel_id=1, source_target_pairs={{2,3},{5,4},{10,11},{13,12},{18,19},{21,20},{26,27},{29,28}} | collective-permute-start | bytes 6291464 | tf_op jit(solution)/shard_map/ppermute | solution.py:432
  175.0 11.8 %copy-start.12 = (f32[512,512]{1,0:T(8,128)S(1)}, f32[512,512]{1,0:T(8,128)}, u32[]{:S(2)}) copy-start(f32[512,512]{1,0:T(8,128)} %copy-done.11) | copy-start | bytes 3145732
  175.0 11.8 %copy-start.14 = (f32[512,512]{1,0:T(8,128)S(1)}, f32[512,512]{1,0:T(8,128)}, u32[]{:S(2)}) copy-start(f32[512,512]{1,0:T(8,128)} %copy-done.13) | copy-start | bytes 3145732
  175.0 89.2 %collective-permute-start.5 = (f32[1024,512]{1,0:T(8,128)}, f32[1024,512]{1,0:T(8,128)}, u32[]{:S(2)}, u32[]{:S(2)}) collective-permute-start(f32[1024,512]{1,0:T(8,128)} %get-tuple-element.35), channel_id=1, source_target_pairs={{2,3},{5,4},{10,11},{13,12},{18,19},{21,20},{26,27},{29,28}} | collective-permute-start | bytes 6291464 | tf_op jit(solution)/shard_map/ppermute | solution.py:432
  186.8 14.3 %copy-start = (bf16[1536,2048]{1,0:T(8,128)(2,1)S(1)}, bf16[1536,2048]{1,0:T(8,128)(2,1)}, u32[]{:S(2)}) copy-start(bf16[1536,2048]{1,0:T(8,128)(2,1)} %factor_at_columns.1.refs_3_) | copy-start | bytes 18874372
  186.8 14.3 %copy-start.5 = (f32[4096]{0:T(1024)S(1)}, f32[4096]{0:T(1024)}, u32[]{:S(2)}) copy-start(f32[4096]{0:T(1024)} %param.7) | copy-start | bytes 49156
  201.0 2.8 copy-start.16
  203.8 20.7 %copy-start.17 = (f32[4,128,1024]{2,1,0:T(8,128)S(1)}, f32[4,128,1024]{2,1,0:T(8,128)}, u32[]{:S(2)}) copy-start(f32[4,128,1024]{2,1,0:T(8,128)} %dynamic-slice_bitcast_fusion.1) | copy-start | bytes 6291460
  203.8 22.1 %copy-start.15 = (f32[512,512]{1,0:T(8,128)S(1)}, f32[512,512]{1,0:T(8,128)}, u32[]{:S(2)}) copy-start(f32[512,512]{1,0:T(8,128)} %copy-done.13) | copy-start | bytes 3145732
  224.5 48.2 %collective-permute-start.12 = (f32[4,128,1024]{2,1,0:T(8,128)S(1)}, f32[4,128,1024]{2,1,0:T(8,128)S(1)}, u32[]{:S(2)}, u32[]{:S(2)}) collective-permute-start(f32[4,128,1024]{2,1,0:T(8,128)S(1)} %copy-done.17), channel_id=1, source_target_pairs={{0,4},{4,0},{1,5},{5,1},{2,6},{6,2},{3,7},{7,3},{8,12},{12,8},{9,1... | collective-permute-start | bytes 6291464 | tf_op jit(solution)/shard_map/ppermute | solution.py:31
  224.7 1.3 copy-start.7
  226.0 1.6 copy-start.8

commit v8 on v7

--- a/solution.py
+++ b/solution.py
@@ -506,7 +506,7 @@
     diag_view = front_diag.reshape(2, child_slots, sources, 1, BLK)
     mine_of = lambda m: info.row(m) // half
     square = pl.BlockSpec((depth, depth), whole)
-    few = min(2, width)
+    few = width
     counts = [1] + [halves] * (sources - 1)
     row_parts = [[] for _ in counts]
 
@@ -567,7 +567,7 @@
                 input_output_aliases=aliases,
                 compiler_params=params(1, 40),
                 name="factor_rows",
-                cost_estimate=about(3.0 * steps_here * (LATE if turn else 1.0)),
+                cost_estimate=about(1.5 * few * steps_here * (LATE if turn else 1.0)),
             )(meta, *operands)
             row_parts[turn].append(row_part)
             continue

time: 285 us -> 286 us (level)
  no operation moved by 1% of the time
where the time goes in v8:
time: 286 us; the launch traced here: 285 us
  Pallas kernels  151 us (53%)
  waiting for transfers between devices  64.5 us (23%)
  local copies, waits for them, and re-layouts  36.6 us (13%)
  starting transfers between devices  20.6 us (7%)
  between operations  8.57 us (3%)
  other arithmetic  3.74 us (1%)
    pallas_call x1, Pallas kernels, per_device(): pl.pallas_call(functools.partial(cholesky_kernel, pivot_count), out_shape...  58.9 us
    pallas_call x3, Pallas kernels, per_device(): pl.pallas_call(functools.partial(update_kernel, info, rows, cols, child_s...  44.1 us
    ppermute x7, waiting for transfers between devices, swapped(): lax.ppermute(shard, axis, [(i, i ^ 1 << bit) for i in range(lax.axis_size...  37 us
    pallas_call x3, Pallas kernels, per_device(): pl.pallas_call(functools.partial(rows_kernel, info, rows, cols, few, shar...  33.3 us
    ppermute x6, waiting for transfers between devices, per_device(): held.append([lax.ppermute(part, ('row', 'col'), pairs) for part in sent])  27.5 us
    reshape x3, local copies, waits for them, and re-layouts, per_device(): part = lax.dynamic_slice(own_view, (first, partner_turns[turn] * start, 1...  11.4 us
    ppermute x6, starting transfers between devices, per_device(): held.append([lax.ppermute(part, ('row', 'col'), pairs) for part in sent])  11 us
    pallas_call x1, Pallas kernels, per_device(): pl.pallas_call(functools.partial(columns_kernel, info, rows, cols, child_...  10.1 us
  transfers between devices with their start and end apart: 13, of which 4 were waited for; matrix products, arithmetic and copies ran while one was open for 10% of the time, Pallas kernels for 47%

profile of v8, /device:TPU:6, one launch (start us, length us, event | category | flops | bytes accessed | tf_op | source)
XLA Modules:
  0.0 285.2 jit_solution(8384121375437933041)
XLA Ops:
  0.6 0.8 reshape.61
  1.4 0.7 fusion
  2.1 1.2 concatenate.6.meta.refs_6_
  3.3 4.2 %pick.1 = (f32[4,128,1024]{2,1,0:T(8,128)}, f32[10,128,128]{2,1,0:T(8,128)}) custom-call(s32[74]{0:T(128)} %concatenate.6.meta.refs_6_, f32[32,128,1024]{2,1,0:T(8,128)} %bitcast.33, f32[32,128,1024]{2,1,0:T(8,128)} %bitcast.34, f32[32,128,1024]{2,1,0:T(8,128)} %bitcast.35, f32[32,128,1024]{2,1,0:T(8,128)} %bitcast.36, f32[32,1,128]{2,1,0:T(1,128)} %bitcast.26, ...), custom_call_target="tpu_custom_call" | custom-call | flops 5750000128 | bytes 18450000 | tf_op jit(solution)/shard_map/pick/pallas_call | solution.py:381
  7.5 0.5 collective-permute-start
  8.0 1.6 collective-permute-start.1
  9.5 14.8 %collective-permute-done.1 = f32[10,128,128]{2,1,0:T(8,128)S(1)} collective-permute-done((f32[10,128,128]{2,1,0:T(8,128)}, f32[10,128,128]{2,1,0:T(8,128)S(1)}, u32[]{:S(2)}, u32[]{:S(2)}) %collective-permute-start.1) | collective-permute-done | bytes 655392 | tf_op jit(solution)/shard_map/ppermute | solution.py:31
  24.4 0.8 copy-done.18
  25.2 1.2 add.37
  26.4 2.7 collective-permute-start.2
  29.1 0.6 fusion.3
  29.7 1.2 slice.33
  32.9 22.2 %collective-permute-done.other = f32[512,1024]{1,0:T(8,128)S(1)} collective-permute-done((f32[512,1024]{1,0:T(8,128)}, f32[512,1024]{1,0:T(8,128)S(1)}, u32[]{:S(2)}, u32[]{:S(2)}) %collective-permute-start) | collective-permute-done | bytes 2097184 | tf_op jit(solution)/shard_map/ppermute | solution.py:31
  55.0 0.5 slice.32
  57.0 1.3 collective-permute-start.6
  58.3 4.9 %dynamic-slice_bitcast_fusion = f32[8,128,1024]{2,1,0:T(8,128)} fusion(f32[8,2,2,128,1024]{4,3,2,1,0:T(8,128)} %bitcast.37, s32[]{:T(128)S(6)} %select_n.52, s32[]{:T(128)S(6)} %select_n.53), kind=kLoop, calls=%fused_computation.1 | loop fusion | bytes 8388616 | tf_op jit(solution)/shard_map/reshape | solution.py:475
  63.3 0.7 collective-permute-start.10
  64.0 0.5 slice.31
  65.9 2.4 maximum_multiply_fusion.refs_0_
  68.3 2.7 collective-permute-start.9
  71.0 1.3 collective-permute-start.3
  72.3 4.7 %fusion.2 = (f32[1024,512]{1,0:T(8,128)}, f32[1024,512]{1,0:T(8,128)}) fusion(f32[1024,1024]{1,0:T(8,128)} %maximum_multiply_fusion.refs_0_), kind=kLoop, calls=%fused_computation.9 | loop fusion | bytes 8388608 | tf_op jit(solution)/shard_map/split | solution.py:429
  76.9 2.0 collective-permute-start.7
  79.0 2.1 collective-permute-start.4
  81.1 58.9 %factor_pivots.1 = (f32[512,512]{1,0:T(8,128)S(1)}, f32[512,512]{1,0:T(8,128)S(1)}, f32[512,512]{1,0:T(8,128)S(1)}) custom-call(f32[10,128,128]{2,1,0:T(8,128)S(1)} %add.39.blocks), custom_call_target="tpu_custom_call" | custom-call | flops 67849998336 | bytes 217710000 | tf_op jit(solution)/shard_map/factor_pivots/pallas_call | solution.py:437
  140.0 1.0 copy-done.11
  141.0 1.0 copy-done.13
  141.9 0.6 slice.29
  144.4 3.2 %dynamic-slice_bitcast_fusion.2.refs_1_ = f32[4,128,1024]{2,1,0:T(8,128)} fusion(f32[8,2,2,128,1024]{4,3,2,1,0:T(8,128)} %bitcast.38, s32[]{:T(128)S(6)} %select_n.56, s32[]{:T(128)S(6)} %select_n.53), kind=kLoop, calls=%fused_computation.3 | loop fusion | bytes 4194312 | tf_op jit(solution)/shard_map/reshape | solution.py:475
  147.6 0.6 pause.1
  148.2 1.3 slice.30
  150.7 3.2 %dynamic-slice_bitcast_fusion.1 = f32[4,128,1024]{2,1,0:T(8,128)} fusion(f32[8,2,2,128,1024]{4,3,2,1,0:T(8,128)} %bitcast.39, s32[]{:T(128)S(6)} %select_n.57, s32[]{:T(128)S(6)} %select_n.53), kind=kLoop, calls=%fused_computation.2 | loop fusion | bytes 4194312 | tf_op jit(solution)/shard_map/reshape | solution.py:475
  154.0 12.4 %collective-permute-done.3.refs_1_.refs_0_ = f32[1024,1024]{1,0:T(8,128)} collective-permute-done((f32[1024,1024]{1,0:T(8,128)}, f32[1024,1024]{1,0:T(8,128)}, u32[]{:S(2)}, u32[]{:S(2)}) %collective-permute-start.3) | collective-permute-done | bytes 4194336 | tf_op jit(solution)/shard_map/ppermute | solution.py:432
  166.4 2.6 collective-permute-start.11
  169.0 4.7 %fusion.1 = (f32[1024,512]{1,0:T(8,128)}, f32[1024,512]{1,0:T(8,128)}) fusion(f32[1024,1024]{1,0:T(8,128)} %collective-permute-done.3.refs_1_.refs_0_), kind=kLoop, calls=%fused_computation.8 | loop fusion | bytes 8388608 | tf_op jit(solution)/shard_map/split | solution.py:429
  173.7 1.3 collective-permute-start.8
  175.0 1.6 collective-permute-start.5
  176.6 10.1 %factor_at_columns.1.refs_3_ = bf16[1536,2048]{1,0:T(8,128)(2,1)} custom-call(s32[74]{0:T(128)S(1)} %copy-done.6, f32[512,1024]{1,0:T(8,128)S(1)} %bitcast.25, f32[512,1024]{1,0:T(8,128)S(1)} %copy-done.4, f32[512,512]{1,0:T(8,128)S(1)} %copy-done.10, f32[1024,1024]{1,0:T(8,128)} %collective-permute-done.3.refs_1_.refs_0_, ...), custom_call_target="tpu_custom_call" | custom-call | flops 11500000256 | bytes 36900000 | tf_op jit(solution)/shard_map/factor_at_columns/pallas_call | solution.py:484
  186.8 15.4 %factor_rows.3 = (f32[2,8,2,128,128]{4,3,2,1,0:T(8,128)}, bf16[2,8,128,1536]{3,2,1,0:T(8,128)(2,1)}) custom-call(s32[74]{0:T(128)S(1)} %copy-done.6, f32[1024,1024]{1,0:T(8,128)} %maximum_multiply_fusion.refs_0_, f32[1024,1024]{1,0:T(8,128)} %collective-permute-done.3.refs_1_.refs_0_, f32[1024,1024]{1,0:T(8,128)} %collective-permute-done.9.refs_2_.refs_1_, ...), custom_call_target="tpu_custom_call" | custom-call | flops 13799999488 | bytes 44280000 | tf_op jit(solution)/shard_map/factor_rows/pallas_call | solution.py:548
  202.2 2.8 copy-done.16
  205.0 20.7 %update_tile.3 = (f32[2,8,2,128,2048]{4,3,2,1,0:T(8,128)}, f32[8,128]{1,0:T(8,128)S(1)}) custom-call(s32[74]{0:T(128)S(1)} %copy-done.6, f32[8,2,2,128,1024]{4,3,2,1,0:T(8,128)} %bitcast.40, f32[8,128,1024]{2,1,0:T(8,128)} %collective-permute-done.10.refs_2_.refs_1_, bf16[2,8,128,1536]{3,2,1,0:T(8,128)(2,1)S(1)} %copy-done.16, ...), custom_call_target="tpu_custom_call" | custom-call | flops 27599998976 | bytes 88560000 | tf_op jit(solution)/shard_map/update_tile/pallas_call | solution.py:602
  225.9 1.3 copy-done.7
  227.2 1.6 copy-done.8
  228.8 8.5 %factor_rows.4 = (f32[2,8,2,128,128]{4,3,2,1,0:T(8,128)}, bf16[2,4,128,1536]{3,2,1,0:T(8,128)(2,1)S(1)}) custom-call(s32[74]{0:T(128)S(1)} %copy-done.6, f32[1024,1024]{1,0:T(8,128)} %collective-permute-done.3.refs_1_.refs_0_, f32[1024,512]{1,0:T(8,128)} %collective-permute-done.7.refs_1_, ...), custom_call_target="tpu_custom_call", output_to_operand_aliasing={{0}: (6, {})} | custom-call | flops 6899999744 | bytes 22140000 | tf_op jit(solution)/shard_map/factor_rows/pallas_call | solution.py:548
  237.3 11.8 %update_tile.4 = (f32[2,8,2,128,2048]{4,3,2,1,0:T(8,128)}, f32[8,128]{1,0:T(8,128)S(1)}) custom-call(s32[74]{0:T(128)S(1)} %copy-done.6, f32[8,2,2,128,1024]{4,3,2,1,0:T(8,128)} %bitcast.41, f32[4,128,1024]{2,1,0:T(8,128)} %collective-permute-done.11.refs_1_, ...), custom_call_target="tpu_custom_call", output_to_operand_aliasing={{0}: (6, {})} | custom-call | flops 13799999488 | bytes 44280000 | tf_op jit(solution)/shard_map/update_tile/pallas_call | solution.py:602
  249.1 15.1 %collective-permute-done.5.refs_2_ = f32[1024,512]{1,0:T(8,128)} collective-permute-done((f32[1024,512]{1,0:T(8,128)}, f32[1024,512]{1,0:T(8,128)}, u32[]{:S(2)}, u32[]{:S(2)}) %collective-permute-start.5) | collective-permute-done | bytes 2097184 | tf_op jit(solution)/shard_map/ppermute | solution.py:432
  264.2 9.4 %factor_rows.5 = (f32[2,8,2,128,128]{4,3,2,1,0:T(8,128)}, bf16[2,4,128,1536]{3,2,1,0:T(8,128)(2,1)S(1)}) custom-call(s32[74]{0:T(128)S(1)} %copy-done.6, f32[1024,1024]{1,0:T(8,128)} %collective-permute-done.3.refs_1_.refs_0_, f32[1024,512]{1,0:T(8,128)} %collective-permute-done.4.refs_1_, ...), custom_call_target="tpu_custom_call", output_to_operand_aliasing={{0}: (6, {})} | custom-call | flops 6899999744 | bytes 22140000 | tf_op jit(solution)/shard_map/factor_rows/pallas_call | solution.py:548
  273.6 11.6 %update_tile.5 = (f32[2,8,2,128,2048]{4,3,2,1,0:T(8,128)}, f32[8,128]{1,0:T(8,128)}) custom-call(s32[74]{0:T(128)S(1)} %copy-done.6, f32[8,2,2,128,1024]{4,3,2,1,0:T(8,128)} %bitcast.42, f32[4,128,1024]{2,1,0:T(8,128)S(1)} %collective-permute-done.12.refs_1_, ...), custom_call_target="tpu_custom_call", output_to_operand_aliasing={{0}: (6, {})} | custom-call | flops 13799999488 | bytes 44280000 | tf_op jit(solution)/shard_map/update_tile/pallas_call | solution.py:602
  (47 shorter events, 0.5 us)
Async XLA Ops:
  3.3 25.8 %copy-start.19 = (s32[2,2,4]{2,1,0:T(2,128)S(1)}, s32[2,2,4]{2,1,0:T(2,128)}, u32[]{:S(2)}) copy-start(s32[2,2,4]{2,1,0:T(2,128)} %constant.48.clone) | copy-start | bytes 196
  7.5 47.6 %collective-permute-start = (f32[512,1024]{1,0:T(8,128)}, f32[512,1024]{1,0:T(8,128)S(1)}, u32[]{:S(2)}, u32[]{:S(2)}) collective-permute-start(f32[512,1024]{1,0:T(8,128)} %bitcast.23), channel_id=1, source_target_pairs={{0,4},{4,0},{1,5},{5,1},{2,6},{6,2},{3,7},{7,3},{8,12},{12,8},{9,1... | collective-permute-start | bytes 6291464 | tf_op jit(solution)/shard_map/ppermute | solution.py:31
  8.0 16.4 %collective-permute-start.1 = (f32[10,128,128]{2,1,0:T(8,128)}, f32[10,128,128]{2,1,0:T(8,128)S(1)}, u32[]{:S(2)}, u32[]{:S(2)}) collective-permute-start(f32[10,128,128]{2,1,0:T(8,128)} %get-tuple-element.19), channel_id=1, source_target_pairs={{0,1},{1,0},{2,3},{3,2},{4,5},{5,4},{6,7},{7,6},{8,9},{9,8},{10,11... | collective-permute-start | bytes 1966088 | tf_op jit(solution)/shard_map/ppermute | solution.py:31
  24.4 0.8 copy-start.18
  26.4 30.5 %collective-permute-start.2 = (f32[10,128,128]{2,1,0:T(8,128)S(1)}, f32[10,128,128]{2,1,0:T(8,128)S(1)}, u32[]{:S(2)}, u32[]{:S(2)}) collective-permute-start(f32[10,128,128]{2,1,0:T(8,128)S(1)} %add.37), channel_id=1, source_target_pairs={{0,2},{1,3},{2,0},{3,1},{4,6},{5,7},{6,4},{7,5},{8,10},{9,11},{10,... | collective-permute-start | bytes 1966088 | tf_op jit(solution)/shard_map/ppermute | solution.py:31
  55.0 3.3 %copy-start.2 = (f32[512,1024]{1,0:T(8,128)}, f32[512,1024]{1,0:T(8,128)S(1)}, u32[]{:S(2)}) copy-start(f32[512,1024]{1,0:T(8,128)S(1)} %collective-permute-done.other) | copy-start | bytes 6291460
  57.0 22.0 %collective-permute-start.6 = (f32[10,128,128]{2,1,0:T(8,128)S(1)}, f32[10,128,128]{2,1,0:T(8,128)S(1)}, u32[]{:S(2)}, u32[]{:S(2)}) collective-permute-start(f32[10,128,128]{2,1,0:T(8,128)S(1)} %add_multiply_fusion), channel_id=1, source_target_pairs={{0,4},{4,0},{1,5},{5,1},{2,6},{6,2},{3,7},{7,3},{8,12},{12,8},{9,1... | collective-permute-start | bytes 1966088 | tf_op jit(solution)/shard_map/ppermute | solution.py:31
  58.3 7.5 %copy-start.1 = (f32[4,128,1024]{2,1,0:T(8,128)S(1)}, f32[4,128,1024]{2,1,0:T(8,128)}, u32[]{:S(2)}) copy-start(f32[4,128,1024]{2,1,0:T(8,128)} %get-tuple-element.18) | copy-start | bytes 6291460
  58.3 7.5 %copy-start.3 = (f32[512,1024]{1,0:T(8,128)S(1)}, f32[512,1024]{1,0:T(8,128)}, u32[]{:S(2)}) copy-start(f32[512,1024]{1,0:T(8,128)} %copy-done.2) | copy-start | bytes 6291460
  63.3 110.4 %collective-permute-start.10 = (f32[8,128,1024]{2,1,0:T(8,128)}, f32[8,128,1024]{2,1,0:T(8,128)}, u32[]{:S(2)}, u32[]{:S(2)}) collective-permute-start(f32[8,128,1024]{2,1,0:T(8,128)} %dynamic-slice_bitcast_fusion), channel_id=1, source_target_pairs={{0,4},{4,0},{1,5},{5,1},{2,6},{6,2},{3,7},{7,3},{8,12},{12,8},{9,1... | collective-permute-start | bytes 12582920 | tf_op jit(solution)/shard_map/ppermute | solution.py:31
  68.3 106.7 %collective-permute-start.9 = (f32[1024,1024]{1,0:T(8,128)}, f32[1024,1024]{1,0:T(8,128)}, u32[]{:S(2)}, u32[]{:S(2)}) collective-permute-start(f32[1024,1024]{1,0:T(8,128)} %maximum_multiply_fusion.refs_0_), channel_id=1, source_target_pairs={{2,1},{5,6},{10,9},{13,14},{18,17},{21,22},{26,25},{29,30}} | collective-permute-start | bytes 12582920 | tf_op jit(solution)/shard_map/ppermute | solution.py:432
  71.0 95.5 %collective-permute-start.3 = (f32[1024,1024]{1,0:T(8,128)}, f32[1024,1024]{1,0:T(8,128)}, u32[]{:S(2)}, u32[]{:S(2)}) collective-permute-start(f32[1024,1024]{1,0:T(8,128)} %maximum_multiply_fusion.refs_0_), channel_id=1, source_target_pairs={{2,3},{0,2},{5,4},{7,5},{10,11},{8,10},{13,12},{15,13},{18,19},{16... | collective-permute-start | bytes 12582920 | tf_op jit(solution)/shard_map/ppermute | solution.py:432
  76.9 148.8 %collective-permute-start.7 = (f32[1024,512]{1,0:T(8,128)}, f32[1024,512]{1,0:T(8,128)}, u32[]{:S(2)}, u32[]{:S(2)}) collective-permute-start(f32[1024,512]{1,0:T(8,128)} %get-tuple-element.36), channel_id=1, source_target_pairs={{2,0},{0,1},{5,7},{7,6},{10,8},{8,9},{13,15},{15,14},{18,16},{16,1... | collective-permute-start | bytes 6291464 | tf_op jit(solution)/shard_map/ppermute | solution.py:432
  79.0 170.2 %collective-permute-start.4 = (f32[1024,512]{1,0:T(8,128)}, f32[1024,512]{1,0:T(8,128)}, u32[]{:S(2)}, u32[]{:S(2)}) collective-permute-start(f32[1024,512]{1,0:T(8,128)} %get-tuple-element.37), channel_id=1, source_target_pairs={{2,0},{0,1},{5,7},{7,6},{10,8},{8,9},{13,15},{15,14},{18,16},{16,1... | collective-permute-start | bytes 6291464 | tf_op jit(solution)/shard_map/ppermute | solution.py:432
  140.0 1.0 copy-start.11
  141.0 1.0 copy-start.13
  141.9 5.7 %copy-start.9 = (f32[512,512]{1,0:T(8,128)}, f32[512,512]{1,0:T(8,128)S(1)}, u32[]{:S(2)}) copy-start(f32[512,512]{1,0:T(8,128)S(1)} %get-tuple-element.24.inverse.refs_0_) | copy-start | bytes 3145732
  154.0 22.6 %copy-start.4 = (f32[512,1024]{1,0:T(8,128)S(1)}, f32[512,1024]{1,0:T(8,128)}, u32[]{:S(2)}) copy-start(f32[512,1024]{1,0:T(8,128)} %copy-done.2) | copy-start | bytes 6291460
  154.0 22.6 %copy-start.6 = (s32[74]{0:T(128)S(1)}, s32[74]{0:T(128)}, u32[]{:S(2)}) copy-start(s32[74]{0:T(128)} %concatenate.6.meta.refs_6_) | copy-start | bytes 892
  154.0 22.6 %copy-start.10 = (f32[512,512]{1,0:T(8,128)S(1)}, f32[512,512]{1,0:T(8,128)}, u32[]{:S(2)}) copy-start(f32[512,512]{1,0:T(8,128)} %copy-done.9) | copy-start | bytes 3145732
  166.4 70.8 %collective-permute-start.11 = (f32[4,128,1024]{2,1,0:T(8,128)}, f32[4,128,1024]{2,1,0:T(8,128)}, u32[]{:S(2)}, u32[]{:S(2)}) collective-permute-start(f32[4,128,1024]{2,1,0:T(8,128)} %dynamic-slice_bitcast_fusion.2.refs_1_), channel_id=1, source_target_pairs={{0,4},{4,0},{1,5},{5,1},{2,6},{6,2},{3,7},{7,3},{8,12},{12,8},{9,1... | collective-permute-start | bytes 6291464 | tf_op jit(solution)/shard_map/ppermute | solution.py:31
  173.7 52.2 %collective-permute-start.8 = (f32[1024,512]{1,0:T(8,128)}, f32[1024,512]{1,0:T(8,128)S(1)}, u32[]{:S(2)}, u32[]{:S(2)}) collective-permute-start(f32[1024,512]{1,0:T(8,128)} %get-tuple-element.34), channel_id=1, source_target_pairs={{2,3},{5,4},{10,11},{13,12},{18,19},{21,20},{26,27},{29,28}} | collective-permute-start | bytes 6291464 | tf_op jit(solution)/shard_map/ppermute | solution.py:432
  175.0 11.8 %copy-start.12 = (f32[512,512]{1,0:T(8,128)S(1)}, f32[512,512]{1,0:T(8,128)}, u32[]{:S(2)}) copy-start(f32[512,512]{1,0:T(8,128)} %copy-done.11) | copy-start | bytes 3145732
  175.0 11.8 %copy-start.14 = (f32[512,512]{1,0:T(8,128)S(1)}, f32[512,512]{1,0:T(8,128)}, u32[]{:S(2)}) copy-start(f32[512,512]{1,0:T(8,128)} %copy-done.13) | copy-start | bytes 3145732
  175.0 89.2 %collective-permute-start.5 = (f32[1024,512]{1,0:T(8,128)}, f32[1024,512]{1,0:T(8,128)}, u32[]{:S(2)}, u32[]{:S(2)}) collective-permute-start(f32[1024,512]{1,0:T(8,128)} %get-tuple-element.35), channel_id=1, source_target_pairs={{2,3},{5,4},{10,11},{13,12},{18,19},{21,20},{26,27},{29,28}} | collective-permute-start | bytes 6291464 | tf_op jit(solution)/shard_map/ppermute | solution.py:432
  186.8 15.4 %copy-start = (bf16[1536,2048]{1,0:T(8,128)(2,1)S(1)}, bf16[1536,2048]{1,0:T(8,128)(2,1)}, u32[]{:S(2)}) copy-start(bf16[1536,2048]{1,0:T(8,128)(2,1)} %factor_at_columns.1.refs_3_) | copy-start | bytes 18874372
  186.8 15.4 %copy-start.5 = (f32[4096]{0:T(1024)S(1)}, f32[4096]{0:T(1024)}, u32[]{:S(2)}) copy-start(f32[4096]{0:T(1024)} %param.7) | copy-start | bytes 49156
  202.2 2.8 copy-start.16
  205.0 20.7 %copy-start.17 = (f32[4,128,1024]{2,1,0:T(8,128)S(1)}, f32[4,128,1024]{2,1,0:T(8,128)}, u32[]{:S(2)}) copy-start(f32[4,128,1024]{2,1,0:T(8,128)} %dynamic-slice_bitcast_fusion.1) | copy-start | bytes 6291460
  205.0 22.2 %copy-start.15 = (f32[512,512]{1,0:T(8,128)S(1)}, f32[512,512]{1,0:T(8,128)}, u32[]{:S(2)}) copy-start(f32[512,512]{1,0:T(8,128)} %copy-done.13) | copy-start | bytes 3145732
  225.7 47.9 %collective-permute-start.12 = (f32[4,128,1024]{2,1,0:T(8,128)S(1)}, f32[4,128,1024]{2,1,0:T(8,128)S(1)}, u32[]{:S(2)}, u32[]{:S(2)}) collective-permute-start(f32[4,128,1024]{2,1,0:T(8,128)S(1)} %copy-done.17), channel_id=1, source_target_pairs={{0,4},{4,0},{1,5},{5,1},{2,6},{6,2},{3,7},{7,3},{8,12},{12,8},{9,1... | collective-permute-start | bytes 6291464 | tf_op jit(solution)/shard_map/ppermute | solution.py:31
  225.9 1.3 copy-start.7
  227.2 1.6 copy-start.8
